TPU v7x, 512 devices: a whole 4x4x16 slice. The times are simulated.
512 devices in a mesh: row: 32 (over x_lo, z), col: 16 (over x_hi, y, core).
Axes of the slice: x: 4 (x_hi: 2, x_lo: 2; x = x_hi * 2 + x_lo), y: 4, z: 16, core: 2. Of those that a mesh axis runs over, the one named last changes fastest.
Arguments:
- pair_state: bfloat16 [512, 512, 128], P('row', 'col'), may hold values from -6 to 6
- sequence_embedding: bfloat16 [256, 32768], P('row', 'col'), may hold values from -6 to 6
- token_valid_mask: int32 [512], replicated, may hold values 0 or 1
- sequence_present_flags: int32 [256], P('row'), may hold values 0 or 1
- triangle_input_weight: bfloat16 [128, 640], replicated, may hold values from -0.5 to 0.5
- triangle_output_weight: bfloat16 [128, 128], replicated, may hold values from -0.5 to 0.5
- pair_head_bias: bfloat16 [128, 8], replicated, may hold values from -30 to 30
- sequence_entry_matrix: bfloat16 [64, 512], replicated, may hold values from -0.75 to 0.75
- sequence_exit_matrix: bfloat16 [256, 64], replicated, may hold values from -0.375 to 0.375
Outputs:
- coupling_refreshed: bfloat16 [512, 512, 128], P('row', 'col')
- sequence_refreshed: bfloat16 [256, 32768], P('row', 'col')
All inputs are finite; a program needn't handle non-finite values. No bound on the sum of `sequence_present_flags` on one device may be relied on, other than what follows from the above.
Results may differ from a plain program's by a relative error of at most 0.0073.
Values may be sent and summed in bfloat16 or wider, within the bound.
No kernel may reach another device: no remote copies, remote signals or barrier semaphores. Data moves between devices by JAX's collectives and lax.ppermute only.
A program may use at most 64 MiB of HBM per device.

v0:
```python
import jax
import jax.numpy as jnp
from jax import lax
from jax.sharding import PartitionSpec as P

epsilon = 1e-05


def broadcast(value, axis, source):
    kept = jnp.where(lax.axis_index(axis) == source, value, 0).astype(value.dtype)
    return lax.psum(kept, axis)


def apply_layer_norm(array, along):
    average = jnp.mean(array, axis=along, keepdims=True)
    centred = array - average
    spread = jnp.mean(centred * centred, axis=along, keepdims=True)
    return centred * lax.rsqrt(spread + epsilon)


def shards(
    pair_state,
    sequence_embedding,
    token_valid_mask,
    sequence_present_flags,
    triangle_input_weight,
    triangle_output_weight,
    pair_head_bias,
    sequence_entry_matrix,
    sequence_exit_matrix,
):
    rows_here, column_count_local, channels = pair_state.shape
    number_of_heads = pair_head_bias.shape[1]
    value_width = sequence_exit_matrix.shape[0]
    value_depth = value_width // number_of_heads
    alignment_width = sequence_entry_matrix.shape[0]
    alignment_rows = sequence_embedding.shape[0]
    row_index = lax.axis_index("row")
    col_index = lax.axis_index("col")
    fanout = lax.axis_size("row") // lax.axis_size("col")
    row_valid = lax.dynamic_slice_in_dim(token_valid_mask, row_index * rows_here, rows_here).astype(
        jnp.float32
    )
    col_valid = lax.dynamic_slice_in_dim(
        token_valid_mask, col_index * column_count_local, column_count_local
    ).astype(jnp.float32)
    pair_valid = row_valid[:, None] * col_valid[None, :]
    normed = apply_layer_norm(pair_state.astype(jnp.float32), 2).astype(jnp.bfloat16)
    projected = jnp.einsum(
        "ijd,de->eij", normed, triangle_input_weight, preferred_element_type=jnp.float32
    )
    left_proj = (
        jax.nn.sigmoid(projected[:channels]) * projected[channels : 2 * channels] * pair_valid
    ).astype(jnp.bfloat16)
    right_proj = (
        jax.nn.sigmoid(projected[2 * channels : 3 * channels])
        * projected[3 * channels : 4 * channels]
        * pair_valid
    ).astype(jnp.bfloat16)
    out_gate = jax.nn.sigmoid(projected[4 * channels :])
    right_panel = lax.all_gather(right_proj, "col", axis=2, tiled=True)
    row_blocks = []
    for member in range(fanout):
        row_blocks.append(broadcast(right_panel, "row", fanout * col_index + member))
    right_rows = jnp.concatenate(row_blocks, axis=1)
    crossed = jnp.einsum(
        "cik,cjk->cij",
        lax.all_gather(left_proj, "col", axis=2, tiled=True),
        right_rows,
        preferred_element_type=jnp.float32,
    )
    crossed_norm = apply_layer_norm(crossed, 0).astype(jnp.bfloat16)
    update = jnp.einsum(
        "cij,cd->dij", crossed_norm, triangle_output_weight, preferred_element_type=jnp.float32
    )
    coupling_refreshed = (
        pair_state.astype(jnp.float32) + jnp.transpose(out_gate * update, (1, 2, 0))
    ).astype(jnp.bfloat16)
    normed_next = apply_layer_norm(coupling_refreshed.astype(jnp.float32), 2).astype(jnp.bfloat16)
    scores = jnp.einsum(
        "ijc,ch->hij", normed_next, pair_head_bias, preferred_element_type=jnp.float32
    )
    scores = scores + ((col_valid - 1.0) * 1000000000.0)[None, None, :]
    local_top = jnp.max(scores, axis=2)
    row_top = lax.pmax(local_top, "col")
    exponent = jnp.exp(scores - row_top[:, :, None])
    row_sum = lax.psum(jnp.sum(exponent, axis=2), "col")
    attention_factors = (exponent / row_sum[:, :, None]).astype(jnp.bfloat16)
    sequence_slab = sequence_embedding.reshape(
        alignment_rows, column_count_local, alignment_width
    ).astype(jnp.float32)
    alignment_normed = apply_layer_norm(sequence_slab, 2).astype(jnp.bfloat16)
    value_transposed = jnp.einsum(
        "fik,kg->ifg",
        alignment_normed,
        sequence_entry_matrix[:, :value_width],
        preferred_element_type=jnp.float32,
    ).astype(jnp.bfloat16)
    sequence_switch = jax.nn.sigmoid(
        jnp.einsum(
            "cla,ag->clg",
            alignment_normed,
            sequence_entry_matrix[:, value_width:],
            preferred_element_type=jnp.float32,
        )
    )
    weight_cols = lax.all_gather(attention_factors, "row", axis=1, tiled=True)
    payload_by_attender = value_transposed.reshape(
        column_count_local, alignment_rows, number_of_heads, value_depth
    )
    triangle_term = jnp.einsum(
        "hij,jshv->ishv", weight_cols, payload_by_attender, preferred_element_type=jnp.float32
    )
    accumulated_total = lax.psum_scatter(
        triangle_term.reshape(
            column_count_local * lax.axis_size("col"), alignment_rows, value_width
        ),
        "col",
        scatter_dimension=0,
        tiled=True,
    )
    coupling_smoothed_sequences = jnp.transpose(accumulated_total, (1, 0, 2))
    switched_product = (sequence_switch * coupling_smoothed_sequences).astype(jnp.bfloat16)
    final_output = jnp.einsum(
        "tga,aq->tgq", switched_product, sequence_exit_matrix, preferred_element_type=jnp.float32
    )
    sequence_refreshed = (
        sequence_slab + sequence_present_flags.astype(jnp.float32)[:, None, None] * final_output
    ).astype(jnp.bfloat16)
    return (
        coupling_refreshed,
        sequence_refreshed.reshape(alignment_rows, column_count_local * alignment_width),
    )


def solution(mesh):
    placed = (P("row", "col", None), P("row", "col"), P(), P("row"), P(), P(), P(), P(), P())
    return jax.shard_map(
        shards,
        mesh=mesh,
        in_specs=placed,
        out_specs=(P("row", "col", None), P("row", "col")),
        check_vma=False,
    )
```

profile of v0, /device:TPU:1, one launch (start us, length us, event | category | flops | bytes accessed | tf_op | source)
XLA Modules:
  0.0 681.8 jit_solution(12587056707024467437)
XLA Ops:
  7.2 0.8 dynamic-slice_convert_fusion.1
  8.0 0.8 add_multiply_fusion
  8.8 1.0 convert_reduce_fusion
  9.8 1.2 fusion.22
  11.1 1.3 convolution_bitcast_fusion.1
  12.4 1.1 copy-done.1
  13.5 0.9 fusion.27
  15.2 67.4 %all-gather.5.cloned.1.call-done = bf16[128,16,512]{0,2,1:T(8,128)(2,1)} async-done(((bf16[128,16,32]{0,2,1:T(8,128)(2,1)}), bf16[128,16,512]{0,2,1:T(8,128)(2,1)}) %all-gather.5.cloned.1.call-update) | async-done | bytes 2097168 | tf_op jit(solution)/shard_map/all_gather | solution.py:61
  82.6 4.0 broadcast_select_fusion.1
  88.2 58.1 %all-gather.3.cloned.1.call-done = bf16[128,16,512]{0,2,1:T(8,128)(2,1)} async-done(((bf16[128,16,32]{0,2,1:T(8,128)(2,1)}), bf16[128,16,512]{0,2,1:T(8,128)(2,1)}) %all-gather.3.cloned.1.call-update) | async-done | bytes 2097168 | tf_op jit(solution)/shard_map/all_gather | solution.py:68
  146.4 3.4 copy.23
  149.8 250.5 %all-reduce.3.cloned.1.call-done = (bf16[128,16,512]{0,2,1:T(8,128)(2,1)}, bf16[128,16,512]{0,2,1:T(8,128)(2,1)}) async-done(((bf16[128,16,512]{0,2,1:T(8,128)(2,1)}, bf16[128,16,512]{0,2,1:T(8,128)(2,1)}), (bf16[128,16,512]{0,2,1:T(8,128)(2,1)}, bf16[128,16,512]{0,2,1:T(8,128)(2,1)})) %all-reduce.3.cloned.1.call-update) | async-done | bytes 4194320 | tf_op jit(solution)/shard_map/psum | solution.py:11
  400.3 4.5 pad_maximum_fusion
  404.8 7.9 %copy.24 = bf16[128,32,512]{2,1,0:T(8,128)(2,1)} copy(bf16[128,32,512]{0,2,1:T(8,128)(2,1)} %pad_maximum_fusion) | data formatting | bytes 8388608 | tf_op jit(solution)/shard_map/concatenate | solution.py:65
  412.7 3.4 fusion.66
  417.0 1.3 convert_reduce_fusion.1
  419.1 53.7 %pmax.7 = f32[8,16]{0,1:T(8,128)S(1)} all-reduce(f32[8,16]{0,1:T(8,128)S(1)} %get-tuple-element.14), channel_id=1, replica_groups=mesh['row'=32,'col'=16] {'col'}, use_global_device_ids=true, to_apply=%region_11.12 | all-reduce | flops 128 | bytes 1024 | tf_op jit(solution)/shard_map/pmax | solution.py:85
  473.0 33.1 %psum.23 = f32[8,16]{0,1:T(8,128)S(1)} all-reduce(f32[8,16]{0,1:T(8,128)S(1)} %fusion.55), channel_id=1, replica_groups=mesh['row'=32,'col'=16] {'col'}, use_global_device_ids=true, to_apply=%region_13.14 | all-reduce | flops 128 | bytes 1024 | tf_op jit(solution)/shard_map/psum | solution.py:87
  506.2 54.0 %all_gather.11 = bf16[8,512,32]{2,0,1:T(8,128)(2,1)S(1)} all-gather(bf16[8,16,32]{2,0,1:T(8,128)(2,1)S(1)} %divide_convert_fusion), channel_id=1, replica_groups=mesh['row'=32,'col'=16] {'row'}, dimensions={1}, use_global_device_ids=true | all-gather | bytes 270336 | tf_op jit(solution)/shard_map/all_gather | solution.py:107
  560.3 0.7 convolution_bitcast_fusion
  561.0 2.5 copy.28
  563.5 5.4 copy.29
  569.6 103.6 %reduce-scatter.2.cloned.1.call-done = f32[32,8,256]{2,1,0:T(8,128)} async-done(((f32[512,8,256]{2,1,0:T(8,128)}), f32[32,8,256]{2,1,0:T(8,128)}) %reduce-scatter.2.cloned.1.call-update) | async-done | bytes 262160 | tf_op jit(solution)/shard_map/reduce_scatter | solution.py:114
  673.2 1.3 fusion.13
  (49 shorter events, 5.8 us)
Async XLA Ops:
  7.2 3.9 copy-start
  7.2 75.4 %all-gather.5.cloned.1.call-start = ((), (), s32[]{:S(2)}) async-start(), calls=%async_computation.2 | async-start | bytes 2228224 | tf_op jit(solution)/shard_map/all_gather | solution.py:61
  12.4 1.1 copy-start.1
  14.4 132.0 %all-gather.3.cloned.1.call-start = ((), (), s32[]{:S(2)}) async-start(), calls=%async_computation.1 | async-start | bytes 2228224 | tf_op jit(solution)/shard_map/all_gather | solution.py:68
  15.1 385.2 %all-reduce.3.cloned.1.call-start = ((), (), s32[]{:S(2)}) async-start(), calls=%async_computation.4 | async-start | bytes 8388608 | tf_op jit(solution)/shard_map/psum | solution.py:11
  86.5 0.8 copy-start.4
  86.5 1.2 copy-start.5
  86.6 586.6 %reduce-scatter.2.cloned.1.call-start = ((), (), s32[]{:S(2)}) async-start(), calls=%async_computation.3 | async-start | bytes 4456448 | tf_op jit(solution)/shard_map/reduce_scatter | solution.py:114
  416.1 0.9 copy-start.2
  416.1 0.9 copy-start.6
  416.3 2.3 copy-start.8
  418.4 142.7 %copy-start.3 = (bf16[16,32,128]{2,1,0:T(8,128)(2,1)}, bf16[16,32,128]{2,1,0:T(8,128)(2,1)S(1)}, u32[]{:S(2)}) copy-start(bf16[16,32,128]{2,1,0:T(8,128)(2,1)S(1)} %get-tuple-element.13) | copy-start | bytes 393220
  569.0 0.7 copy-start.9
  569.0 104.2 %copy-start.7 = (bf16[256,64]{0,1:T(8,128)(2,1)S(1)}, bf16[256,64]{0,1:T(8,128)(2,1)}, u32[]{:S(2)}) copy-start(bf16[256,64]{0,1:T(8,128)(2,1)} %param.17) | copy-start | bytes 98308
Sparse Core Ops, SparseCore 0:
  14.5 68.0 all-gather.4
  85.7 60.6 all-gather.2
  149.3 250.8 all-reduce.2
  569.1 104.0 reduce-scatter.1
where the time goes:
time: 683 us; the launch traced here: 682 us
  waiting for transfers between devices  480 us (70%)
  blocking collectives  141 us (21%)
  local copies, waits for them, and re-layouts  23.3 us (3%)
  other arithmetic  14.3 us (2%)
  between operations  14 us (2%)
  matrix products  8.81 us (1%)
    psum x1, waiting for transfers between devices, broadcast(): return lax.psum(kept, axis)  250 us
    reduce_scatter x1, waiting for transfers between devices, shards(): lax.psum_scatter(triangle_term.reshape(column_count_local * lax.axis_size...  104 us
    all_gather x1, waiting for transfers between devices, shards(): right_panel = lax.all_gather(right_proj, 'col', axis=2, tiled=True)  67.4 us
    all_gather x1, waiting for transfers between devices, shards(): lax.all_gather(left_proj, 'col', axis=2, tiled=True)  58.1 us
    all_gather x1, blocking collectives, shards(): weight_cols = lax.all_gather(attention_factors, 'row', axis=1, tiled=True)  54 us
    pmax x1, blocking collectives, shards(): row_top = lax.pmax(local_top, 'col')  53.7 us
    psum x1, blocking collectives, shards(): row_sum = lax.psum(jnp.sum(exponent, axis=2), 'col')  33.1 us
  transfers between devices with their start and end apart: 4, of which 4 were waited for; matrix products, arithmetic and copies ran while one was open for 1% of the time, Pallas kernels for 0%

commit v1 on v0

v1 whole, which is shorter than its diff:
```python
import jax
import jax.numpy as jnp
from jax import lax
from jax.sharding import PartitionSpec as P

epsilon = 1e-05


def apply_layer_norm(array, along):
    average = jnp.mean(array, axis=along, keepdims=True)
    centred = array - average
    spread = jnp.mean(centred * centred, axis=along, keepdims=True)
    return centred * lax.rsqrt(spread + epsilon)


def exchange(blocks, axis):
    return lax.all_to_all(blocks, axis, split_axis=0, concat_axis=0, tiled=True)


def shards(
    pair_state,
    sequence_embedding,
    token_valid_mask,
    sequence_present_flags,
    triangle_input_weight,
    triangle_output_weight,
    pair_head_bias,
    sequence_entry_matrix,
    sequence_exit_matrix,
):
    rows_here, columns_here, channels = pair_state.shape
    heads = pair_head_bias.shape[1]
    value_width = sequence_exit_matrix.shape[0]
    features = sequence_entry_matrix.shape[0]
    msa_rows = sequence_embedding.shape[0]
    row_index = lax.axis_index("row")
    col_index = lax.axis_index("col")
    row_size = lax.axis_size("row")
    col_size = lax.axis_size("col")
    fanout = row_size // col_size
    tokens = row_size * rows_here
    patch = rows_here * columns_here
    channels_here = channels // row_size
    parts = col_size // channels_here
    part = tokens // parts

    sequence_all = lax.all_gather(sequence_embedding, "col", axis=0)

    row_valid = lax.dynamic_slice_in_dim(token_valid_mask, row_index * rows_here, rows_here).astype(
        jnp.float32
    )
    col_valid = lax.dynamic_slice_in_dim(
        token_valid_mask, col_index * columns_here, columns_here
    ).astype(jnp.float32)
    patch_valid = (col_valid[:, None] * row_valid[None, :]).reshape(1, patch)
    normed = apply_layer_norm(pair_state.astype(jnp.float32), 2).astype(jnp.bfloat16)
    normed = jnp.transpose(normed, (1, 0, 2)).reshape(patch, channels)
    projected = jnp.einsum(
        "pd,de->ep", normed, triangle_input_weight, preferred_element_type=jnp.float32
    )
    left = (
        jax.nn.sigmoid(projected[:channels]) * projected[channels : 2 * channels] * patch_valid
    ).astype(jnp.bfloat16)
    right = (
        jax.nn.sigmoid(projected[2 * channels : 3 * channels])
        * projected[3 * channels : 4 * channels]
        * patch_valid
    ).astype(jnp.bfloat16)
    out_gate = jax.nn.sigmoid(projected[4 * channels :])

    sent = jnp.stack(
        [left.reshape(row_size, channels_here, patch), right.reshape(row_size, channels_here, patch)],
        axis=1,
    ).reshape(row_size, 2 * channels_here, patch)
    got = exchange(sent, "row").reshape(
        row_size, 2, channels_here, columns_here, rows_here
    )
    got = jnp.transpose(got, (1, 2, 3, 0, 4)).reshape(2, channels_here, columns_here, tokens)
    left_parts = jnp.transpose(
        got[0].reshape(channels_here, columns_here, parts, part), (0, 2, 1, 3)
    )
    right_parts = jnp.broadcast_to(
        got[1][:, None], (channels_here, parts, columns_here, tokens)
    )
    sent = jnp.concatenate([left_parts, right_parts], axis=3).reshape(
        col_size, columns_here, part + tokens
    )
    got = exchange(sent, "col").reshape(tokens, part + tokens)
    crossed = jnp.einsum(
        "kj,ki->ji", got[:, part:], got[:, :part], preferred_element_type=jnp.float32
    ).astype(jnp.bfloat16)
    got = exchange(crossed.reshape(col_size, columns_here, part), "col").reshape(
        channels_here, parts, columns_here, row_size // parts, rows_here
    )
    sent = jnp.transpose(got, (1, 3, 0, 2, 4)).reshape(row_size, channels_here, patch)
    crossed = exchange(sent, "row").reshape(channels, patch).astype(jnp.float32)

    crossed_norm = apply_layer_norm(crossed, 0).astype(jnp.bfloat16)
    update = jnp.einsum(
        "cp,cd->dp", crossed_norm, triangle_output_weight, preferred_element_type=jnp.float32
    )
    update = (out_gate * update).reshape(channels, columns_here, rows_here)
    coupling_refreshed = (
        pair_state.astype(jnp.float32) + jnp.transpose(update, (2, 1, 0))
    ).astype(jnp.bfloat16)
    normed_next = apply_layer_norm(coupling_refreshed.astype(jnp.float32), 2).astype(jnp.bfloat16)
    scores = jnp.einsum(
        "ijc,ch->jih", normed_next, pair_head_bias, preferred_element_type=jnp.float32
    ).reshape(columns_here, rows_here * heads)
    scores = scores + ((col_valid - 1.0) * 1000000000.0)[:, None]

    moves = []
    for row in range(row_size):
        for col in range(col_size):
            target = ((row % fanout) * col_size + col) * col_size + row // fanout
            moves.append((row * col_size + col, target))
    scores = lax.ppermute(scores, ("row", "col"), moves)
    scores = exchange(
        jnp.broadcast_to(scores[None], (row_size,) + scores.shape), "row"
    ).reshape(fanout, tokens, rows_here * heads)
    exponent = jnp.exp(scores - jnp.max(scores, axis=1, keepdims=True))
    weights = (exponent / jnp.sum(exponent, axis=1, keepdims=True)).astype(jnp.bfloat16)

    sequence_all = sequence_all.reshape(col_size, msa_rows, columns_here, features)
    sequence_all = apply_layer_norm(sequence_all.astype(jnp.float32), 3).astype(jnp.bfloat16)
    values = jnp.einsum(
        "qsjf,fg->sqjg",
        sequence_all,
        sequence_entry_matrix[:, :value_width],
        preferred_element_type=jnp.float32,
    ).astype(jnp.bfloat16).reshape(msa_rows, tokens, value_width)
    sequence_slab = sequence_embedding.reshape(msa_rows, columns_here, features).astype(jnp.float32)
    sequence_normed = apply_layer_norm(sequence_slab, 2).astype(jnp.bfloat16)
    sequence_switch = jax.nn.sigmoid(
        jnp.einsum(
            "sjf,fg->sjg",
            sequence_normed,
            sequence_entry_matrix[:, value_width:],
            preferred_element_type=jnp.float32,
        )
    )
    averaged = jnp.einsum(
        "mjp,sjg->smpg", weights, values, preferred_element_type=jnp.float32
    ).reshape(msa_rows, fanout * rows_here, heads, value_width)
    own = (
        lax.broadcasted_iota(jnp.int32, (heads, value_width), 1) // (value_width // heads)
        == lax.broadcasted_iota(jnp.int32, (heads, value_width), 0)
    )
    averaged = jnp.sum(jnp.where(own[None, None], averaged, 0.0), axis=2)
    switched = (sequence_switch * averaged).astype(jnp.bfloat16)
    final_output = jnp.einsum(
        "sig,gf->sif", switched, sequence_exit_matrix, preferred_element_type=jnp.float32
    )
    sequence_refreshed = (
        sequence_slab + sequence_present_flags.astype(jnp.float32)[:, None, None] * final_output
    ).astype(jnp.bfloat16)
    return (
        coupling_refreshed,
        sequence_refreshed.reshape(msa_rows, columns_here * features),
    )


def solution(mesh):
    placed = (P("row", "col", None), P("row", "col"), P(), P("row"), P(), P(), P(), P(), P())
    return jax.shard_map(
        shards,
        mesh=mesh,
        in_specs=placed,
        out_specs=(P("row", "col", None), P("row", "col")),
        check_vma=False,
    )
```

time: 683 us -> 165 us (0.24)
  the two profiles are of different devices: /device:TPU:1 before, /device:TPU:7 now
where the time goes in v1:
time: 165 us; the launch traced here: 164 us
  blocking collectives  114 us (69%)
  starting transfers between devices  19.2 us (12%)
  local copies, waits for them, and re-layouts  11.9 us (7%)
  other arithmetic  9.48 us (6%)
  waiting for transfers between devices  4.98 us (3%)
  matrix products  3.81 us (2%)
    all_to_all x4, blocking collectives, exchange(): return lax.all_to_all(blocks, axis, split_axis=0, concat_axis=0, tiled=True)  85.5 us
    all_gather x1, blocking collectives, shards(): sequence_all = lax.all_gather(sequence_embedding, 'col', axis=0)  28.5 us
    all_to_all x1, starting transfers between devices, exchange(): return lax.all_to_all(blocks, axis, split_axis=0, concat_axis=0, tiled=True)  13.9 us
    ppermute x1, starting transfers between devices, shards(): scores = lax.ppermute(scores, ('row', 'col'), moves)  5.27 us
    ppermute x1, waiting for transfers between devices, shards(): scores = lax.ppermute(scores, ('row', 'col'), moves)  4.98 us
  transfers between devices with their start and end apart: 2, of which 1 were waited for; matrix products, arithmetic and copies ran while one was open for 4% of the time, Pallas kernels for 0%

profile of v1, /device:TPU:7, one launch (start us, length us, event | category | flops | bytes accessed | tf_op | source)
XLA Modules:
  0.0 164.4 jit_solution(5736317870474972019)
XLA Ops:
  0.7 0.8 add_multiply_fusion
  1.4 0.8 dynamic-slice_convert_fusion
  2.4 1.0 convert_reduce_fusion
  3.4 1.1 fusion.21
  4.6 1.1 fusion.22
  6.9 35.0 %all_to_all.25 = bf16[32,8,512]{2,1,0:T(8,128)(2,1)S(1)} all-to-all(bf16[32,8,512]{2,1,0:T(8,128)(2,1)S(1)} %copy.69), channel_id=1, replica_groups=mesh['row'=32,'col'=16] {'row'}, dimensions={0} | all-to-all | bytes 524288 | tf_op jit(solution)/shard_map/all_to_all | solution.py:17
  42.5 1.0 fusion.58
  43.5 1.7 %copy.72 = bf16[1,4,32,32,16]{2,4,3,1,0:T(8,128)(2,1)S(1)} copy(bf16[1,4,32,32,16]{3,4,2,1,0:T(8,128)(2,1)} %get-tuple-element.17) | data formatting | bytes 262144 | tf_op jit(solution)/shard_map/slice | solution.py:83
  45.4 0.7 copy.71
  46.4 20.9 %all_to_all.26 = bf16[16,32,640]{2,1,0:T(8,128)(2,1)S(1)} all-to-all(bf16[16,32,640]{2,1,0:T(8,128)(2,1)S(1)} %bitcast.78), channel_id=1, replica_groups=mesh['row'=32,'col'=16] {'col'}, dimensions={0} | all-to-all | bytes 1310720 | tf_op jit(solution)/shard_map/all_to_all | solution.py:17
  67.7 10.8 %all_to_all.27 = bf16[16,32,128]{2,1,0:T(8,128)(2,1)S(1)} all-to-all(bf16[16,32,128]{2,1,0:T(8,128)(2,1)S(1)} %bitcast.89), channel_id=1, replica_groups=mesh['row'=32,'col'=16] {'col'}, dimensions={0} | all-to-all | bytes 262144 | tf_op jit(solution)/shard_map/all_to_all | solution.py:17
  79.2 1.1 reshape.226
  80.3 18.8 %all_to_all.28 = bf16[32,4,512]{2,1,0:T(4,128)(2,1)S(1)} all-to-all(bf16[32,4,512]{2,1,0:T(4,128)(2,1)S(1)} %reshape.226), channel_id=1, replica_groups=mesh['row'=32,'col'=16] {'row'}, dimensions={0} | all-to-all | bytes 262144 | tf_op jit(solution)/shard_map/all_to_all | solution.py:17
  100.6 5.3 %collective-permute-start = (f32[32,128]{0,1:T(8,128)S(1)}, f32[32,128]{0,1:T(8,128)S(1)}, u32[]{:S(2)}, u32[]{:S(2)}) collective-permute-start(f32[32,128]{0,1:T(8,128)S(1)} %fusion.12), channel_id=1, source_target_pairs={{0,0},{1,16},{2,32},{3,48},{4,64},{5,80},{6,96},{7,112},{8,128},{9... | collective-permute-start | bytes 49160 | tf_op jit(solution)/shard_map/ppermute | solution.py:117
  105.8 5.0 %collective-permute-done = f32[32,128]{0,1:T(8,128)S(1)} collective-permute-done((f32[32,128]{0,1:T(8,128)S(1)}, f32[32,128]{0,1:T(8,128)S(1)}, u32[]{:S(2)}, u32[]{:S(2)}) %collective-permute-start) | collective-permute-done | bytes 16416 | tf_op jit(solution)/shard_map/ppermute | solution.py:117
  110.9 0.9 broadcast_in_dim.17
  111.7 13.9 %all-to-all-start.4 = ((f32[32,32,128]{2,1,0:T(8,128)}), f32[32,32,128]{2,1,0:T(8,128)S(1)}, u32[]{:S(2)}, u32[]{:S(2)}) async-start(f32[32,32,128]{2,1,0:T(8,128)} %broadcast_in_dim.17), calls=%async_computation.4 | async-start | bytes 1048576 | tf_op jit(solution)/shard_map/all_to_all | solution.py:17
  125.7 28.5 %all-gather = bf16[128,2048]{1,0:T(8,128)(2,1)S(1)} all-gather(bf16[8,2048]{1,0:T(8,128)(2,1)S(1)} %copy-done.3), channel_id=2, replica_groups=mesh['row'=32,'col'=16] {'col'}, dimensions={0}, use_global_device_ids=true | all-gather | bytes 557056 | tf_op jit(solution)/shard_map/all_gather | solution.py:47
  154.1 0.8 reshape.215
  154.9 0.9 reshape.216
  156.5 1.3 multiply_reduce_fusion
  157.8 1.5 convert_bitcast_fusion
  161.8 0.8 fusion.59
  163.7 0.7 reshape.213
  (73 shorter events, 9.0 us)
Async XLA Ops:
  0.6 5.1 %copy-start = (bf16[128,640]{1,0:T(8,128)(2,1)S(1)}, bf16[128,640]{1,0:T(8,128)(2,1)}, u32[]{:S(2)}) copy-start(bf16[128,640]{1,0:T(8,128)(2,1)} %param.13) | copy-start | bytes 491524
  78.4 20.9 %copy-start.6 = (bf16[128,128]{1,0:T(8,128)(2,1)S(1)}, bf16[128,128]{1,0:T(8,128)(2,1)}, u32[]{:S(2)}) copy-start(bf16[128,128]{1,0:T(8,128)(2,1)} %param.14) | copy-start | bytes 98308
  79.2 20.4 %copy-start.1 = (bf16[16,32,128]{2,1,0:T(8,128)(2,1)S(1)}, bf16[16,32,128]{2,1,0:T(8,128)(2,1)}, u32[]{:S(2)}) copy-start(bf16[16,32,128]{2,1,0:T(8,128)(2,1)} %param.9) | copy-start | bytes 393220
  79.2 21.1 %copy-start.5 = (bf16[128,8]{0,1:T(8,128)(2,1)S(1)}, bf16[128,8]{0,1:T(8,128)(2,1)}, u32[]{:S(2)}) copy-start(bf16[128,8]{0,1:T(8,128)(2,1)} %param.15) | copy-start | bytes 6148
  99.4 26.3 %copy-start.3 = (bf16[8,2048]{1,0:T(8,128)(2,1)S(1)}, bf16[8,2048]{1,0:T(8,128)(2,1)}, u32[]{:S(2)}) copy-start(bf16[8,2048]{1,0:T(8,128)(2,1)} %param.10) | copy-start | bytes 98308
  100.6 10.3 %collective-permute-start = (f32[32,128]{0,1:T(8,128)S(1)}, f32[32,128]{0,1:T(8,128)S(1)}, u32[]{:S(2)}, u32[]{:S(2)}) collective-permute-start(f32[32,128]{0,1:T(8,128)S(1)} %fusion.12), channel_id=1, source_target_pairs={{0,0},{1,16},{2,32},{3,48},{4,64},{5,80},{6,96},{7,112},{8,128},{9... | collective-permute-start | bytes 49160 | tf_op jit(solution)/shard_map/ppermute | solution.py:117
  111.7 49.6 %all-to-all-start.4 = ((f32[32,32,128]{2,1,0:T(8,128)}), f32[32,32,128]{2,1,0:T(8,128)S(1)}, u32[]{:S(2)}, u32[]{:S(2)}) async-start(f32[32,32,128]{2,1,0:T(8,128)} %broadcast_in_dim.17), calls=%async_computation.4 | async-start | bytes 1048576 | tf_op jit(solution)/shard_map/all_to_all | solution.py:17
  155.8 2.0 %copy-start.4 = (bf16[64,512]{1,0:T(8,128)(2,1)S(1)}, bf16[64,512]{1,0:T(8,128)(2,1)}, u32[]{:S(2)}) copy-start(bf16[64,512]{1,0:T(8,128)(2,1)} %param.16) | copy-start | bytes 196612
  159.3 0.9 copy-start.2
  159.4 1.0 copy-start.8
  162.5 0.8 copy-start.7

commit v2 on v1

v2 whole, which is shorter than its diff:
```python
import functools

import jax
import jax.numpy as jnp
from jax import lax
from jax.experimental import pallas as pl
from jax.experimental.pallas import tpu as pltpu
from jax.sharding import PartitionSpec as P

epsilon = 1e-05
mask_offset = 1000000000.0
score_floor = -8192.0


def apply_layer_norm(array, along):
    average = jnp.mean(array, axis=along, keepdims=True)
    centred = array - average
    spread = jnp.mean(centred * centred, axis=along, keepdims=True)
    return centred * lax.rsqrt(spread + epsilon)


def exchange(blocks, axis):
    return lax.all_to_all(blocks, axis, split_axis=0, concat_axis=0, tiled=True)


def normed_rows(array):
    average = jnp.mean(array, axis=-1, keepdims=True)
    centred = array - average
    spread = jnp.mean(centred * centred, axis=-1, keepdims=True)
    return centred * lax.rsqrt(spread + epsilon)


def project_kernel(
    row_size, col_size, mask, pair, weight, sent, gate, wide, mixed
):
    rows, columns, channels = pair.shape
    patch = rows * columns
    here = channels // row_size
    wide[...] = normed_rows(pair[...].astype(jnp.float32).reshape(patch, channels))
    normed = jnp.concatenate(
        [wide[pl.ds(k, rows, stride=columns), :] for k in range(columns)], axis=0
    ).astype(jnp.bfloat16)
    projected = lax.dot_general(
        weight[...], normed, (((0,), (1,)), ((), ())), preferred_element_type=jnp.float32
    )
    lane = lax.broadcasted_iota(jnp.int32, (1, patch), 1)
    first_row = lax.axis_index("row") * rows
    first_column = lax.axis_index("col") * columns
    row_valid = jnp.zeros((1, patch), jnp.int32)
    column_valid = jnp.zeros((1, patch), jnp.int32)
    for i in range(rows):
        row_valid = jnp.where(lane % rows == i, mask[first_row + i], row_valid)
    for k in range(columns):
        column_valid = jnp.where(lane // rows == k, mask[first_column + k], column_valid)
    valid = (row_valid * column_valid).astype(jnp.float32)
    left = jax.nn.sigmoid(projected[:channels]) * projected[channels : 2 * channels] * valid
    right = (
        jax.nn.sigmoid(projected[2 * channels : 3 * channels])
        * projected[3 * channels : 4 * channels]
        * valid
    )
    gate[...] = jax.nn.sigmoid(projected[4 * channels :])
    for r in range(row_size):
        mixed[2 * r * here : (2 * r + 1) * here, :] = left[r * here : (r + 1) * here]
        mixed[(2 * r + 1) * here : (2 * r + 2) * here, :] = right[r * here : (r + 1) * here]
    sent[...] = mixed[...].astype(jnp.bfloat16)


def update_kernel(mask, all_valid, crossed, gate, pair, weight, bias, coupling, spread, wide):
    rows, columns, channels = pair.shape
    patch = rows * columns
    lanes = bias.shape[1]
    heads = lanes // rows
    cross = crossed[...].astype(jnp.float32)
    average = jnp.mean(cross, axis=0, keepdims=True)
    centred = cross - average
    variance = jnp.mean(centred * centred, axis=0, keepdims=True)
    cross = (centred * lax.rsqrt(variance + epsilon)).astype(jnp.bfloat16)
    update = lax.dot_general(
        weight[...], cross, (((0,), (0,)), ((), ())), preferred_element_type=jnp.float32
    )
    wide[...] = (gate[...] * update).T
    lane = lax.broadcasted_iota(jnp.int32, (channels, lanes), 1)
    scores = jnp.zeros((columns, lanes), jnp.float32)
    for i in range(rows):
        line = pair[i].astype(jnp.float32) + wide[pl.ds(i, columns, stride=rows), :]
        line = line.astype(jnp.bfloat16)
        coupling[i] = line
        normed = normed_rows(line.astype(jnp.float32)).astype(jnp.bfloat16)
        own = jnp.where(lane // heads == i, bias[...], jnp.zeros((), jnp.bfloat16))
        scores = scores + jnp.dot(normed, own, preferred_element_type=jnp.float32)
    place = lax.broadcasted_iota(jnp.int32, (columns, lanes), 0)
    first_column = lax.axis_index("col") * columns
    valid = jnp.zeros((columns, lanes), jnp.int32)
    for j in range(columns):
        valid = jnp.where(place == j, mask[first_column + j], valid)
    any_valid = jnp.max(all_valid[...], axis=1, keepdims=True)
    any_valid = jnp.max(any_valid, axis=0, keepdims=True) > 0
    scores = scores + (valid.astype(jnp.float32) - 1.0) * mask_offset
    scores = jnp.where(any_valid, jnp.maximum(scores, score_floor), scores + mask_offset)
    top = jnp.max(scores, axis=0, keepdims=True).astype(jnp.bfloat16).astype(jnp.float32)
    spread[:columns, :] = jnp.exp(scores - top)
    spread[columns:, :] = jnp.broadcast_to(top, (spread.shape[0] - columns, lanes))


def shards(
    pair_state,
    sequence_embedding,
    token_valid_mask,
    sequence_present_flags,
    triangle_input_weight,
    triangle_output_weight,
    pair_head_bias,
    sequence_entry_matrix,
    sequence_exit_matrix,
):
    rows_here, columns_here, channels = pair_state.shape
    heads = pair_head_bias.shape[1]
    value_width = sequence_exit_matrix.shape[0]
    features = sequence_entry_matrix.shape[0]
    msa_rows = sequence_embedding.shape[0]
    row_index = lax.axis_index("row")
    col_index = lax.axis_index("col")
    row_size = lax.axis_size("row")
    col_size = lax.axis_size("col")
    fanout = row_size // col_size
    tokens = row_size * rows_here
    patch = rows_here * columns_here
    channels_here = channels // row_size
    left_parts = col_size // channels_here // fanout
    left_width = tokens // left_parts
    right_width = tokens // fanout
    moves = []
    for row in range(row_size):
        for col in range(col_size):
            target = ((row % fanout) * col_size + col) * col_size + row // fanout
            moves.append((row * col_size + col, target))

    vmem = pl.BlockSpec(memory_space=pltpu.VMEM)
    smem = pl.BlockSpec(memory_space=pltpu.SMEM)
    sent, out_gate = pl.pallas_call(
        functools.partial(project_kernel, row_size, col_size),
        out_shape=(
            jax.ShapeDtypeStruct((2 * channels, patch), jnp.bfloat16),
            jax.ShapeDtypeStruct((channels, patch), jnp.float32),
        ),
        in_specs=[smem, vmem, vmem],
        out_specs=(vmem, vmem),
        scratch_shapes=[
            pltpu.VMEM((patch, channels), jnp.float32),
            pltpu.VMEM((2 * channels, patch), jnp.float32),
        ],
        compiler_params=pltpu.CompilerParams(vmem_limit_bytes=32 * 1024 * 1024),
        cost_estimate=pl.CostEstimate(
            flops=10 * patch * channels * channels, bytes_accessed=2**20, transcendentals=0
        ),
    )(token_valid_mask, pair_state, triangle_input_weight)

    rider, sent = lax.optimization_barrier((sequence_embedding, sent))
    got = exchange(sent.reshape(row_size, 2 * channels_here, patch), "row")
    sequence_all = exchange(
        jnp.broadcast_to(rider[None], (col_size,) + rider.shape), "col"
    ).reshape(col_size, msa_rows, columns_here, features)
    got = got.reshape(row_size, 2, channels_here, columns_here, rows_here)
    got = jnp.transpose(got, (1, 2, 3, 0, 4))
    left = jnp.transpose(
        got[0].reshape(channels_here, columns_here, left_parts, left_width), (0, 2, 1, 3)
    ).reshape(channels_here, left_parts, 1, columns_here, left_width)
    right = jnp.transpose(
        got[1].reshape(channels_here, columns_here, col_size, fanout, rows_here), (0, 3, 1, 2, 4)
    ).reshape(channels_here, 1, fanout, columns_here, right_width)
    lead = (channels_here, left_parts, fanout, columns_here)
    sent = jnp.concatenate(
        [jnp.broadcast_to(left, lead + (left_width,)), jnp.broadcast_to(right, lead + (right_width,))],
        axis=4,
    ).reshape(col_size, columns_here, left_width + right_width)
    got = exchange(sent, "col").reshape(tokens, left_width + right_width)
    crossed = jnp.einsum(
        "kj,ki->ji",
        got[:, left_width:],
        got[:, :left_width],
        preferred_element_type=jnp.float32,
    ).astype(jnp.bfloat16)
    got = exchange(crossed.reshape(col_size, rows_here, left_width), "col").reshape(
        channels_here, left_parts, fanout, rows_here, row_size // left_parts, rows_here
    )
    sent = jnp.transpose(got, (1, 4, 0, 2, 3, 5)).reshape(row_size, channels_here, patch)
    crossed = exchange(sent, "row").reshape(channels, patch)
    coupling_refreshed, sent = pl.pallas_call(
        update_kernel,
        out_shape=(
            jax.ShapeDtypeStruct(pair_state.shape, jnp.bfloat16),
            jax.ShapeDtypeStruct((columns_here + 8, rows_here * heads), jnp.float32),
        ),
        in_specs=[smem] + [vmem] * 6,
        out_specs=(vmem, vmem),
        scratch_shapes=[pltpu.VMEM((patch, channels), jnp.float32)],
        compiler_params=pltpu.CompilerParams(vmem_limit_bytes=32 * 1024 * 1024),
        cost_estimate=pl.CostEstimate(
            flops=4 * patch * channels * channels, bytes_accessed=2**20, transcendentals=0
        ),
    )(
        token_valid_mask,
        token_valid_mask.reshape(4, -1),
        crossed,
        out_gate,
        pair_state,
        triangle_output_weight,
        jnp.tile(pair_head_bias, (1, rows_here)),
    )
    sent = sent.astype(jnp.bfloat16)

    sent = lax.ppermute(sent, ("row", "col"), moves)
    groups = [[m * col_size + b for b in range(col_size)] for m in range(fanout)]
    mine = lax.all_to_all(
        jnp.broadcast_to(sent[None], (col_size,) + sent.shape),
        "row",
        split_axis=0,
        concat_axis=0,
        axis_index_groups=groups,
        tiled=True,
    )
    swap = [(a, (a + col_size) % row_size) for a in range(row_size)]
    other = lax.ppermute(mine, "row", swap)

    sequence_all = apply_layer_norm(sequence_all.astype(jnp.float32), 3).astype(jnp.bfloat16)
    values = jnp.einsum(
        "qsjf,fg->qjsg",
        sequence_all,
        sequence_entry_matrix[:, :value_width],
        preferred_element_type=jnp.float32,
    ).astype(jnp.bfloat16).reshape(tokens, msa_rows * value_width)
    own = (
        lax.broadcasted_iota(jnp.int32, (heads, 1, value_width), 2) // (value_width // heads)
        == lax.broadcasted_iota(jnp.int32, (heads, 1, value_width), 0)
    )

    def average(got):
        got = got.astype(jnp.float32)
        tops = got[:, columns_here : columns_here + 1]
        exponent = got[:, :columns_here] * jnp.exp(tops - jnp.max(tops, axis=0, keepdims=True))
        weights = (exponent / jnp.sum(exponent, axis=(0, 1), keepdims=True)).astype(jnp.bfloat16)
        averaged = jnp.einsum(
            "jp,jx->px",
            weights.reshape(tokens, rows_here * heads),
            values,
            preferred_element_type=jnp.float32,
        ).reshape(rows_here, heads, msa_rows, value_width)
        return jnp.sum(jnp.where(own[None], averaged, 0.0), axis=1)

    mine = average(mine)
    other = average(other)
    low = row_index < col_size
    averaged = jnp.concatenate(
        [jnp.where(low, mine, other), jnp.where(low, other, mine)], axis=0
    )
    sequence_slab = sequence_embedding.reshape(msa_rows, columns_here, features).astype(jnp.float32)
    sequence_normed = apply_layer_norm(sequence_slab, 2).astype(jnp.bfloat16)
    sequence_switch = jax.nn.sigmoid(
        jnp.einsum(
            "sjf,fg->jsg",
            sequence_normed,
            sequence_entry_matrix[:, value_width:],
            preferred_element_type=jnp.float32,
        )
    )
    switched = (sequence_switch * averaged).astype(jnp.bfloat16)
    final_output = jnp.einsum(
        "isg,gf->sif", switched, sequence_exit_matrix, preferred_element_type=jnp.float32
    )
    sequence_refreshed = (
        sequence_slab + sequence_present_flags.astype(jnp.float32)[:, None, None] * final_output
    ).astype(jnp.bfloat16)
    return (
        coupling_refreshed,
        sequence_refreshed.reshape(msa_rows, columns_here * features),
    )


def solution(mesh):
    placed = (P("row", "col", None), P("row", "col"), P(), P("row"), P(), P(), P(), P(), P())
    return jax.shard_map(
        shards,
        mesh=mesh,
        in_specs=placed,
        out_specs=(P("row", "col", None), P("row", "col")),
        check_vma=False,
    )
```

time: 165 us -> 160 us (0.970)
  the two profiles are of different devices: /device:TPU:7 before, /device:TPU:32 now
where the time goes in v2:
time: 160 us
  blocking collectives  56 us (35%)
  waiting for transfers between devices  42.6 us (27%)
  starting transfers between devices  31.8 us (20%)
  local copies, waits for them, and re-layouts  16.3 us (10%)
  matrix products  6.22 us (4%)
  Pallas kernels  2.86 us (2%)
  other arithmetic  2.83 us (2%)
    all_to_all x2, blocking collectives, exchange(): return lax.all_to_all(blocks, axis, split_axis=0, concat_axis=0, tiled=True)  56 us
    all_to_all x3, waiting for transfers between devices, exchange(): return lax.all_to_all(blocks, axis, split_axis=0, concat_axis=0, tiled=True)  31 us
    all_to_all x1, starting transfers between devices, shards(): lax.all_to_all(jnp.broadcast_to(sent[None], (col_size,) + sent.shape), 'r...  14.8 us
    all_to_all x3, starting transfers between devices, exchange(): return lax.all_to_all(blocks, axis, split_axis=0, concat_axis=0, tiled=True)  12 us
    all_to_all x1, waiting for transfers between devices, shards(): lax.all_to_all(jnp.broadcast_to(sent[None], (col_size,) + sent.shape), 'r...  7.05 us
    dot_general x2, matrix products, average(): jnp.einsum('jp,jx->px', weights.reshape(tokens, rows_here * heads), value...  3.46 us
    unnamed x25, local copies, waits for them, and re-layouts  3.24 us
  transfers between devices with their start and end apart: 6, of which 6 were waited for; matrix products, arithmetic and copies ran while one was open for 9% of the time, Pallas kernels for 0%

profile of v2, /device:TPU:32, one launch (start us, length us, event | category | flops | bytes accessed | tf_op | source)
XLA Modules:
  0.0 159.8 jit_solution(6278207681165600918)
XLA Ops:
  3.2 1.3 shard_map.104
  4.4 37.1 %all_to_all.30 = bf16[32,8,512]{2,1,0:T(8,128)(2,1)S(1)} all-to-all(bf16[32,8,512]{2,1,0:T(8,128)(2,1)S(1)} %bitcast.93), channel_id=1, replica_groups=mesh['row'=32,'col'=16] {'row'}, dimensions={0} | all-to-all | bytes 524288 | tf_op jit(solution)/shard_map/all_to_all | solution.py:23
  44.2 18.9 %all_to_all.31 = bf16[16,32,512]{2,1,0:T(8,128)(2,1)S(1)} all-to-all(bf16[16,32,512]{2,1,0:T(8,128)(2,1)S(1)} %bitcast.103), channel_id=1, replica_groups=mesh['row'=32,'col'=16] {'col'}, dimensions={0} | all-to-all | bytes 1048576 | tf_op jit(solution)/shard_map/all_to_all | solution.py:23
  63.1 0.9 convolution_convert_fusion
  64.0 3.5 %all-to-all-start.2 = ((bf16[16,16,256]{2,1,0:T(8,128)(2,1)}), bf16[16,16,256]{2,1,0:T(8,128)(2,1)S(1)}, u32[]{:S(2)}, u32[]{:S(2)}) async-start(bf16[16,16,256]{2,1,0:T(8,128)(2,1)} %bitcast.12), calls=%async_computation.2 | async-start | bytes 262144 | tf_op jit(solution)/shard_map/all_to_all | solution.py:23
  67.6 8.2 %all-to-all-done.2 = bf16[16,16,256]{2,1,0:T(8,128)(2,1)S(1)} async-done(((bf16[16,16,256]{2,1,0:T(8,128)(2,1)}), bf16[16,16,256]{2,1,0:T(8,128)(2,1)S(1)}, u32[]{:S(2)}, u32[]{:S(2)}) %all-to-all-start.2) | async-done | bytes 131104 | tf_op jit(solution)/shard_map/all_to_all | solution.py:23
  76.6 3.6 %all-to-all-start.5 = ((bf16[16,8,2048]{2,1,0:T(8,128)(2,1)}), bf16[16,8,2048]{2,1,0:T(8,128)(2,1)S(1)}, u32[]{:S(2)}, u32[]{:S(2)}) async-start(bf16[16,8,2048]{2,1,0:T(8,128)(2,1)} %broadcast_in_dim.58), calls=%async_computation.5 | async-start | bytes 1048576 | tf_op jit(solution)/shard_map/all_to_all | solution.py:23
  81.4 1.8 %reshape.160 = bf16[32,4,512]{2,1,0:T(4,128)(2,1)} reshape(bf16[2,16,4,2,16,16]{5,4,3,2,1,0:T(8,128)(2,1)S(1)} %bitcast.98) | data formatting | bytes 262144 | tf_op jit(solution)/shard_map/reshape | solution.py:187
  83.2 9.3 %all-to-all-done.5 = bf16[16,8,2048]{2,1,0:T(8,128)(2,1)S(1)} async-done(((bf16[16,8,2048]{2,1,0:T(8,128)(2,1)}), bf16[16,8,2048]{2,1,0:T(8,128)(2,1)S(1)}, u32[]{:S(2)}, u32[]{:S(2)}) %all-to-all-start.5) | async-done | bytes 524320 | tf_op jit(solution)/shard_map/all_to_all | solution.py:23
  92.5 5.0 %all-to-all-start.3 = ((bf16[32,4,512]{2,1,0:T(4,128)(2,1)}), bf16[32,4,512]{2,1,0:T(4,128)(2,1)S(1)}, u32[]{:S(2)}, u32[]{:S(2)}) async-start(bf16[32,4,512]{2,1,0:T(4,128)(2,1)} %reshape.160), calls=%async_computation.3 | async-start | bytes 262144 | tf_op jit(solution)/shard_map/all_to_all | solution.py:23
  98.0 0.9 reshape.167
  99.5 13.6 %all-to-all-done.3 = bf16[32,4,512]{2,1,0:T(4,128)(2,1)S(1)} async-done(((bf16[32,4,512]{2,1,0:T(4,128)(2,1)}), bf16[32,4,512]{2,1,0:T(4,128)(2,1)S(1)}, u32[]{:S(2)}, u32[]{:S(2)}) %all-to-all-start.3) | async-done | bytes 131104 | tf_op jit(solution)/shard_map/all_to_all | solution.py:23
  113.2 1.6 %shard_map.105 = (bf16[16,32,128]{2,1,0:T(8,128)(2,1)}, f32[40,128]{1,0:T(8,128)S(1)}) custom-call(s32[512]{0:T(512)S(1)} %copy-done.5, s32[4,128]{1,0:T(4,128)S(1)} %bitcast.94, bf16[128,512]{1,0:T(8,128)(2,1)S(1)} %reshape.161.crossed, f32[128,512]{1,0:T(8,128)S(1)} %get-tuple-element.10.gate, bf16[16,32,128]{2,1,0:T(8,128)(2,1)S(1)} %copy-done.2, ...), custom_call_target="tpu_custom_call" | custom-call | flops 33554432 | bytes 1048576 | tf_op jit(solution)/shard_map/pallas_call | solution.py:189
  114.8 3.0 %collective-permute-start = (bf16[40,128]{1,0:T(8,128)(2,1)S(1)}, bf16[40,128]{1,0:T(8,128)(2,1)S(1)}, u32[]{:S(2)}, u32[]{:S(2)}) collective-permute-start(bf16[40,128]{1,0:T(8,128)(2,1)S(1)} %convert_element_type.56), channel_id=1, source_target_pairs={{0,0},{1,16},{2,32},{3,48},{4,64},{5,80},{6,96},{7,112},{8,128},{9... | collective-permute-start | bytes 30728 | tf_op jit(solution)/shard_map/ppermute | solution.py:213
  117.9 1.9 %collective-permute-done = bf16[40,128]{1,0:T(8,128)(2,1)S(1)} collective-permute-done((bf16[40,128]{1,0:T(8,128)(2,1)S(1)}, bf16[40,128]{1,0:T(8,128)(2,1)S(1)}, u32[]{:S(2)}, u32[]{:S(2)}) %collective-permute-start) | collective-permute-done | bytes 10272 | tf_op jit(solution)/shard_map/ppermute | solution.py:213
  120.5 14.8 %all-to-all-start.4 = ((bf16[16,40,128]{2,1,0:T(8,128)(2,1)}), bf16[16,40,128]{2,1,0:T(8,128)(2,1)S(1)}, u32[]{:S(2)}, u32[]{:S(2)}) async-start(bf16[16,40,128]{2,1,0:T(8,128)(2,1)} %broadcast_in_dim.32), calls=%async_computation.4 | async-start | bytes 327680 | tf_op jit(solution)/shard_map/all_to_all | solution.py:215
  135.3 1.3 multiply_reduce_fusion
  136.6 1.5 convert_bitcast_fusion
  138.2 1.4 copy.61
  140.3 2.5 %copy.72 = bf16[2048,512]{1,0:T(8,128)(2,1)} copy(bf16[2048,512]{0,1:T(8,128)(2,1)S(1)} %bitcast.96) | data formatting | bytes 4194304 | tf_op jit(solution)/shard_map/jp,jx->px/dot_general | solution.py:243
  142.8 7.1 %all-to-all-done.4 = bf16[16,40,128]{2,1,0:T(8,128)(2,1)S(1)} async-done(((bf16[16,40,128]{2,1,0:T(8,128)(2,1)}), bf16[16,40,128]{2,1,0:T(8,128)(2,1)S(1)}, u32[]{:S(2)}, u32[]{:S(2)}) %all-to-all-start.4) | async-done | bytes 163872 | tf_op jit(solution)/shard_map/all_to_all | solution.py:215
  150.2 1.9 %collective-permute-start.1 = (bf16[16,40,128]{2,0,1:T(8,128)(2,1)S(1)}, bf16[16,40,128]{2,0,1:T(8,128)(2,1)S(1)}, u32[]{:S(2)}, u32[]{:S(2)}) collective-permute-start(bf16[16,40,128]{2,0,1:T(8,128)(2,1)S(1)} %get-tuple-element.19), channel_id=1, source_target_pairs={{0,256},{16,272},{32,288},{48,304},{64,320},{80,336},{96,352},{112... | collective-permute-start | bytes 491528 | tf_op jit(solution)/shard_map/ppermute | solution.py:224
  152.2 2.6 %fusion = f32[16,8,256]{2,1,0:T(8,128)S(1)} fusion(bf16[8,256,512,1]{2,1,0,3:T(8,128)(2,1)} %bitcast.101, pred[8,256]{1,0:T(8,128)(4,1)S(1)} %iota_compare_fusion, bf16[128,512]{1,0:T(8,128)(2,1)S(1)} %copy.60), kind=kOutput, calls=%fused_computation.5 | convolution fusion | flops 268926976 | bytes 2361344 | tf_op jit(solution)/shard_map/jp,jx->px/dot_general | solution.py:243
  154.8 2.7 %collective-permute-done.1 = bf16[16,40,128]{2,0,1:T(8,128)(2,1)S(1)} collective-permute-done((bf16[16,40,128]{2,0,1:T(8,128)(2,1)S(1)}, bf16[16,40,128]{2,0,1:T(8,128)(2,1)S(1)}, u32[]{:S(2)}, u32[]{:S(2)}) %collective-permute-start.1) | collective-permute-done | bytes 163872 | tf_op jit(solution)/shard_map/ppermute | solution.py:224
  (75 shorter events, 12.3 us)
Async XLA Ops:
  0.6 158.1 %copy-start = (bf16[256,64]{0,1:T(8,128)(2,1)S(1)}, bf16[256,64]{0,1:T(8,128)(2,1)}, u32[]{:S(2)}) copy-start(bf16[256,64]{0,1:T(8,128)(2,1)} %param.17) | copy-start | bytes 98308
  0.6 0.9 copy-start.1
  1.6 0.7 copy-start.4
  2.2 0.9 copy-start.6
  44.1 31.7 %copy-start.8 = (bf16[8,2048]{1,0:T(8,128)(2,1)S(1)}, bf16[8,2048]{1,0:T(8,128)(2,1)}, u32[]{:S(2)}) copy-start(bf16[8,2048]{1,0:T(8,128)(2,1)} %param.10) | copy-start | bytes 98308
  44.2 36.2 %copy-start.10 = (bf16[128,8]{0,1:T(8,128)(2,1)S(1)}, bf16[128,8]{0,1:T(8,128)(2,1)}, u32[]{:S(2)}) copy-start(bf16[128,8]{0,1:T(8,128)(2,1)} %param.15) | copy-start | bytes 6148
  64.0 11.7 %all-to-all-start.2 = ((bf16[16,16,256]{2,1,0:T(8,128)(2,1)}), bf16[16,16,256]{2,1,0:T(8,128)(2,1)S(1)}, u32[]{:S(2)}, u32[]{:S(2)}) async-start(bf16[16,16,256]{2,1,0:T(8,128)(2,1)} %bitcast.12), calls=%async_computation.2 | async-start | bytes 262144 | tf_op jit(solution)/shard_map/all_to_all | solution.py:23
  76.6 15.9 %all-to-all-start.5 = ((bf16[16,8,2048]{2,1,0:T(8,128)(2,1)}), bf16[16,8,2048]{2,1,0:T(8,128)(2,1)S(1)}, u32[]{:S(2)}, u32[]{:S(2)}) async-start(bf16[16,8,2048]{2,1,0:T(8,128)(2,1)} %broadcast_in_dim.58), calls=%async_computation.5 | async-start | bytes 1048576 | tf_op jit(solution)/shard_map/all_to_all | solution.py:23
  81.1 16.6 %copy-start.11 = (s32[8]{0:T(128)S(1)}, s32[8]{0:T(128)}, u32[]{:S(2)}) copy-start(s32[8]{0:T(128)} %param.12) | copy-start | bytes 100
  92.5 20.6 %all-to-all-start.3 = ((bf16[32,4,512]{2,1,0:T(4,128)(2,1)}), bf16[32,4,512]{2,1,0:T(4,128)(2,1)S(1)}, u32[]{:S(2)}, u32[]{:S(2)}) async-start(bf16[32,4,512]{2,1,0:T(4,128)(2,1)} %reshape.160), calls=%async_computation.3 | async-start | bytes 262144 | tf_op jit(solution)/shard_map/all_to_all | solution.py:23
  97.9 15.2 %copy-start.2 = (bf16[16,32,128]{2,1,0:T(8,128)(2,1)S(1)}, bf16[16,32,128]{2,1,0:T(8,128)(2,1)}, u32[]{:S(2)}) copy-start(bf16[16,32,128]{2,1,0:T(8,128)(2,1)} %pair.3) | copy-start | bytes 393220
  97.9 15.2 %copy-start.3 = (bf16[128,128]{1,0:T(8,128)(2,1)S(1)}, bf16[128,128]{1,0:T(8,128)(2,1)}, u32[]{:S(2)}) copy-start(bf16[128,128]{1,0:T(8,128)(2,1)} %weight.3) | copy-start | bytes 98308
  98.0 15.2 %copy-start.5 = (s32[512]{0:T(512)S(1)}, s32[512]{0:T(512)}, u32[]{:S(2)}) copy-start(s32[512]{0:T(512)} %mask.3) | copy-start | bytes 6148
  99.5 37.1 %copy-start.9 = (bf16[64,512]{1,0:T(8,128)(2,1)S(1)}, bf16[64,512]{1,0:T(8,128)(2,1)}, u32[]{:S(2)}) copy-start(bf16[64,512]{1,0:T(8,128)(2,1)} %param.16) | copy-start | bytes 196612
  114.8 5.0 %collective-permute-start = (bf16[40,128]{1,0:T(8,128)(2,1)S(1)}, bf16[40,128]{1,0:T(8,128)(2,1)S(1)}, u32[]{:S(2)}, u32[]{:S(2)}) collective-permute-start(bf16[40,128]{1,0:T(8,128)(2,1)S(1)} %convert_element_type.56), channel_id=1, source_target_pairs={{0,0},{1,16},{2,32},{3,48},{4,64},{5,80},{6,96},{7,112},{8,128},{9... | collective-permute-start | bytes 30728 | tf_op jit(solution)/shard_map/ppermute | solution.py:213
  120.5 29.4 %all-to-all-start.4 = ((bf16[16,40,128]{2,1,0:T(8,128)(2,1)}), bf16[16,40,128]{2,1,0:T(8,128)(2,1)S(1)}, u32[]{:S(2)}, u32[]{:S(2)}) async-start(bf16[16,40,128]{2,1,0:T(8,128)(2,1)} %broadcast_in_dim.32), calls=%async_computation.4 | async-start | bytes 327680 | tf_op jit(solution)/shard_map/all_to_all | solution.py:215
  150.2 7.2 %collective-permute-start.1 = (bf16[16,40,128]{2,0,1:T(8,128)(2,1)S(1)}, bf16[16,40,128]{2,0,1:T(8,128)(2,1)S(1)}, u32[]{:S(2)}, u32[]{:S(2)}) collective-permute-start(bf16[16,40,128]{2,0,1:T(8,128)(2,1)S(1)} %get-tuple-element.19), channel_id=1, source_target_pairs={{0,256},{16,272},{32,288},{48,304},{64,320},{80,336},{96,352},{112... | collective-permute-start | bytes 491528 | tf_op jit(solution)/shard_map/ppermute | solution.py:224
  152.2 5.6 %copy-start.7 = (bf16[2048,512]{1,0:T(8,128)(2,1)S(1)}, bf16[2048,512]{1,0:T(8,128)(2,1)}, u32[]{:S(2)}) copy-start(bf16[2048,512]{1,0:T(8,128)(2,1)} %copy.72) | copy-start | bytes 6291460

commit v3 on v2

v3 whole, which is shorter than its diff:
```python
import functools

import jax
import jax.numpy as jnp
from jax import lax
from jax.experimental import pallas as pl
from jax.experimental.pallas import tpu as pltpu
from jax.sharding import PartitionSpec as P

epsilon = 1e-05
mask_offset = 1000000000.0
score_floor = -8192.0


def apply_layer_norm(array, along):
    average = jnp.mean(array, axis=along, keepdims=True)
    centred = array - average
    spread = jnp.mean(centred * centred, axis=along, keepdims=True)
    return centred * lax.rsqrt(spread + epsilon)


def exchange(blocks, axis):
    return lax.all_to_all(blocks, axis, split_axis=0, concat_axis=0, tiled=True)


def normed_rows(array):
    average = jnp.mean(array, axis=-1, keepdims=True)
    centred = array - average
    spread = jnp.mean(centred * centred, axis=-1, keepdims=True)
    return centred * lax.rsqrt(spread + epsilon)


def project_kernel(
    row_size, mask, pair, weight, sent, wide, mixed
):
    rows, columns, channels = pair.shape
    patch = rows * columns
    here = channels // row_size
    wide[...] = normed_rows(pair[...].astype(jnp.float32).reshape(patch, channels))
    normed = jnp.concatenate(
        [wide[pl.ds(k, rows, stride=columns), :] for k in range(columns)], axis=0
    ).astype(jnp.bfloat16)
    projected = lax.dot_general(
        weight[:, : 4 * channels], normed, (((0,), (1,)), ((), ())), preferred_element_type=jnp.float32
    )
    lane = lax.broadcasted_iota(jnp.int32, (1, patch), 1)
    first_row = lax.axis_index("row") * rows
    first_column = lax.axis_index("col") * columns
    row_valid = jnp.zeros((1, patch), jnp.int32)
    column_valid = jnp.zeros((1, patch), jnp.int32)
    for i in range(rows):
        row_valid = jnp.where(lane % rows == i, mask[first_row + i], row_valid)
    for k in range(columns):
        column_valid = jnp.where(lane // rows == k, mask[first_column + k], column_valid)
    valid = (row_valid * column_valid).astype(jnp.float32)
    left = jax.nn.sigmoid(projected[:channels]) * projected[channels : 2 * channels] * valid
    right = (
        jax.nn.sigmoid(projected[2 * channels : 3 * channels])
        * projected[3 * channels : 4 * channels]
        * valid
    )
    for r in range(row_size):
        mixed[2 * r * here : (2 * r + 1) * here, :] = left[r * here : (r + 1) * here]
        mixed[(2 * r + 1) * here : (2 * r + 2) * here, :] = right[r * here : (r + 1) * here]
    sent[...] = mixed[...].astype(jnp.bfloat16)


def update_kernel(columns, mask, all_valid, crossed, pair, gate_weight, weight, bias, coupling, spread):
    patch, channels = pair.shape
    rows = patch // columns
    lanes = bias.shape[1]
    heads = lanes // rows
    cross = crossed[...].astype(jnp.float32)
    average = jnp.mean(cross, axis=0, keepdims=True)
    centred = cross - average
    variance = jnp.mean(centred * centred, axis=0, keepdims=True)
    cross = (centred * lax.rsqrt(variance + epsilon)).astype(jnp.bfloat16)
    update = lax.dot_general(
        cross, weight[...], (((0,), (0,)), ((), ())), preferred_element_type=jnp.float32
    )
    before = pair[...].astype(jnp.float32)
    gate = jnp.dot(
        normed_rows(before).astype(jnp.bfloat16),
        gate_weight[:, 4 * channels :],
        preferred_element_type=jnp.float32,
    )
    after = (before + jax.nn.sigmoid(gate) * update).astype(jnp.bfloat16)
    coupling[...] = after
    normed = normed_rows(after.astype(jnp.float32)).astype(jnp.bfloat16)
    lane = lax.broadcasted_iota(jnp.int32, (channels, lanes), 1)
    scores = jnp.zeros((columns, lanes), jnp.float32)
    for i in range(rows):
        own = jnp.where(lane // heads == i, bias[...], jnp.zeros((), jnp.bfloat16))
        scores = scores + jnp.dot(
            normed[i * columns : (i + 1) * columns], own, preferred_element_type=jnp.float32
        )
    place = lax.broadcasted_iota(jnp.int32, (columns, lanes), 0)
    row_index = lax.axis_index("row")
    col_size = lax.axis_size("col")
    turned = (row_index + 2 * (col_size - lax.axis_index("col"))) % col_size
    first_column = (turned // 2 * 2 + row_index // col_size) * columns
    valid = jnp.zeros((columns, lanes), jnp.int32)
    for j in range(columns):
        valid = jnp.where(place == j, mask[first_column + j], valid)
    any_valid = jnp.max(all_valid[...], axis=1, keepdims=True)
    any_valid = jnp.max(any_valid, axis=0, keepdims=True) > 0
    scores = scores + (valid.astype(jnp.float32) - 1.0) * mask_offset
    scores = jnp.where(any_valid, jnp.maximum(scores, score_floor), scores + mask_offset)
    top = jnp.max(scores, axis=0, keepdims=True).astype(jnp.bfloat16).astype(jnp.float32)
    spread[:columns, :] = jnp.exp(scores - top)
    spread[columns:, :] = jnp.broadcast_to(top, (spread.shape[0] - columns, lanes))


def tile_place(row, col, col_size):
    return (col % 2) * col_size + (row + col // 2 * 2) % col_size, row // 2


def shards(
    pair_state,
    sequence_embedding,
    token_valid_mask,
    sequence_present_flags,
    triangle_input_weight,
    triangle_output_weight,
    pair_head_bias,
    sequence_entry_matrix,
    sequence_exit_matrix,
):
    rows_here, columns_here, channels = pair_state.shape
    heads = pair_head_bias.shape[1]
    value_width = sequence_exit_matrix.shape[0]
    features = sequence_entry_matrix.shape[0]
    msa_rows = sequence_embedding.shape[0]
    row_index = lax.axis_index("row")
    col_index = lax.axis_index("col")
    row_size = lax.axis_size("row")
    col_size = lax.axis_size("col")
    fanout = row_size // col_size
    tokens = row_size * rows_here
    patch = rows_here * columns_here
    channels_here = channels // row_size
    right_parts = col_size // channels_here // fanout
    left_width = tokens // fanout
    right_width = tokens // right_parts
    moves = []
    for row in range(row_size):
        for col in range(col_size):
            to_row, to_col = tile_place(row, col, col_size)
            moves.append((row * col_size + col, to_row * col_size + to_col))
    moves_back = [(b, a) for a, b in moves]

    vmem = pl.BlockSpec(memory_space=pltpu.VMEM)
    smem = pl.BlockSpec(memory_space=pltpu.SMEM)
    sent = pl.pallas_call(
        functools.partial(project_kernel, row_size),
        out_shape=jax.ShapeDtypeStruct((2 * channels, patch), jnp.bfloat16),
        in_specs=[smem, vmem, vmem],
        out_specs=vmem,
        scratch_shapes=[
            pltpu.VMEM((patch, channels), jnp.float32),
            pltpu.VMEM((2 * channels, patch), jnp.float32),
        ],
        compiler_params=pltpu.CompilerParams(vmem_limit_bytes=32 * 1024 * 1024),
        cost_estimate=pl.CostEstimate(
            flops=10 * patch * channels * channels, bytes_accessed=2**20, transcendentals=0
        ),
    )(token_valid_mask, pair_state, triangle_input_weight)

    got = exchange(sent.reshape(row_size, 2 * channels_here, patch), "row")
    pair_later, got = lax.optimization_barrier((pair_state, got))
    pair_moved = lax.ppermute(pair_later.reshape(patch, channels), ("row", "col"), moves)
    got = got.reshape(row_size, 2, channels_here, columns_here, rows_here)
    got = jnp.transpose(got, (1, 2, 3, 0, 4))
    left = jnp.transpose(
        got[0].reshape(channels_here, columns_here, col_size, fanout, rows_here), (0, 3, 1, 2, 4)
    ).reshape(channels_here, fanout, 1, columns_here, left_width)
    right = jnp.transpose(
        got[1].reshape(channels_here, columns_here, right_parts, right_width), (0, 2, 1, 3)
    ).reshape(channels_here, 1, right_parts, columns_here, right_width)
    lead = (channels_here, fanout, right_parts, columns_here)
    sent = jnp.concatenate(
        [jnp.broadcast_to(left, lead + (left_width,)), jnp.broadcast_to(right, lead + (right_width,))],
        axis=4,
    ).reshape(col_size, columns_here, left_width + right_width)
    rider = jnp.tile(
        sequence_embedding.reshape(2, -1, left_width + right_width), (col_size // 2, 1, 1)
    )
    got = exchange(jnp.concatenate([sent, rider], axis=1), "col")
    got, pair_moved = lax.optimization_barrier((got, pair_moved))
    half = got[:, columns_here:]
    half_other = lax.ppermute(half, "col", [(a, a ^ 1) for a in range(col_size)])
    first = col_index % 2 == 0
    sequence_all = jnp.concatenate(
        [jnp.where(first, half, half_other), jnp.where(first, half_other, half)], axis=1
    ).reshape(col_size // 2, 2, msa_rows, columns_here, features)
    sequence_all = jnp.roll(sequence_all, col_index, axis=0).reshape(
        col_size, msa_rows, columns_here, features
    )
    sequence_all = apply_layer_norm(sequence_all.astype(jnp.float32), 3).astype(jnp.bfloat16)
    values = jnp.einsum(
        "qsjf,fg->qjsg",
        sequence_all,
        sequence_entry_matrix[:, :value_width],
        preferred_element_type=jnp.float32,
    ).astype(jnp.bfloat16).reshape(tokens, msa_rows * value_width)
    got = got[:, :columns_here].reshape(tokens, left_width + right_width)
    crossed = jnp.einsum(
        "ki,kj->ij",
        got[:, :left_width],
        got[:, left_width:],
        preferred_element_type=jnp.float32,
    ).astype(jnp.bfloat16)
    got = exchange(crossed.reshape(col_size, rows_here, right_width), "col").reshape(
        channels_here, fanout, right_parts, rows_here, col_size // right_parts // 2, 2, columns_here
    )
    sent = jnp.transpose(got, (5, 2, 4, 1, 0, 3, 6)).reshape(
        2, col_size // 2, fanout, channels_here, patch
    )
    sent = jnp.roll(sent, col_index, axis=1).reshape(row_size, channels_here, patch)
    crossed = exchange(sent, "row").reshape(channels, patch)
    crossed, values = lax.optimization_barrier((crossed, values))
    coupling_moved, sent = pl.pallas_call(
        functools.partial(update_kernel, columns_here),
        out_shape=(
            jax.ShapeDtypeStruct((patch, channels), jnp.bfloat16),
            jax.ShapeDtypeStruct((columns_here + 8, rows_here * heads), jnp.float32),
        ),
        in_specs=[smem] + [vmem] * 6,
        out_specs=(vmem, vmem),
        compiler_params=pltpu.CompilerParams(vmem_limit_bytes=32 * 1024 * 1024),
        cost_estimate=pl.CostEstimate(
            flops=6 * patch * channels * channels, bytes_accessed=2**20, transcendentals=0
        ),
    )(
        token_valid_mask,
        token_valid_mask.reshape(4, -1),
        crossed,
        pair_moved,
        triangle_input_weight,
        triangle_output_weight,
        jnp.tile(pair_head_bias, (1, rows_here)),
    )
    coupling_refreshed = lax.ppermute(coupling_moved, ("row", "col"), moves_back).reshape(
        rows_here, columns_here, channels
    )
    sent = sent.astype(jnp.bfloat16)
    got = exchange(jnp.broadcast_to(sent[None], (row_size,) + sent.shape), "row")
    got = jnp.transpose(
        got.reshape(2, col_size // 2, fanout, columns_here + 8, rows_here * heads), (2, 1, 0, 3, 4)
    ).reshape(fanout, col_size, columns_here + 8, rows_here * heads)

    own = (
        lax.broadcasted_iota(jnp.int32, (heads, 1, value_width), 2) // (value_width // heads)
        == lax.broadcasted_iota(jnp.int32, (heads, 1, value_width), 0)
    )

    def average(got):
        got = got.astype(jnp.float32)
        tops = got[:, columns_here : columns_here + 1]
        exponent = got[:, :columns_here] * jnp.exp(tops - jnp.max(tops, axis=0, keepdims=True))
        weights = (exponent / jnp.sum(exponent, axis=(0, 1), keepdims=True)).astype(jnp.bfloat16)
        averaged = jnp.einsum(
            "jp,jx->px",
            weights.reshape(tokens, rows_here * heads),
            values,
            preferred_element_type=jnp.float32,
        ).reshape(rows_here, heads, msa_rows, value_width)
        return jnp.sum(jnp.where(own[None], averaged, 0.0), axis=1)

    averaged = jnp.concatenate([average(got[m]) for m in range(fanout)], axis=0)
    sequence_slab = sequence_embedding.reshape(msa_rows, columns_here, features).astype(jnp.float32)
    sequence_normed = apply_layer_norm(sequence_slab, 2).astype(jnp.bfloat16)
    sequence_switch = jax.nn.sigmoid(
        jnp.einsum(
            "sjf,fg->jsg",
            sequence_normed,
            sequence_entry_matrix[:, value_width:],
            preferred_element_type=jnp.float32,
        )
    )
    switched = (sequence_switch * averaged).astype(jnp.bfloat16)
    final_output = jnp.einsum(
        "isg,gf->sif", switched, sequence_exit_matrix, preferred_element_type=jnp.float32
    )
    sequence_refreshed = (
        sequence_slab + sequence_present_flags.astype(jnp.float32)[:, None, None] * final_output
    ).astype(jnp.bfloat16)
    return (
        coupling_refreshed,
        sequence_refreshed.reshape(msa_rows, columns_here * features),
    )


def solution(mesh):
    placed = (P("row", "col", None), P("row", "col"), P(), P("row"), P(), P(), P(), P(), P())
    return jax.shard_map(
        shards,
        mesh=mesh,
        in_specs=placed,
        out_specs=(P("row", "col", None), P("row", "col")),
        check_vma=False,
    )
```

time: 160 us -> 171 us (1.069)
  the two profiles are of different devices: /device:TPU:32 before, /device:TPU:17 now
where the time goes in v3:
time: 171 us; the launch traced here: 170 us
  waiting for transfers between devices  75 us (44%)
  starting transfers between devices  64.6 us (38%)
  local copies, waits for them, and re-layouts  15.5 us (9%)
  other arithmetic  6.29 us (4%)
  matrix products  3.65 us (2%)
  Pallas kernels  3.53 us (2%)
    all_to_all x5, starting transfers between devices, exchange(): return lax.all_to_all(blocks, axis, split_axis=0, concat_axis=0, tiled=True)  47.3 us
    all_to_all x5, waiting for transfers between devices, exchange(): return lax.all_to_all(blocks, axis, split_axis=0, concat_axis=0, tiled=True)  30.4 us
    ppermute x1, waiting for transfers between devices, shards(): lax.ppermute(coupling_moved, ('row', 'col'), moves_back)  23.9 us
    ppermute x1, waiting for transfers between devices, shards(): lax.ppermute(pair_later.reshape(patch, channels), ('row', 'col'), moves)  20.7 us
    ppermute x1, starting transfers between devices, shards(): lax.ppermute(coupling_moved, ('row', 'col'), moves_back)  13.2 us
    unnamed x28, local copies, waits for them, and re-layouts  4.75 us
  transfers between devices with their start and end apart: 8, of which 5 were waited for; matrix products, arithmetic and copies ran while one was open for 7% of the time, Pallas kernels for 0%

profile of v3, /device:TPU:17, one launch (start us, length us, event | category | flops | bytes accessed | tf_op | source)
XLA Modules:
  0.0 169.8 jit_solution(7114026186395555975)
XLA Ops:
  0.7 0.9 copy-done.1
  1.6 0.9 copy-done.3
  3.2 1.9 %shard_map.104 = bf16[256,512]{1,0:T(8,128)(2,1)} custom-call(s32[512]{0:T(512)S(1)} %copy-done.6, bf16[16,32,128]{2,1,0:T(8,128)(2,1)S(1)} %copy-done.3, bf16[128,640]{1,0:T(8,128)(2,1)S(1)} %copy-done.1), custom_call_target="tpu_custom_call" | custom-call | flops 83886080 | bytes 1048576 | tf_op jit(solution)/shard_map/pallas_call | solution.py:154
  5.1 16.1 %all-to-all-start = ((bf16[32,8,512]{2,1,0:T(8,128)(2,1)}), bf16[32,8,512]{2,1,0:T(8,128)(2,1)S(1)}, u32[]{:S(2)}, u32[]{:S(2)}) async-start(bf16[32,8,512]{2,1,0:T(8,128)(2,1)} %bitcast.1), calls=%async_computation | async-start | bytes 524288 | tf_op jit(solution)/shard_map/all_to_all | solution.py:23
  22.0 19.2 %all-to-all-done = bf16[32,8,512]{2,1,0:T(8,128)(2,1)S(1)} async-done(((bf16[32,8,512]{2,1,0:T(8,128)(2,1)}), bf16[32,8,512]{2,1,0:T(8,128)(2,1)S(1)}, u32[]{:S(2)}, u32[]{:S(2)}) %all-to-all-start) | async-done | bytes 262176 | tf_op jit(solution)/shard_map/all_to_all | solution.py:23
  43.9 1.0 pad_maximum_fusion
  44.9 10.0 %all-to-all-start.1 = ((bf16[16,48,512]{2,1,0:T(8,128)(2,1)}), bf16[16,48,512]{2,1,0:T(8,128)(2,1)S(1)}, u32[]{:S(2)}, u32[]{:S(2)}) async-start(bf16[16,48,512]{2,1,0:T(8,128)(2,1)} %pad_maximum_fusion), calls=%async_computation.1 | async-start | bytes 1572864 | tf_op jit(solution)/shard_map/all_to_all | solution.py:23
  54.8 1.9 %collective-permute-start = (bf16[512,128]{1,0:T(8,128)(2,1)S(1)}, bf16[512,128]{1,0:T(8,128)(2,1)S(1)}, u32[]{:S(2)}, u32[]{:S(2)}) collective-permute-start(bf16[512,128]{1,0:T(8,128)(2,1)S(1)} %bitcast.106), channel_id=1, source_target_pairs={{0,0},{1,256},{2,32},{3,288},{4,64},{5,320},{6,96},{7,352},{8,128}... | collective-permute-start | bytes 393224 | tf_op jit(solution)/shard_map/ppermute | solution.py:171
  56.8 20.7 %collective-permute-done.pair = bf16[512,128]{1,0:T(8,128)(2,1)S(1)} collective-permute-done((bf16[512,128]{1,0:T(8,128)(2,1)S(1)}, bf16[512,128]{1,0:T(8,128)(2,1)S(1)}, u32[]{:S(2)}, u32[]{:S(2)}) %collective-permute-start) | collective-permute-done | bytes 131104 | tf_op jit(solution)/shard_map/ppermute | solution.py:171
  77.6 0.9 convolution_convert_fusion
  78.5 11.2 %all-to-all-start.2 = ((bf16[16,16,256]{2,1,0:T(8,128)(2,1)}), bf16[16,16,256]{2,1,0:T(8,128)(2,1)S(1)}, u32[]{:S(2)}, u32[]{:S(2)}) async-start(bf16[16,16,256]{2,1,0:T(8,128)(2,1)} %bitcast.14), calls=%async_computation.2 | async-start | bytes 262144 | tf_op jit(solution)/shard_map/all_to_all | solution.py:23
  89.7 2.3 %collective-permute-start.1 = (bf16[16,16,512]{2,1,0:T(8,128)(2,1)S(1)}, bf16[16,16,512]{2,1,0:T(8,128)(2,1)S(1)}, u32[]{:S(2)}, u32[]{:S(2)}) collective-permute-start(bf16[16,16,512]{2,1,0:T(8,128)(2,1)S(1)} %slice.49), channel_id=1, source_target_pairs={{0,1},{1,0},{2,3},{3,2},{4,5},{5,4},{6,7},{7,6},{8,9},{9,8},{10,11... | collective-permute-start | bytes 786440 | tf_op jit(solution)/shard_map/ppermute | solution.py:191
  92.1 3.3 %all-to-all-done.2 = bf16[16,16,256]{2,1,0:T(8,128)(2,1)S(1)} async-done(((bf16[16,16,256]{2,1,0:T(8,128)(2,1)}), bf16[16,16,256]{2,1,0:T(8,128)(2,1)S(1)}, u32[]{:S(2)}, u32[]{:S(2)}) %all-to-all-start.2) | async-done | bytes 131104 | tf_op jit(solution)/shard_map/all_to_all | solution.py:23
  97.0 5.4 %all-to-all-start.3 = ((bf16[32,4,512]{2,1,0:T(4,128)(2,1)}), bf16[32,4,512]{2,1,0:T(4,128)(2,1)S(1)}, u32[]{:S(2)}, u32[]{:S(2)}) async-start(bf16[32,4,512]{2,1,0:T(4,128)(2,1)} %bitcast.16), calls=%async_computation.3 | async-start | bytes 262144 | tf_op jit(solution)/shard_map/all_to_all | solution.py:23
  103.8 1.3 multiply_reduce_fusion
  105.2 1.4 fusion.1
  107.3 1.4 copy.50
  109.4 7.9 %all-to-all-done.3 = bf16[32,4,512]{2,1,0:T(4,128)(2,1)S(1)} async-done(((bf16[32,4,512]{2,1,0:T(4,128)(2,1)}), bf16[32,4,512]{2,1,0:T(4,128)(2,1)S(1)}, u32[]{:S(2)}, u32[]{:S(2)}) %all-to-all-start.3) | async-done | bytes 131104 | tf_op jit(solution)/shard_map/all_to_all | solution.py:23
  117.4 1.6 shard_map.105
  119.8 4.6 %all-to-all-start.4 = ((bf16[32,40,128]{2,1,0:T(8,128)(2,1)}), bf16[32,40,128]{2,1,0:T(8,128)(2,1)S(1)}, u32[]{:S(2)}, u32[]{:S(2)}) async-start(bf16[32,40,128]{2,1,0:T(8,128)(2,1)} %broadcast_in_dim.51), calls=%async_computation.4 | async-start | bytes 655360 | tf_op jit(solution)/shard_map/all_to_all | solution.py:23
  125.1 13.2 %collective-permute-start.2 = (bf16[512,128]{1,0:T(8,128)(2,1)S(1)}, bf16[512,128]{1,0:T(8,128)(2,1)S(1)}, u32[]{:S(2)}, u32[]{:S(2)}) collective-permute-start(bf16[512,128]{1,0:T(8,128)(2,1)S(1)} %get-tuple-element.15), channel_id=1, source_target_pairs={{0,0},{256,1},{32,2},{288,3},{64,4},{320,5},{96,6},{352,7},{128,8}... | collective-permute-start | bytes 393224 | tf_op jit(solution)/shard_map/ppermute | solution.py:243
  138.3 2.5 %copy.64 = bf16[2048,512]{1,0:T(8,128)(2,1)} copy(bf16[2048,512]{0,1:T(8,128)(2,1)S(1)} %bitcast.108) | data formatting | bytes 4194304 | tf_op jit(solution)/shard_map/jp,jx->px/dot_general | solution.py:262
  140.8 23.9 %collective-permute-done.2 = bf16[512,128]{1,0:T(8,128)(2,1)S(1)} collective-permute-done((bf16[512,128]{1,0:T(8,128)(2,1)S(1)}, bf16[512,128]{1,0:T(8,128)(2,1)S(1)}, u32[]{:S(2)}, u32[]{:S(2)}) %collective-permute-start.2) | collective-permute-done | bytes 131104 | tf_op jit(solution)/shard_map/ppermute | solution.py:243
  167.1 0.9 fusion.2
  (86 shorter events, 14.2 us)
Async XLA Ops:
  0.6 167.4 %copy-start = (bf16[256,64]{0,1:T(8,128)(2,1)S(1)}, bf16[256,64]{0,1:T(8,128)(2,1)}, u32[]{:S(2)}) copy-start(bf16[256,64]{0,1:T(8,128)(2,1)} %param.17) | copy-start | bytes 98308
  0.6 0.9 copy-start.1
  1.6 0.9 copy-start.3
  2.5 0.7 copy-start.6
  5.1 36.1 %all-to-all-start = ((bf16[32,8,512]{2,1,0:T(8,128)(2,1)}), bf16[32,8,512]{2,1,0:T(8,128)(2,1)S(1)}, u32[]{:S(2)}, u32[]{:S(2)}) async-start(bf16[32,8,512]{2,1,0:T(8,128)(2,1)} %bitcast.1), calls=%async_computation | async-start | bytes 524288 | tf_op jit(solution)/shard_map/all_to_all | solution.py:23
  43.8 11.0 %copy-start.4 = (bf16[16,32,128]{2,1,0:T(8,128)(2,1)S(1)}, bf16[16,32,128]{2,1,0:T(8,128)(2,1)}, u32[]{:S(2)}) copy-start(bf16[16,32,128]{2,1,0:T(8,128)(2,1)} %pair.1) | copy-start | bytes 393220
  44.9 47.1 %copy-start.11 = (bf16[128,8]{0,1:T(8,128)(2,1)S(1)}, bf16[128,8]{0,1:T(8,128)(2,1)}, u32[]{:S(2)}) copy-start(bf16[128,8]{0,1:T(8,128)(2,1)} %param.15) | copy-start | bytes 6148
  44.9 32.6 %all-to-all-start.1 = ((bf16[16,48,512]{2,1,0:T(8,128)(2,1)}), bf16[16,48,512]{2,1,0:T(8,128)(2,1)S(1)}, u32[]{:S(2)}, u32[]{:S(2)}) async-start(bf16[16,48,512]{2,1,0:T(8,128)(2,1)} %pad_maximum_fusion), calls=%async_computation.1 | async-start | bytes 1572864 | tf_op jit(solution)/shard_map/all_to_all | solution.py:23
  54.8 22.7 %collective-permute-start = (bf16[512,128]{1,0:T(8,128)(2,1)S(1)}, bf16[512,128]{1,0:T(8,128)(2,1)S(1)}, u32[]{:S(2)}, u32[]{:S(2)}) collective-permute-start(bf16[512,128]{1,0:T(8,128)(2,1)S(1)} %bitcast.106), channel_id=1, source_target_pairs={{0,0},{1,256},{2,32},{3,288},{4,64},{5,320},{6,96},{7,352},{8,128}... | collective-permute-start | bytes 393224 | tf_op jit(solution)/shard_map/ppermute | solution.py:171
  78.5 16.9 %all-to-all-start.2 = ((bf16[16,16,256]{2,1,0:T(8,128)(2,1)}), bf16[16,16,256]{2,1,0:T(8,128)(2,1)S(1)}, u32[]{:S(2)}, u32[]{:S(2)}) async-start(bf16[16,16,256]{2,1,0:T(8,128)(2,1)} %bitcast.14), calls=%async_computation.2 | async-start | bytes 262144 | tf_op jit(solution)/shard_map/all_to_all | solution.py:23
  89.7 12.6 %collective-permute-start.1 = (bf16[16,16,512]{2,1,0:T(8,128)(2,1)S(1)}, bf16[16,16,512]{2,1,0:T(8,128)(2,1)S(1)}, u32[]{:S(2)}, u32[]{:S(2)}) collective-permute-start(bf16[16,16,512]{2,1,0:T(8,128)(2,1)S(1)} %slice.49), channel_id=1, source_target_pairs={{0,1},{1,0},{2,3},{3,2},{4,5},{5,4},{6,7},{7,6},{8,9},{9,8},{10,11... | collective-permute-start | bytes 786440 | tf_op jit(solution)/shard_map/ppermute | solution.py:191
  97.0 20.3 %all-to-all-start.3 = ((bf16[32,4,512]{2,1,0:T(4,128)(2,1)}), bf16[32,4,512]{2,1,0:T(4,128)(2,1)S(1)}, u32[]{:S(2)}, u32[]{:S(2)}) async-start(bf16[32,4,512]{2,1,0:T(4,128)(2,1)} %bitcast.16), calls=%async_computation.3 | async-start | bytes 262144 | tf_op jit(solution)/shard_map/all_to_all | solution.py:23
  105.1 1.4 copy-start.10
  108.7 8.7 %copy-start.2 = (bf16[128,640]{1,0:T(8,128)(2,1)S(1)}, bf16[128,640]{1,0:T(8,128)(2,1)}, u32[]{:S(2)}) copy-start(bf16[128,640]{1,0:T(8,128)(2,1)} %gate_weight.1) | copy-start | bytes 491524
  108.7 8.7 %copy-start.5 = (bf16[128,128]{1,0:T(8,128)(2,1)S(1)}, bf16[128,128]{1,0:T(8,128)(2,1)}, u32[]{:S(2)}) copy-start(bf16[128,128]{1,0:T(8,128)(2,1)} %weight.3) | copy-start | bytes 98308
  108.7 8.7 %copy-start.7 = (s32[512]{0:T(512)S(1)}, s32[512]{0:T(512)}, u32[]{:S(2)}) copy-start(s32[512]{0:T(512)} %mask.3) | copy-start | bytes 6148
  108.7 15.7 %copy-start.9 = (bf16[8,2048]{1,0:T(8,128)(2,1)S(1)}, bf16[8,2048]{1,0:T(8,128)(2,1)}, u32[]{:S(2)}) copy-start(bf16[8,2048]{1,0:T(8,128)(2,1)} %param.10) | copy-start | bytes 98308
  108.7 15.8 %copy-start.12 = (s32[8]{0:T(128)S(1)}, s32[8]{0:T(128)}, u32[]{:S(2)}) copy-start(s32[8]{0:T(128)} %param.12) | copy-start | bytes 100
  119.8 44.9 %all-to-all-start.4 = ((bf16[32,40,128]{2,1,0:T(8,128)(2,1)}), bf16[32,40,128]{2,1,0:T(8,128)(2,1)S(1)}, u32[]{:S(2)}, u32[]{:S(2)}) async-start(bf16[32,40,128]{2,1,0:T(8,128)(2,1)} %broadcast_in_dim.51), calls=%async_computation.4 | async-start | bytes 655360 | tf_op jit(solution)/shard_map/all_to_all | solution.py:23
  125.1 39.6 %collective-permute-start.2 = (bf16[512,128]{1,0:T(8,128)(2,1)S(1)}, bf16[512,128]{1,0:T(8,128)(2,1)S(1)}, u32[]{:S(2)}, u32[]{:S(2)}) collective-permute-start(bf16[512,128]{1,0:T(8,128)(2,1)S(1)} %get-tuple-element.15), channel_id=1, source_target_pairs={{0,0},{256,1},{32,2},{288,3},{64,4},{320,5},{96,6},{352,7},{128,8}... | collective-permute-start | bytes 393224 | tf_op jit(solution)/shard_map/ppermute | solution.py:243
  164.7 1.6 copy-start.8

commit v4 on v2

--- a/solution.py
+++ b/solution.py
@@ -31,8 +31,17 @@
 
 
 def project_kernel(
-    row_size, col_size, mask, pair, weight, sent, gate, wide, mixed
+    row_size, mask_far, pair_far, weight_far, sent, gate, mask, pair, weight, wide, mixed, arrived
 ):
+    copies = [
+        pltpu.make_async_copy(pair_far, pair, arrived.at[0]),
+        pltpu.make_async_copy(weight_far, weight, arrived.at[1]),
+        pltpu.make_async_copy(mask_far, mask, arrived.at[2]),
+    ]
+    for copy in copies:
+        copy.start()
+    for copy in copies:
+        copy.wait()
     rows, columns, channels = pair.shape
     patch = rows * columns
     here = channels // row_size
@@ -139,28 +148,28 @@
     vmem = pl.BlockSpec(memory_space=pltpu.VMEM)
     smem = pl.BlockSpec(memory_space=pltpu.SMEM)
     sent, out_gate = pl.pallas_call(
-        functools.partial(project_kernel, row_size, col_size),
+        functools.partial(project_kernel, row_size),
         out_shape=(
             jax.ShapeDtypeStruct((2 * channels, patch), jnp.bfloat16),
             jax.ShapeDtypeStruct((channels, patch), jnp.float32),
         ),
-        in_specs=[smem, vmem, vmem],
+        in_specs=[pl.BlockSpec(memory_space=pltpu.HBM)] * 3,
         out_specs=(vmem, vmem),
         scratch_shapes=[
+            pltpu.SMEM(token_valid_mask.shape, jnp.int32),
+            pltpu.VMEM(pair_state.shape, jnp.bfloat16),
+            pltpu.VMEM(triangle_input_weight.shape, jnp.bfloat16),
             pltpu.VMEM((patch, channels), jnp.float32),
             pltpu.VMEM((2 * channels, patch), jnp.float32),
+            pltpu.SemaphoreType.DMA((3,)),
         ],
-        compiler_params=pltpu.CompilerParams(vmem_limit_bytes=32 * 1024 * 1024),
+        compiler_params=pltpu.CompilerParams(vmem_limit_bytes=63 * 1024 * 1024),
         cost_estimate=pl.CostEstimate(
             flops=10 * patch * channels * channels, bytes_accessed=2**20, transcendentals=0
         ),
     )(token_valid_mask, pair_state, triangle_input_weight)
 
-    rider, sent = lax.optimization_barrier((sequence_embedding, sent))
     got = exchange(sent.reshape(row_size, 2 * channels_here, patch), "row")
-    sequence_all = exchange(
-        jnp.broadcast_to(rider[None], (col_size,) + rider.shape), "col"
-    ).reshape(col_size, msa_rows, columns_here, features)
     got = got.reshape(row_size, 2, channels_here, columns_here, rows_here)
     got = jnp.transpose(got, (1, 2, 3, 0, 4))
     left = jnp.transpose(
@@ -174,7 +183,17 @@
         [jnp.broadcast_to(left, lead + (left_width,)), jnp.broadcast_to(right, lead + (right_width,))],
         axis=4,
     ).reshape(col_size, columns_here, left_width + right_width)
-    got = exchange(sent, "col").reshape(tokens, left_width + right_width)
+    rider = jnp.tile(
+        sequence_embedding.reshape(2, -1, left_width + right_width), (col_size // 2, 1, 1)
+    )
+    got = exchange(jnp.concatenate([sent, rider], axis=1), "col")
+    half = got[:, columns_here:]
+    half_other = lax.ppermute(half, "col", [(a, a ^ 1) for a in range(col_size)])
+    first = col_index % 2 == 0
+    sequence_all = jnp.concatenate(
+        [jnp.where(first, half, half_other), jnp.where(first, half_other, half)], axis=1
+    ).reshape(col_size, msa_rows, columns_here, features)
+    got = got[:, :columns_here].reshape(tokens, left_width + right_width)
     crossed = jnp.einsum(
         "kj,ki->ji",
         got[:, left_width:],

time: 160 us -> 150 us (0.938)
  the two profiles are of different devices: /device:TPU:32 before, /device:TPU:8 now
where the time goes in v4:
time: 150 us
  waiting for transfers between devices  64.9 us (43%)
  starting transfers between devices  51.6 us (34%)
  local copies, waits for them, and re-layouts  15.3 us (10%)
  other arithmetic  6.39 us (4%)
  matrix products  6.22 us (4%)
  Pallas kernels  4.09 us (3%)
    all_to_all x4, waiting for transfers between devices, exchange(): return lax.all_to_all(blocks, axis, split_axis=0, concat_axis=0, tiled=True)  47.9 us
    all_to_all x4, starting transfers between devices, exchange(): return lax.all_to_all(blocks, axis, split_axis=0, concat_axis=0, tiled=True)  35.1 us
    all_to_all x1, starting transfers between devices, shards(): lax.all_to_all(jnp.broadcast_to(sent[None], (col_size,) + sent.shape), 'r...  9.33 us
    ppermute x1, waiting for transfers between devices, shards(): sent = lax.ppermute(sent, ('row', 'col'), moves)  7.18 us
    all_to_all x1, waiting for transfers between devices, shards(): lax.all_to_all(jnp.broadcast_to(sent[None], (col_size,) + sent.shape), 'r...  7.12 us
    dot_general x2, matrix products, average(): jnp.einsum('jp,jx->px', weights.reshape(tokens, rows_here * heads), value...  3.46 us
    ppermute x1, starting transfers between devices, shards(): sent = lax.ppermute(sent, ('row', 'col'), moves)  3.16 us
  transfers between devices with their start and end apart: 8, of which 7 were waited for; matrix products, arithmetic and copies ran while one was open for 13% of the time, Pallas kernels for 0%

profile of v4, /device:TPU:8, one launch (start us, length us, event | category | flops | bytes accessed | tf_op | source)
XLA Modules:
  0.0 149.6 jit_solution(5398119673701967415)
XLA Ops:
  0.6 2.5 %shard_map.104 = (bf16[256,512]{1,0:T(8,128)(2,1)}, f32[128,512]{1,0:T(8,128)}) custom-call(s32[512]{0:T(512)} %mask.1, bf16[16,32,128]{2,1,0:T(8,128)(2,1)} %pair.1, bf16[128,640]{1,0:T(8,128)(2,1)} %weight_far.1), custom_call_target="tpu_custom_call" | custom-call | flops 83886080 | bytes 1048576 | tf_op jit(solution)/shard_map/pallas_call | solution.py:150
  3.1 16.4 %all-to-all-start = ((bf16[32,8,512]{2,1,0:T(8,128)(2,1)}), bf16[32,8,512]{2,1,0:T(8,128)(2,1)S(1)}, u32[]{:S(2)}, u32[]{:S(2)}) async-start(bf16[32,8,512]{2,1,0:T(8,128)(2,1)} %bitcast.109), calls=%async_computation | async-start | bytes 524288 | tf_op jit(solution)/shard_map/all_to_all | solution.py:23
  21.4 20.4 %all-to-all-done = bf16[32,8,512]{2,1,0:T(8,128)(2,1)S(1)} async-done(((bf16[32,8,512]{2,1,0:T(8,128)(2,1)}), bf16[32,8,512]{2,1,0:T(8,128)(2,1)S(1)}, u32[]{:S(2)}, u32[]{:S(2)}) %all-to-all-start) | async-done | bytes 262176 | tf_op jit(solution)/shard_map/all_to_all | solution.py:23
  45.4 7.2 %all-to-all-start.1 = ((bf16[16,48,512]{2,1,0:T(8,128)(2,1)}), bf16[16,48,512]{2,1,0:T(8,128)(2,1)S(1)}, u32[]{:S(2)}, u32[]{:S(2)}) async-start(bf16[16,48,512]{2,1,0:T(8,128)(2,1)} %pad_maximum_fusion), calls=%async_computation.1 | async-start | bytes 1572864 | tf_op jit(solution)/shard_map/all_to_all | solution.py:23
  53.0 10.7 %all-to-all-done.1 = bf16[16,48,512]{2,1,0:T(8,128)(2,1)S(1)} async-done(((bf16[16,48,512]{2,1,0:T(8,128)(2,1)}), bf16[16,48,512]{2,1,0:T(8,128)(2,1)S(1)}, u32[]{:S(2)}, u32[]{:S(2)}) %all-to-all-start.1) | async-done | bytes 786464 | tf_op jit(solution)/shard_map/all_to_all | solution.py:23
  64.7 7.6 %all-to-all-start.2 = ((bf16[16,16,256]{2,1,0:T(8,128)(2,1)}), bf16[16,16,256]{2,1,0:T(8,128)(2,1)S(1)}, u32[]{:S(2)}, u32[]{:S(2)}) async-start(bf16[16,16,256]{2,1,0:T(8,128)(2,1)} %bitcast.13), calls=%async_computation.2 | async-start | bytes 262144 | tf_op jit(solution)/shard_map/all_to_all | solution.py:23
  72.3 2.1 %collective-permute-start.1 = (bf16[16,16,512]{2,1,0:T(8,128)(2,1)S(1)}, bf16[16,16,512]{2,1,0:T(8,128)(2,1)}, u32[]{:S(2)}, u32[]{:S(2)}) collective-permute-start(bf16[16,16,512]{2,1,0:T(8,128)(2,1)S(1)} %slice.55), channel_id=1, source_target_pairs={{0,1},{1,0},{2,3},{3,2},{4,5},{5,4},{6,7},{7,6},{8,9},{9,8},{10,11... | collective-permute-start | bytes 786440 | tf_op jit(solution)/shard_map/ppermute | solution.py:191
  75.0 3.7 %all-to-all-done.2 = bf16[16,16,256]{2,1,0:T(8,128)(2,1)S(1)} async-done(((bf16[16,16,256]{2,1,0:T(8,128)(2,1)}), bf16[16,16,256]{2,1,0:T(8,128)(2,1)S(1)}, u32[]{:S(2)}, u32[]{:S(2)}) %all-to-all-start.2) | async-done | bytes 131104 | tf_op jit(solution)/shard_map/all_to_all | solution.py:23
  79.7 1.8 %reshape.163 = bf16[32,4,512]{2,1,0:T(4,128)(2,1)} reshape(bf16[2,16,4,2,16,16]{5,4,3,2,1,0:T(8,128)(2,1)S(1)} %bitcast.98) | data formatting | bytes 262144 | tf_op jit(solution)/shard_map/reshape | solution.py:206
  81.4 3.9 %all-to-all-start.3 = ((bf16[32,4,512]{2,1,0:T(4,128)(2,1)}), bf16[32,4,512]{2,1,0:T(4,128)(2,1)S(1)}, u32[]{:S(2)}, u32[]{:S(2)}) async-start(bf16[32,4,512]{2,1,0:T(4,128)(2,1)} %reshape.163), calls=%async_computation.3 | async-start | bytes 262144 | tf_op jit(solution)/shard_map/all_to_all | solution.py:23
  87.4 1.6 %reshape.170 = f32[16,8,32,64]{3,2,1,0:T(8,128)S(1)} reshape(f32[16,32,512]{2,1,0:T(8,128)} %maximum_convert_fusion) | data formatting | bytes 2097152 | tf_op jit(solution)/shard_map/convert_element_type | solution.py:245
  89.7 13.2 %all-to-all-done.3 = bf16[32,4,512]{2,1,0:T(4,128)(2,1)S(1)} async-done(((bf16[32,4,512]{2,1,0:T(4,128)(2,1)}), bf16[32,4,512]{2,1,0:T(4,128)(2,1)S(1)}, u32[]{:S(2)}, u32[]{:S(2)}) %all-to-all-start.3) | async-done | bytes 131104 | tf_op jit(solution)/shard_map/all_to_all | solution.py:23
  103.0 1.6 %shard_map.105 = (bf16[16,32,128]{2,1,0:T(8,128)(2,1)}, f32[40,128]{1,0:T(8,128)S(1)}) custom-call(s32[512]{0:T(512)S(1)} %copy-done.4, s32[4,128]{1,0:T(4,128)S(1)} %bitcast.94, bf16[128,512]{1,0:T(8,128)(2,1)S(1)} %reshape.164.crossed, f32[128,512]{1,0:T(8,128)S(1)} %copy-done.1, bf16[16,32,128]{2,1,0:T(8,128)(2,1)S(1)} %copy-done.2, ...), custom_call_target="tpu_custom_call" | custom-call | flops 33554432 | bytes 1048576 | tf_op jit(solution)/shard_map/pallas_call | solution.py:208
  104.6 3.2 %collective-permute-start = (bf16[40,128]{1,0:T(8,128)(2,1)S(1)}, bf16[40,128]{1,0:T(8,128)(2,1)S(1)}, u32[]{:S(2)}, u32[]{:S(2)}) collective-permute-start(bf16[40,128]{1,0:T(8,128)(2,1)S(1)} %convert_element_type.56), channel_id=1, source_target_pairs={{0,0},{1,16},{2,32},{3,48},{4,64},{5,80},{6,96},{7,112},{8,128},{9... | collective-permute-start | bytes 30728 | tf_op jit(solution)/shard_map/ppermute | solution.py:232
  107.7 7.2 %collective-permute-done = bf16[40,128]{1,0:T(8,128)(2,1)S(1)} collective-permute-done((bf16[40,128]{1,0:T(8,128)(2,1)S(1)}, bf16[40,128]{1,0:T(8,128)(2,1)S(1)}, u32[]{:S(2)}, u32[]{:S(2)}) %collective-permute-start) | collective-permute-done | bytes 10272 | tf_op jit(solution)/shard_map/ppermute | solution.py:232
  115.6 9.3 %all-to-all-start.4 = ((bf16[16,40,128]{2,1,0:T(8,128)(2,1)}), bf16[16,40,128]{2,1,0:T(8,128)(2,1)S(1)}, u32[]{:S(2)}, u32[]{:S(2)}) async-start(bf16[16,40,128]{2,1,0:T(8,128)(2,1)} %broadcast_in_dim.51), calls=%async_computation.4 | async-start | bytes 327680 | tf_op jit(solution)/shard_map/all_to_all | solution.py:234
  125.0 1.3 multiply_reduce_fusion
  126.3 1.5 %convert_bitcast_fusion = bf16[16,32,8,256]{3,1,2,0:T(8,128)(2,1)S(1)} fusion(f32[16,8,32,64]{3,2,1,0:T(8,128)S(1)} %reshape.170, f32[16,8,32]{2,1,0:T(8,128)S(1)} %add_rsqrt_fusion, f32[16,8,32]{2,1,0:T(8,128)S(1)} %broadcast_multiply_fusion, bf16[64,512]{1,0:T(8,128)(2,1)S(1)} %copy-done.6), kind=kOutput, calls=%fused_computation | convolution fusion | flops 136052736 | bytes 4358144 | tf_op jit(solution)/shard_map/qsjf,fg->qjsg/dot_general | solution.py:246
  127.8 1.4 copy.60
  130.0 2.5 %copy.71 = bf16[2048,512]{1,0:T(8,128)(2,1)} copy(bf16[2048,512]{0,1:T(8,128)(2,1)S(1)} %bitcast.96) | data formatting | bytes 4194304 | tf_op jit(solution)/shard_map/jp,jx->px/dot_general | solution.py:262
  132.5 7.1 %all-to-all-done.4 = bf16[16,40,128]{2,1,0:T(8,128)(2,1)S(1)} async-done(((bf16[16,40,128]{2,1,0:T(8,128)(2,1)}), bf16[16,40,128]{2,1,0:T(8,128)(2,1)S(1)}, u32[]{:S(2)}, u32[]{:S(2)}) %all-to-all-start.4) | async-done | bytes 163872 | tf_op jit(solution)/shard_map/all_to_all | solution.py:234
  140.0 1.9 %collective-permute-start.2 = (bf16[16,40,128]{2,0,1:T(8,128)(2,1)S(1)}, bf16[16,40,128]{2,0,1:T(8,128)(2,1)S(1)}, u32[]{:S(2)}, u32[]{:S(2)}) collective-permute-start(bf16[16,40,128]{2,0,1:T(8,128)(2,1)S(1)} %get-tuple-element.17), channel_id=1, source_target_pairs={{0,256},{16,272},{32,288},{48,304},{64,320},{80,336},{96,352},{112... | collective-permute-start | bytes 491528 | tf_op jit(solution)/shard_map/ppermute | solution.py:243
  141.9 2.6 %fusion = f32[16,8,256]{2,1,0:T(8,128)S(1)} fusion(bf16[8,256,512,1]{2,1,0,3:T(8,128)(2,1)} %bitcast.102, pred[8,256]{1,0:T(8,128)(4,1)S(1)} %iota_compare_fusion, bf16[128,512]{1,0:T(8,128)(2,1)S(1)} %copy.59), kind=kOutput, calls=%fused_computation.5 | convolution fusion | flops 268926976 | bytes 2361344 | tf_op jit(solution)/shard_map/jp,jx->px/dot_general | solution.py:262
  144.5 2.7 %collective-permute-done.2 = bf16[16,40,128]{2,0,1:T(8,128)(2,1)S(1)} collective-permute-done((bf16[16,40,128]{2,0,1:T(8,128)(2,1)S(1)}, bf16[16,40,128]{2,0,1:T(8,128)(2,1)S(1)}, u32[]{:S(2)}, u32[]{:S(2)}) %collective-permute-start.2) | collective-permute-done | bytes 163872 | tf_op jit(solution)/shard_map/ppermute | solution.py:243
  (81 shorter events, 15.1 us)
Async XLA Ops:
  0.6 147.8 %copy-start = (bf16[256,64]{0,1:T(8,128)(2,1)S(1)}, bf16[256,64]{0,1:T(8,128)(2,1)}, u32[]{:S(2)}) copy-start(bf16[256,64]{0,1:T(8,128)(2,1)} %param.17) | copy-start | bytes 98308
  3.1 38.7 %all-to-all-start = ((bf16[32,8,512]{2,1,0:T(8,128)(2,1)}), bf16[32,8,512]{2,1,0:T(8,128)(2,1)S(1)}, u32[]{:S(2)}, u32[]{:S(2)}) async-start(bf16[32,8,512]{2,1,0:T(8,128)(2,1)} %bitcast.109), calls=%async_computation | async-start | bytes 524288 | tf_op jit(solution)/shard_map/all_to_all | solution.py:23
  44.4 8.5 %copy-start.8 = (bf16[128,8]{0,1:T(8,128)(2,1)S(1)}, bf16[128,8]{0,1:T(8,128)(2,1)}, u32[]{:S(2)}) copy-start(bf16[128,8]{0,1:T(8,128)(2,1)} %param.15) | copy-start | bytes 6148
  45.4 29.0 %copy-start.9 = (s32[8]{0:T(128)S(1)}, s32[8]{0:T(128)}, u32[]{:S(2)}) copy-start(s32[8]{0:T(128)} %param.12) | copy-start | bytes 100
  45.4 18.3 %all-to-all-start.1 = ((bf16[16,48,512]{2,1,0:T(8,128)(2,1)}), bf16[16,48,512]{2,1,0:T(8,128)(2,1)S(1)}, u32[]{:S(2)}, u32[]{:S(2)}) async-start(bf16[16,48,512]{2,1,0:T(8,128)(2,1)} %pad_maximum_fusion), calls=%async_computation.1 | async-start | bytes 1572864 | tf_op jit(solution)/shard_map/all_to_all | solution.py:23
  64.7 14.0 %all-to-all-start.2 = ((bf16[16,16,256]{2,1,0:T(8,128)(2,1)}), bf16[16,16,256]{2,1,0:T(8,128)(2,1)S(1)}, u32[]{:S(2)}, u32[]{:S(2)}) async-start(bf16[16,16,256]{2,1,0:T(8,128)(2,1)} %bitcast.13), calls=%async_computation.2 | async-start | bytes 262144 | tf_op jit(solution)/shard_map/all_to_all | solution.py:23
  72.3 13.1 %collective-permute-start.1 = (bf16[16,16,512]{2,1,0:T(8,128)(2,1)S(1)}, bf16[16,16,512]{2,1,0:T(8,128)(2,1)}, u32[]{:S(2)}, u32[]{:S(2)}) collective-permute-start(bf16[16,16,512]{2,1,0:T(8,128)(2,1)S(1)} %slice.55), channel_id=1, source_target_pairs={{0,1},{1,0},{2,3},{3,2},{4,5},{5,4},{6,7},{7,6},{8,9},{9,8},{10,11... | collective-permute-start | bytes 786440 | tf_op jit(solution)/shard_map/ppermute | solution.py:191
  81.4 21.4 %all-to-all-start.3 = ((bf16[32,4,512]{2,1,0:T(4,128)(2,1)}), bf16[32,4,512]{2,1,0:T(4,128)(2,1)S(1)}, u32[]{:S(2)}, u32[]{:S(2)}) async-start(bf16[32,4,512]{2,1,0:T(4,128)(2,1)} %reshape.163), calls=%async_computation.3 | async-start | bytes 262144 | tf_op jit(solution)/shard_map/all_to_all | solution.py:23
  87.4 15.5 %copy-start.1 = (f32[128,512]{1,0:T(8,128)S(1)}, f32[128,512]{1,0:T(8,128)}, u32[]{:S(2)}) copy-start(f32[128,512]{1,0:T(8,128)} %get-tuple-element.7.gate) | copy-start | bytes 786436
  87.4 15.5 %copy-start.2 = (bf16[16,32,128]{2,1,0:T(8,128)(2,1)S(1)}, bf16[16,32,128]{2,1,0:T(8,128)(2,1)}, u32[]{:S(2)}) copy-start(bf16[16,32,128]{2,1,0:T(8,128)(2,1)} %pair.1) | copy-start | bytes 393220
  87.4 15.5 %copy-start.3 = (bf16[128,128]{1,0:T(8,128)(2,1)S(1)}, bf16[128,128]{1,0:T(8,128)(2,1)}, u32[]{:S(2)}) copy-start(bf16[128,128]{1,0:T(8,128)(2,1)} %weight.1) | copy-start | bytes 98308
  87.4 15.5 %copy-start.4 = (s32[512]{0:T(512)S(1)}, s32[512]{0:T(512)}, u32[]{:S(2)}) copy-start(s32[512]{0:T(512)} %mask.1) | copy-start | bytes 6148
  89.7 36.6 %copy-start.6 = (bf16[64,512]{1,0:T(8,128)(2,1)S(1)}, bf16[64,512]{1,0:T(8,128)(2,1)}, u32[]{:S(2)}) copy-start(bf16[64,512]{1,0:T(8,128)(2,1)} %param.16) | copy-start | bytes 196612
  104.6 10.4 %collective-permute-start = (bf16[40,128]{1,0:T(8,128)(2,1)S(1)}, bf16[40,128]{1,0:T(8,128)(2,1)S(1)}, u32[]{:S(2)}, u32[]{:S(2)}) collective-permute-start(bf16[40,128]{1,0:T(8,128)(2,1)S(1)} %convert_element_type.56), channel_id=1, source_target_pairs={{0,0},{1,16},{2,32},{3,48},{4,64},{5,80},{6,96},{7,112},{8,128},{9... | collective-permute-start | bytes 30728 | tf_op jit(solution)/shard_map/ppermute | solution.py:232
  115.6 24.0 %all-to-all-start.4 = ((bf16[16,40,128]{2,1,0:T(8,128)(2,1)}), bf16[16,40,128]{2,1,0:T(8,128)(2,1)S(1)}, u32[]{:S(2)}, u32[]{:S(2)}) async-start(bf16[16,40,128]{2,1,0:T(8,128)(2,1)} %broadcast_in_dim.51), calls=%async_computation.4 | async-start | bytes 327680 | tf_op jit(solution)/shard_map/all_to_all | solution.py:234
  140.0 7.2 %collective-permute-start.2 = (bf16[16,40,128]{2,0,1:T(8,128)(2,1)S(1)}, bf16[16,40,128]{2,0,1:T(8,128)(2,1)S(1)}, u32[]{:S(2)}, u32[]{:S(2)}) collective-permute-start(bf16[16,40,128]{2,0,1:T(8,128)(2,1)S(1)} %get-tuple-element.17), channel_id=1, source_target_pairs={{0,256},{16,272},{32,288},{48,304},{64,320},{80,336},{96,352},{112... | collective-permute-start | bytes 491528 | tf_op jit(solution)/shard_map/ppermute | solution.py:243
  141.9 5.7 %copy-start.5 = (bf16[2048,512]{1,0:T(8,128)(2,1)S(1)}, bf16[2048,512]{1,0:T(8,128)(2,1)}, u32[]{:S(2)}) copy-start(bf16[2048,512]{1,0:T(8,128)(2,1)} %copy.71) | copy-start | bytes 6291460
  147.2 1.2 copy-start.7
  147.2 1.2 copy-start.10

commit v5 on v4

--- a/solution.py
+++ b/solution.py
@@ -2,6 +2,7 @@
 
 import jax
 import jax.numpy as jnp
+import numpy as np
 from jax import lax
 from jax.experimental import pallas as pl
 from jax.experimental.pallas import tpu as pltpu
@@ -110,6 +111,57 @@
     top = jnp.max(scores, axis=0, keepdims=True).astype(jnp.bfloat16).astype(jnp.float32)
     spread[:columns, :] = jnp.exp(scores - top)
     spread[columns:, :] = jnp.broadcast_to(top, (spread.shape[0] - columns, lanes))
+
+
+def average_kernel(value_width, places, got, values, averaged, wide, ordered):
+    blocks, deep, lanes = got.shape
+    columns = deep - 8
+    rows, across = averaged.shape
+    heads = lanes // rows
+    wide[...] = got[...].astype(jnp.float32)
+    top = jnp.max(wide[:, columns : columns + 1, :], axis=0)
+    total = jnp.zeros((1, lanes), jnp.float32)
+    for block in range(blocks):
+        place = places[block]
+        factor = jnp.exp(wide[place, columns : columns + 1, :] - top)
+        piece = wide[place, :columns, :] * factor
+        total = total + jnp.sum(piece, axis=0, keepdims=True)
+        ordered[block * columns : (block + 1) * columns, :] = piece
+    weights = (ordered[...] / total).astype(jnp.bfloat16)
+    own = lax.broadcasted_iota(jnp.int32, (lanes, value_width), 0) % heads == (
+        lax.broadcasted_iota(jnp.int32, (lanes, value_width), 1) // (value_width // heads)
+    )
+    for start in range(0, across, value_width):
+        product = lax.dot_general(
+            weights,
+            values[:, start : start + value_width],
+            (((0,), (0,)), ((), ())),
+            preferred_element_type=jnp.float32,
+        )
+        product = jnp.where(own, product, 0.0).reshape(rows, heads, value_width)
+        averaged[:, start : start + value_width] = jnp.sum(product, axis=1)
+
+
+def ring(a, b, size):
+    return min((a - b) % size, (b - a) % size)
+
+
+def score_places(row_size, col_size):
+    around = col_size // 4
+    offsets = sorted(range(-(col_size // 2) + 1, col_size // 2 + 1), key=abs)
+    places = np.zeros((col_size, 2, col_size), np.int32)
+    for row in range(row_size):
+        to_col, to_x = row // 2, row % 2
+
+        def far(col):
+            x = ring(2 * (col // (col_size // 2)) + row // col_size,
+                     2 * (to_col // (col_size // 2)) + to_x, 4)
+            return x + ring(col // 2 % around, to_col // 2 % around, around) + (col ^ to_col) % 2
+
+        order = sorted(range(col_size), key=far, reverse=True)
+        for offset, col in zip(offsets, order):
+            places[to_col, to_x, col] = (row + offset) % col_size
+    return places
 
 
 def shards(
@@ -139,11 +191,12 @@
     left_parts = col_size // channels_here // fanout
     left_width = tokens // left_parts
     right_width = tokens // fanout
+    places = score_places(row_size, col_size)
     moves = []
     for row in range(row_size):
         for col in range(col_size):
-            target = ((row % fanout) * col_size + col) * col_size + row // fanout
-            moves.append((row * col_size + col, target))
+            to_row = row % fanout * col_size + int(places[row // fanout, row % fanout, col])
+            moves.append((row * col_size + col, to_row * col_size + row // fanout))
 
     vmem = pl.BlockSpec(memory_space=pltpu.VMEM)
     smem = pl.BlockSpec(memory_space=pltpu.SMEM)
@@ -249,26 +302,31 @@
         sequence_entry_matrix[:, :value_width],
         preferred_element_type=jnp.float32,
     ).astype(jnp.bfloat16).reshape(tokens, msa_rows * value_width)
-    own = (
-        lax.broadcasted_iota(jnp.int32, (heads, 1, value_width), 2) // (value_width // heads)
-        == lax.broadcasted_iota(jnp.int32, (heads, 1, value_width), 0)
-    )
-
-    def average(got):
-        got = got.astype(jnp.float32)
-        tops = got[:, columns_here : columns_here + 1]
-        exponent = got[:, :columns_here] * jnp.exp(tops - jnp.max(tops, axis=0, keepdims=True))
-        weights = (exponent / jnp.sum(exponent, axis=(0, 1), keepdims=True)).astype(jnp.bfloat16)
-        averaged = jnp.einsum(
-            "jp,jx->px",
-            weights.reshape(tokens, rows_here * heads),
-            values,
-            preferred_element_type=jnp.float32,
-        ).reshape(rows_here, heads, msa_rows, value_width)
-        return jnp.sum(jnp.where(own[None], averaged, 0.0), axis=1)
-
-    mine = average(mine)
-    other = average(other)
+    places = lax.dynamic_index_in_dim(jnp.asarray(places), col_index, 0, keepdims=False)
+    half_index = row_index // col_size
+
+    def average(got, which):
+        return pl.pallas_call(
+            functools.partial(average_kernel, value_width),
+            out_shape=jax.ShapeDtypeStruct((rows_here, msa_rows * value_width), jnp.float32),
+            in_specs=[smem, vmem, vmem],
+            out_specs=vmem,
+            scratch_shapes=[
+                pltpu.VMEM(got.shape, jnp.float32),
+                pltpu.VMEM((tokens, rows_here * heads), jnp.float32),
+            ],
+            compiler_params=pltpu.CompilerParams(vmem_limit_bytes=32 * 1024 * 1024),
+            cost_estimate=pl.CostEstimate(
+                flops=2 * tokens * rows_here * heads * msa_rows * value_width,
+                bytes_accessed=3 * 2**20,
+                transcendentals=0,
+            ),
+        )(
+            lax.dynamic_index_in_dim(places, which, 0, keepdims=False), got, values
+        ).reshape(rows_here, msa_rows, value_width)
+
+    mine = average(mine, half_index)
+    other = average(other, 1 - half_index)
     low = row_index < col_size
     averaged = jnp.concatenate(
         [jnp.where(low, mine, other), jnp.where(low, other, mine)], axis=0

time: 150 us -> 149 us (level)
  the two profiles are of different devices: /device:TPU:8 before, /device:TPU:32 now
where the time goes in v5:
time: 149 us; the launch traced here: 148 us
  waiting for transfers between devices  70.8 us (48%)
  starting transfers between devices  47.5 us (32%)
  local copies, waits for them, and re-layouts  12 us (8%)
  other arithmetic  7.13 us (5%)
  Pallas kernels  6.57 us (4%)
  matrix products  2.76 us (2%)
    all_to_all x4, waiting for transfers between devices, exchange(): return lax.all_to_all(blocks, axis, split_axis=0, concat_axis=0, tiled=True)  51.6 us
    all_to_all x4, starting transfers between devices, exchange(): return lax.all_to_all(blocks, axis, split_axis=0, concat_axis=0, tiled=True)  31.5 us
    all_to_all x1, waiting for transfers between devices, shards(): lax.all_to_all(jnp.broadcast_to(sent[None], (col_size,) + sent.shape), 'r...  12.7 us
    all_to_all x1, starting transfers between devices, shards(): lax.all_to_all(jnp.broadcast_to(sent[None], (col_size,) + sent.shape), 'r...  7.99 us
    ppermute x1, waiting for transfers between devices, shards(): sent = lax.ppermute(sent, ('row', 'col'), moves)  6.41 us
    ppermute x1, starting transfers between devices, shards(): other = lax.ppermute(mine, 'row', swap)  3.11 us
  transfers between devices with their start and end apart: 8, of which 6 were waited for; matrix products, arithmetic and copies ran while one was open for 10% of the time, Pallas kernels for 1%

profile of v5, /device:TPU:32, one launch (start us, length us, event | category | flops | bytes accessed | tf_op | source)
XLA Modules:
  0.0 147.9 jit_solution(10255424363193044462)
XLA Ops:
  0.6 2.5 %shard_map.113 = (bf16[256,512]{1,0:T(8,128)(2,1)}, f32[128,512]{1,0:T(8,128)}) custom-call(s32[512]{0:T(512)} %mask.1, bf16[16,32,128]{2,1,0:T(8,128)(2,1)} %pair.1, bf16[128,640]{1,0:T(8,128)(2,1)} %weight_far.1), custom_call_target="tpu_custom_call" | custom-call | flops 83886080 | bytes 1048576 | tf_op jit(solution)/shard_map/pallas_call | solution.py:203
  3.1 16.3 %all-to-all-start = ((bf16[32,8,512]{2,1,0:T(8,128)(2,1)}), bf16[32,8,512]{2,1,0:T(8,128)(2,1)S(1)}, u32[]{:S(2)}, u32[]{:S(2)}) async-start(bf16[32,8,512]{2,1,0:T(8,128)(2,1)} %bitcast.84), calls=%async_computation | async-start | bytes 524288 | tf_op jit(solution)/shard_map/all_to_all | solution.py:24
  20.2 20.3 %all-to-all-done = bf16[32,8,512]{2,1,0:T(8,128)(2,1)S(1)} async-done(((bf16[32,8,512]{2,1,0:T(8,128)(2,1)}), bf16[32,8,512]{2,1,0:T(8,128)(2,1)S(1)}, u32[]{:S(2)}, u32[]{:S(2)}) %all-to-all-start) | async-done | bytes 262176 | tf_op jit(solution)/shard_map/all_to_all | solution.py:24
  44.1 6.7 %all-to-all-start.1 = ((bf16[16,48,512]{2,1,0:T(8,128)(2,1)}), bf16[16,48,512]{2,1,0:T(8,128)(2,1)S(1)}, u32[]{:S(2)}, u32[]{:S(2)}) async-start(bf16[16,48,512]{2,1,0:T(8,128)(2,1)} %pad_maximum_fusion), calls=%async_computation.1 | async-start | bytes 1572864 | tf_op jit(solution)/shard_map/all_to_all | solution.py:24
  51.4 14.7 %all-to-all-done.1 = bf16[16,48,512]{2,1,0:T(8,128)(2,1)S(1)} async-done(((bf16[16,48,512]{2,1,0:T(8,128)(2,1)}), bf16[16,48,512]{2,1,0:T(8,128)(2,1)S(1)}, u32[]{:S(2)}, u32[]{:S(2)}) %all-to-all-start.1) | async-done | bytes 786464 | tf_op jit(solution)/shard_map/all_to_all | solution.py:24
  67.1 3.5 %all-to-all-start.2 = ((bf16[16,16,256]{2,1,0:T(8,128)(2,1)}), bf16[16,16,256]{2,1,0:T(8,128)(2,1)S(1)}, u32[]{:S(2)}, u32[]{:S(2)}) async-start(bf16[16,16,256]{2,1,0:T(8,128)(2,1)} %bitcast.13), calls=%async_computation.2 | async-start | bytes 262144 | tf_op jit(solution)/shard_map/all_to_all | solution.py:24
  71.9 2.2 %collective-permute-start.1 = (bf16[16,16,512]{2,1,0:T(8,128)(2,1)}, bf16[16,16,512]{2,1,0:T(8,128)(2,1)}, u32[]{:S(2)}, u32[]{:S(2)}) collective-permute-start(bf16[16,16,512]{2,1,0:T(8,128)(2,1)} %slice.37), channel_id=1, source_target_pairs={{0,1},{1,0},{2,3},{3,2},{4,5},{5,4},{6,7},{7,6},{8,9},{9,8},{10,11... | collective-permute-start | bytes 786440 | tf_op jit(solution)/shard_map/ppermute | solution.py:244
  74.1 4.7 %all-to-all-done.2 = bf16[16,16,256]{2,1,0:T(8,128)(2,1)S(1)} async-done(((bf16[16,16,256]{2,1,0:T(8,128)(2,1)}), bf16[16,16,256]{2,1,0:T(8,128)(2,1)S(1)}, u32[]{:S(2)}, u32[]{:S(2)}) %all-to-all-start.2) | async-done | bytes 131104 | tf_op jit(solution)/shard_map/all_to_all | solution.py:24
  79.8 1.8 %reshape.98 = bf16[32,4,512]{2,1,0:T(4,128)(2,1)} reshape(bf16[2,16,4,2,16,16]{5,4,3,2,1,0:T(8,128)(2,1)S(1)} %bitcast.75) | data formatting | bytes 262144 | tf_op jit(solution)/shard_map/reshape | solution.py:259
  81.6 4.9 %all-to-all-start.3 = ((bf16[32,4,512]{2,1,0:T(4,128)(2,1)}), bf16[32,4,512]{2,1,0:T(4,128)(2,1)S(1)}, u32[]{:S(2)}, u32[]{:S(2)}) async-start(bf16[32,4,512]{2,1,0:T(4,128)(2,1)} %reshape.98), calls=%async_computation.3 | async-start | bytes 262144 | tf_op jit(solution)/shard_map/all_to_all | solution.py:24
  88.1 1.4 multiply_convert_fusion.2
  89.5 1.0 broadcast_select_fusion.1
  90.5 12.0 %all-to-all-done.3 = bf16[32,4,512]{2,1,0:T(4,128)(2,1)S(1)} async-done(((bf16[32,4,512]{2,1,0:T(4,128)(2,1)}), bf16[32,4,512]{2,1,0:T(4,128)(2,1)S(1)}, u32[]{:S(2)}, u32[]{:S(2)}) %all-to-all-start.3) | async-done | bytes 131104 | tf_op jit(solution)/shard_map/all_to_all | solution.py:24
  102.7 1.6 %shard_map.114 = (bf16[16,32,128]{2,1,0:T(8,128)(2,1)}, f32[40,128]{1,0:T(8,128)S(1)}) custom-call(s32[512]{0:T(512)S(1)} %copy-done.4, s32[4,128]{1,0:T(4,128)S(1)} %bitcast.72, bf16[128,512]{1,0:T(8,128)(2,1)S(1)} %reshape.99.crossed, f32[128,512]{1,0:T(8,128)S(1)} %copy-done.1, bf16[16,32,128]{2,1,0:T(8,128)(2,1)S(1)} %copy-done.2, ...), custom_call_target="tpu_custom_call" | custom-call | flops 33554432 | bytes 1048576 | tf_op jit(solution)/shard_map/pallas_call | solution.py:261
  104.3 2.8 %collective-permute-start = (bf16[40,128]{1,0:T(8,128)(2,1)S(1)}, bf16[40,128]{1,0:T(8,128)(2,1)S(1)}, u32[]{:S(2)}, u32[]{:S(2)}) collective-permute-start(bf16[40,128]{1,0:T(8,128)(2,1)S(1)} %convert_element_type.44), channel_id=1, source_target_pairs={{0,128},{1,96},{2,144},{3,64},{4,176},{5,32},{6,112},{7,80},{8,160... | collective-permute-start | bytes 30728 | tf_op jit(solution)/shard_map/ppermute | solution.py:285
  108.2 6.4 %collective-permute-done = bf16[40,128]{1,0:T(8,128)(2,1)S(1)} collective-permute-done((bf16[40,128]{1,0:T(8,128)(2,1)S(1)}, bf16[40,128]{1,0:T(8,128)(2,1)S(1)}, u32[]{:S(2)}, u32[]{:S(2)}) %collective-permute-start) | collective-permute-done | bytes 10272 | tf_op jit(solution)/shard_map/ppermute | solution.py:285
  115.3 8.0 %all-to-all-start.4 = ((bf16[16,40,128]{2,1,0:T(8,128)(2,1)}), bf16[16,40,128]{2,1,0:T(8,128)(2,1)S(1)}, u32[]{:S(2)}, u32[]{:S(2)}) async-start(bf16[16,40,128]{2,1,0:T(8,128)(2,1)} %broadcast_in_dim.11), calls=%async_computation.4 | async-start | bytes 327680 | tf_op jit(solution)/shard_map/all_to_all | solution.py:287
  123.3 1.3 multiply_reduce_fusion
  124.7 12.7 %all-to-all-done.4.got = bf16[16,40,128]{2,1,0:T(8,128)(2,1)S(1)} async-done(((bf16[16,40,128]{2,1,0:T(8,128)(2,1)}), bf16[16,40,128]{2,1,0:T(8,128)(2,1)S(1)}, u32[]{:S(2)}, u32[]{:S(2)}) %all-to-all-start.4) | async-done | bytes 163872 | tf_op jit(solution)/shard_map/all_to_all | solution.py:287
  137.4 3.1 %collective-permute-start.2 = (bf16[16,40,128]{2,1,0:T(8,128)(2,1)S(1)}, bf16[16,40,128]{2,1,0:T(8,128)(2,1)S(1)}, u32[]{:S(2)}, u32[]{:S(2)}) collective-permute-start(bf16[16,40,128]{2,1,0:T(8,128)(2,1)S(1)} %all-to-all-done.4.got), channel_id=1, source_target_pairs={{0,256},{16,272},{32,288},{48,304},{64,320},{80,336},{96,352},{112... | collective-permute-start | bytes 491528 | tf_op jit(solution)/shard_map/ppermute | solution.py:296
  140.5 1.5 %convert_bitcast_fusion = bf16[16,32,8,256]{3,1,2,0:T(8,128)(2,1)S(1)} fusion(f32[16,8,32,64]{3,2,1,0:T(8,128)S(1)} %reshape.103, f32[16,8,32]{2,1,0:T(8,128)S(1)} %add_rsqrt_fusion, f32[16,8,32]{2,1,0:T(8,128)S(1)} %broadcast_multiply_fusion, bf16[64,512]{1,0:T(8,128)(2,1)S(1)} %copy-done.7), kind=kOutput, calls=%fused_computation | convolution fusion | flops 136052736 | bytes 4358144 | tf_op jit(solution)/shard_map/qsjf,fg->qjsg/dot_general | solution.py:299
  142.1 1.4 copy.46
  144.2 1.2 shard_map.115
  145.4 1.2 shard_map.116
  (62 shorter events, 13.4 us)
Async XLA Ops:
  0.6 146.2 %copy-start = (bf16[256,64]{0,1:T(8,128)(2,1)S(1)}, bf16[256,64]{0,1:T(8,128)(2,1)}, u32[]{:S(2)}) copy-start(bf16[256,64]{0,1:T(8,128)(2,1)} %param.18) | copy-start | bytes 98308
  3.1 37.3 %all-to-all-start = ((bf16[32,8,512]{2,1,0:T(8,128)(2,1)}), bf16[32,8,512]{2,1,0:T(8,128)(2,1)S(1)}, u32[]{:S(2)}, u32[]{:S(2)}) async-start(bf16[32,8,512]{2,1,0:T(8,128)(2,1)} %bitcast.84), calls=%async_computation | async-start | bytes 524288 | tf_op jit(solution)/shard_map/all_to_all | solution.py:24
  43.1 7.8 %copy-start.5 = (bf16[8,2048]{1,0:T(8,128)(2,1)S(1)}, bf16[8,2048]{1,0:T(8,128)(2,1)}, u32[]{:S(2)}) copy-start(bf16[8,2048]{1,0:T(8,128)(2,1)} %param.11) | copy-start | bytes 98308
  43.1 8.2 %copy-start.8 = (bf16[128,8]{0,1:T(8,128)(2,1)S(1)}, bf16[128,8]{0,1:T(8,128)(2,1)}, u32[]{:S(2)}) copy-start(bf16[128,8]{0,1:T(8,128)(2,1)} %param.16) | copy-start | bytes 6148
  44.1 21.9 %all-to-all-start.1 = ((bf16[16,48,512]{2,1,0:T(8,128)(2,1)}), bf16[16,48,512]{2,1,0:T(8,128)(2,1)S(1)}, u32[]{:S(2)}, u32[]{:S(2)}) async-start(bf16[16,48,512]{2,1,0:T(8,128)(2,1)} %pad_maximum_fusion), calls=%async_computation.1 | async-start | bytes 1572864 | tf_op jit(solution)/shard_map/all_to_all | solution.py:24
  67.1 11.7 %all-to-all-start.2 = ((bf16[16,16,256]{2,1,0:T(8,128)(2,1)}), bf16[16,16,256]{2,1,0:T(8,128)(2,1)S(1)}, u32[]{:S(2)}, u32[]{:S(2)}) async-start(bf16[16,16,256]{2,1,0:T(8,128)(2,1)} %bitcast.13), calls=%async_computation.2 | async-start | bytes 262144 | tf_op jit(solution)/shard_map/all_to_all | solution.py:24
  71.9 17.6 %collective-permute-start.1 = (bf16[16,16,512]{2,1,0:T(8,128)(2,1)}, bf16[16,16,512]{2,1,0:T(8,128)(2,1)}, u32[]{:S(2)}, u32[]{:S(2)}) collective-permute-start(bf16[16,16,512]{2,1,0:T(8,128)(2,1)} %slice.37), channel_id=1, source_target_pairs={{0,1},{1,0},{2,3},{3,2},{4,5},{5,4},{6,7},{7,6},{8,9},{9,8},{10,11... | collective-permute-start | bytes 786440 | tf_op jit(solution)/shard_map/ppermute | solution.py:244
  79.5 23.2 %copy-start.1 = (f32[128,512]{1,0:T(8,128)S(1)}, f32[128,512]{1,0:T(8,128)}, u32[]{:S(2)}) copy-start(f32[128,512]{1,0:T(8,128)} %get-tuple-element.7.gate) | copy-start | bytes 786436
  79.5 23.2 %copy-start.2 = (bf16[16,32,128]{2,1,0:T(8,128)(2,1)S(1)}, bf16[16,32,128]{2,1,0:T(8,128)(2,1)}, u32[]{:S(2)}) copy-start(bf16[16,32,128]{2,1,0:T(8,128)(2,1)} %pair.1) | copy-start | bytes 393220
  79.5 23.2 %copy-start.3 = (bf16[128,128]{1,0:T(8,128)(2,1)S(1)}, bf16[128,128]{1,0:T(8,128)(2,1)}, u32[]{:S(2)}) copy-start(bf16[128,128]{1,0:T(8,128)(2,1)} %weight.1) | copy-start | bytes 98308
  79.5 23.2 %copy-start.4 = (s32[512]{0:T(512)S(1)}, s32[512]{0:T(512)}, u32[]{:S(2)}) copy-start(s32[512]{0:T(512)} %mask.1) | copy-start | bytes 6148
  81.6 21.0 %all-to-all-start.3 = ((bf16[32,4,512]{2,1,0:T(4,128)(2,1)}), bf16[32,4,512]{2,1,0:T(4,128)(2,1)S(1)}, u32[]{:S(2)}, u32[]{:S(2)}) async-start(bf16[32,4,512]{2,1,0:T(4,128)(2,1)} %reshape.98), calls=%async_computation.3 | async-start | bytes 262144 | tf_op jit(solution)/shard_map/all_to_all | solution.py:24
  104.3 10.4 %collective-permute-start = (bf16[40,128]{1,0:T(8,128)(2,1)S(1)}, bf16[40,128]{1,0:T(8,128)(2,1)S(1)}, u32[]{:S(2)}, u32[]{:S(2)}) collective-permute-start(bf16[40,128]{1,0:T(8,128)(2,1)S(1)} %convert_element_type.44), channel_id=1, source_target_pairs={{0,128},{1,96},{2,144},{3,64},{4,176},{5,32},{6,112},{7,80},{8,160... | collective-permute-start | bytes 30728 | tf_op jit(solution)/shard_map/ppermute | solution.py:285
  107.6 32.9 %copy-start.7 = (bf16[64,512]{1,0:T(8,128)(2,1)S(1)}, bf16[64,512]{1,0:T(8,128)(2,1)}, u32[]{:S(2)}) copy-start(bf16[64,512]{1,0:T(8,128)(2,1)} %param.17) | copy-start | bytes 196612
  115.3 22.1 %all-to-all-start.4 = ((bf16[16,40,128]{2,1,0:T(8,128)(2,1)}), bf16[16,40,128]{2,1,0:T(8,128)(2,1)S(1)}, u32[]{:S(2)}, u32[]{:S(2)}) async-start(bf16[16,40,128]{2,1,0:T(8,128)(2,1)} %broadcast_in_dim.11), calls=%async_computation.4 | async-start | bytes 327680 | tf_op jit(solution)/shard_map/all_to_all | solution.py:287
  137.4 8.0 %collective-permute-start.2 = (bf16[16,40,128]{2,1,0:T(8,128)(2,1)S(1)}, bf16[16,40,128]{2,1,0:T(8,128)(2,1)S(1)}, u32[]{:S(2)}, u32[]{:S(2)}) collective-permute-start(bf16[16,40,128]{2,1,0:T(8,128)(2,1)S(1)} %all-to-all-done.4.got), channel_id=1, source_target_pairs={{0,256},{16,272},{32,288},{48,304},{64,320},{80,336},{96,352},{112... | collective-permute-start | bytes 491528 | tf_op jit(solution)/shard_map/ppermute | solution.py:296
  145.4 1.4 copy-start.6

commit v6 on v5

--- a/solution.py
+++ b/solution.py
@@ -32,7 +32,7 @@
 
 
 def project_kernel(
-    row_size, mask_far, pair_far, weight_far, sent, gate, mask, pair, weight, wide, mixed, arrived
+    row_size, mask_far, pair_far, weight_far, sent, gate, mask, pair, weight, mixed, arrived
 ):
     copies = [
         pltpu.make_async_copy(pair_far, pair, arrived.at[0]),
@@ -46,12 +46,13 @@
     rows, columns, channels = pair.shape
     patch = rows * columns
     here = channels // row_size
-    wide[...] = normed_rows(pair[...].astype(jnp.float32).reshape(patch, channels))
-    normed = jnp.concatenate(
-        [wide[pl.ds(k, rows, stride=columns), :] for k in range(columns)], axis=0
-    ).astype(jnp.bfloat16)
+    normed = normed_rows(pair[...].astype(jnp.float32).reshape(patch, channels))
+    normed = normed.astype(jnp.bfloat16)
     projected = lax.dot_general(
-        weight[...], normed, (((0,), (1,)), ((), ())), preferred_element_type=jnp.float32
+        weight[:, : 4 * channels],
+        normed,
+        (((0,), (1,)), ((), ())),
+        preferred_element_type=jnp.float32,
     )
     lane = lax.broadcasted_iota(jnp.int32, (1, patch), 1)
     first_row = lax.axis_index("row") * rows
@@ -59,9 +60,9 @@
     row_valid = jnp.zeros((1, patch), jnp.int32)
     column_valid = jnp.zeros((1, patch), jnp.int32)
     for i in range(rows):
-        row_valid = jnp.where(lane % rows == i, mask[first_row + i], row_valid)
+        row_valid = jnp.where(lane // columns == i, mask[first_row + i], row_valid)
     for k in range(columns):
-        column_valid = jnp.where(lane // rows == k, mask[first_column + k], column_valid)
+        column_valid = jnp.where(lane % columns == k, mask[first_column + k], column_valid)
     valid = (row_valid * column_valid).astype(jnp.float32)
     left = jax.nn.sigmoid(projected[:channels]) * projected[channels : 2 * channels] * valid
     right = (
@@ -69,16 +70,108 @@
         * projected[3 * channels : 4 * channels]
         * valid
     )
-    gate[...] = jax.nn.sigmoid(projected[4 * channels :])
     for r in range(row_size):
         mixed[2 * r * here : (2 * r + 1) * here, :] = left[r * here : (r + 1) * here]
         mixed[(2 * r + 1) * here : (2 * r + 2) * here, :] = right[r * here : (r + 1) * here]
     sent[...] = mixed[...].astype(jnp.bfloat16)
-
-
-def update_kernel(mask, all_valid, crossed, gate, pair, weight, bias, coupling, spread, wide):
-    rows, columns, channels = pair.shape
-    patch = rows * columns
+    gate[...] = jax.nn.sigmoid(
+        jnp.dot(normed, weight[:, 4 * channels :], preferred_element_type=jnp.float32)
+    )
+
+
+def tiled(rows, lanes):
+    return lanes // min(lanes, 128), rows, min(lanes, 128)
+
+
+def put_tiles(ref, value, rows=slice(None)):
+    for tile in range(ref.shape[0]):
+        ref[tile, rows, :] = value[:, tile * ref.shape[2] : (tile + 1) * ref.shape[2]]
+
+
+def get_tiles(ref, rows):
+    return jnp.concatenate([ref[tile, rows, :] for tile in range(ref.shape[0])], axis=1)
+
+
+def regroup(pieces, here):
+    lanes = pieces[0].shape[1]
+    step = lanes // here
+    group = lax.broadcasted_iota(jnp.int32, pieces[0].shape, 1) // step
+    results = []
+    for c in range(here):
+        tiles = []
+        for first in range(0, len(pieces), here):
+            tile = pieces[first + c]
+            for n in range(here):
+                if n != c:
+                    moved = pltpu.roll(pieces[first + n], (n - c) % here * step, axis=1)
+                    tile = jnp.where(group == n, moved, tile)
+            tiles.append(tile)
+        results.append(jnp.concatenate(tiles, axis=1))
+    return results
+
+
+def gathered_kernel(columns, got, rider, sent, wide, turned):
+    row_size, double, patch = got.shape
+    here = double // 2
+    rows = patch // columns
+    put_tiles(wide, got[...].astype(jnp.float32).reshape(row_size * double, patch))
+    sides = []
+    for side in range(2):
+        stacked = jnp.concatenate(
+            [get_tiles(wide, pl.ds(side * here + c, row_size, stride=double)) for c in range(here)],
+            axis=0,
+        )
+        turned[...] = stacked.T
+        pieces = [turned[t * columns : (t + 1) * columns, :] for t in range(rows)]
+        sides.append(
+            [[block.astype(jnp.bfloat16) for block in regroup(pieces[h : h + rows // 2], here)]
+             for h in (0, rows // 2)]
+        )
+    width = rows // 2 * row_size
+    for c in range(here):
+        for i in range(2):
+            for j in range(2):
+                place = (c * 2 + i) * 2 + j
+                sent[place, :columns, :width] = sides[0][i][c]
+                sent[place, :columns, width:] = sides[1][j][c]
+                sent[place, columns:, :] = rider[place % 2]
+
+
+def multiply_kernel(columns, row_size, got, crossed, wide):
+    blocks = got.shape[0]
+    width = got.shape[2] // 2
+    both = jnp.concatenate([got[q, :columns, :] for q in range(blocks)], axis=0)
+    product = lax.dot_general(
+        both[:, width:], both[:, :width], (((0,), (0,)), ((), ())), preferred_element_type=jnp.float32
+    )
+    put_tiles(wide, product)
+    half = width // row_size
+    for q in range(blocks):
+        crossed[q] = jnp.concatenate(
+            [get_tiles(wide, pl.ds(2 * q + m, half, stride=row_size)) for m in range(2)], axis=0
+        ).astype(jnp.bfloat16)
+
+
+def returned_kernel(here, row_size, got, sent, wide):
+    half = got.shape[1] // 2
+    pieces = []
+    for i in range(2):
+        stacked = []
+        for c in range(here):
+            for m in range(2):
+                for j in range(2):
+                    place = (c * 2 + i) * 2 + j
+                    stacked.append(got[place].astype(jnp.float32)[m * half : (m + 1) * half])
+        turned = jnp.concatenate(stacked, axis=0).T
+        pieces += [turned[t * row_size : (t + 1) * row_size] for t in range(half)]
+    for c, block in enumerate(regroup(pieces, here)):
+        put_tiles(wide, block, pl.ds(c, row_size, stride=here))
+    sent[...] = get_tiles(wide, slice(None)).astype(jnp.bfloat16)
+
+
+def update_kernel(columns, mask, all_valid, crossed, gate, pair, weight, bias, coupling, spread):
+    patch, channels = pair.shape
+    rows = patch // columns
     lanes = bias.shape[1]
     heads = lanes // rows
     cross = crossed[...].astype(jnp.float32)
@@ -87,18 +180,18 @@
     variance = jnp.mean(centred * centred, axis=0, keepdims=True)
     cross = (centred * lax.rsqrt(variance + epsilon)).astype(jnp.bfloat16)
     update = lax.dot_general(
-        weight[...], cross, (((0,), (0,)), ((), ())), preferred_element_type=jnp.float32
-    )
-    wide[...] = (gate[...] * update).T
+        cross, weight[...], (((0,), (0,)), ((), ())), preferred_element_type=jnp.float32
+    )
+    after = (pair[...].astype(jnp.float32) + gate[...] * update).astype(jnp.bfloat16)
+    coupling[...] = after
+    normed = normed_rows(after.astype(jnp.float32)).astype(jnp.bfloat16)
     lane = lax.broadcasted_iota(jnp.int32, (channels, lanes), 1)
     scores = jnp.zeros((columns, lanes), jnp.float32)
     for i in range(rows):
-        line = pair[i].astype(jnp.float32) + wide[pl.ds(i, columns, stride=rows), :]
-        line = line.astype(jnp.bfloat16)
-        coupling[i] = line
-        normed = normed_rows(line.astype(jnp.float32)).astype(jnp.bfloat16)
         own = jnp.where(lane // heads == i, bias[...], jnp.zeros((), jnp.bfloat16))
-        scores = scores + jnp.dot(normed, own, preferred_element_type=jnp.float32)
+        scores = scores + jnp.dot(
+            normed[i * columns : (i + 1) * columns], own, preferred_element_type=jnp.float32
+        )
     place = lax.broadcasted_iota(jnp.int32, (columns, lanes), 0)
     first_column = lax.axis_index("col") * columns
     valid = jnp.zeros((columns, lanes), jnp.int32)
@@ -188,9 +281,7 @@
     tokens = row_size * rows_here
     patch = rows_here * columns_here
     channels_here = channels // row_size
-    left_parts = col_size // channels_here // fanout
-    left_width = tokens // left_parts
-    right_width = tokens // fanout
+    width = tokens // 2
     places = score_places(row_size, col_size)
     moves = []
     for row in range(row_size):
@@ -200,11 +291,16 @@
 
     vmem = pl.BlockSpec(memory_space=pltpu.VMEM)
     smem = pl.BlockSpec(memory_space=pltpu.SMEM)
+    spacious = pltpu.CompilerParams(vmem_limit_bytes=32 * 1024 * 1024)
+
+    def work(flops):
+        return pl.CostEstimate(flops=flops, bytes_accessed=2**20, transcendentals=0)
+
     sent, out_gate = pl.pallas_call(
         functools.partial(project_kernel, row_size),
         out_shape=(
             jax.ShapeDtypeStruct((2 * channels, patch), jnp.bfloat16),
-            jax.ShapeDtypeStruct((channels, patch), jnp.float32),
+            jax.ShapeDtypeStruct((patch, channels), jnp.float32),
         ),
         in_specs=[pl.BlockSpec(memory_space=pltpu.HBM)] * 3,
         out_specs=(vmem, vmem),
@@ -212,74 +308,76 @@
             pltpu.SMEM(token_valid_mask.shape, jnp.int32),
             pltpu.VMEM(pair_state.shape, jnp.bfloat16),
             pltpu.VMEM(triangle_input_weight.shape, jnp.bfloat16),
-            pltpu.VMEM((patch, channels), jnp.float32),
             pltpu.VMEM((2 * channels, patch), jnp.float32),
             pltpu.SemaphoreType.DMA((3,)),
         ],
         compiler_params=pltpu.CompilerParams(vmem_limit_bytes=63 * 1024 * 1024),
-        cost_estimate=pl.CostEstimate(
-            flops=10 * patch * channels * channels, bytes_accessed=2**20, transcendentals=0
+        cost_estimate=work(10 * patch * channels * channels),
+    )(token_valid_mask, pair_state, triangle_input_weight)
+
+    got = exchange(sent.reshape(row_size, 2 * channels_here, patch), "row")
+    rider = sequence_embedding.reshape(2, -1, 2 * width)
+    sent = pl.pallas_call(
+        functools.partial(gathered_kernel, columns_here),
+        out_shape=jax.ShapeDtypeStruct(
+            (col_size, columns_here + rider.shape[1], 2 * width), jnp.bfloat16
         ),
-    )(token_valid_mask, pair_state, triangle_input_weight)
-
-    got = exchange(sent.reshape(row_size, 2 * channels_here, patch), "row")
-    got = got.reshape(row_size, 2, channels_here, columns_here, rows_here)
-    got = jnp.transpose(got, (1, 2, 3, 0, 4))
-    left = jnp.transpose(
-        got[0].reshape(channels_here, columns_here, left_parts, left_width), (0, 2, 1, 3)
-    ).reshape(channels_here, left_parts, 1, columns_here, left_width)
-    right = jnp.transpose(
-        got[1].reshape(channels_here, columns_here, col_size, fanout, rows_here), (0, 3, 1, 2, 4)
-    ).reshape(channels_here, 1, fanout, columns_here, right_width)
-    lead = (channels_here, left_parts, fanout, columns_here)
-    sent = jnp.concatenate(
-        [jnp.broadcast_to(left, lead + (left_width,)), jnp.broadcast_to(right, lead + (right_width,))],
-        axis=4,
-    ).reshape(col_size, columns_here, left_width + right_width)
-    rider = jnp.tile(
-        sequence_embedding.reshape(2, -1, left_width + right_width), (col_size // 2, 1, 1)
-    )
-    got = exchange(jnp.concatenate([sent, rider], axis=1), "col")
+        in_specs=[vmem, vmem],
+        out_specs=vmem,
+        scratch_shapes=[
+            pltpu.VMEM(tiled(2 * channels, patch), jnp.float32),
+            pltpu.VMEM((patch, channels), jnp.float32),
+        ],
+        compiler_params=spacious,
+        cost_estimate=work(patch * channels),
+    )(got, rider)
+    got = exchange(sent, "col")
     half = got[:, columns_here:]
     half_other = lax.ppermute(half, "col", [(a, a ^ 1) for a in range(col_size)])
     first = col_index % 2 == 0
     sequence_all = jnp.concatenate(
         [jnp.where(first, half, half_other), jnp.where(first, half_other, half)], axis=1
     ).reshape(col_size, msa_rows, columns_here, features)
-    got = got[:, :columns_here].reshape(tokens, left_width + right_width)
-    crossed = jnp.einsum(
-        "kj,ki->ji",
-        got[:, left_width:],
-        got[:, :left_width],
-        preferred_element_type=jnp.float32,
-    ).astype(jnp.bfloat16)
-    got = exchange(crossed.reshape(col_size, rows_here, left_width), "col").reshape(
-        channels_here, left_parts, fanout, rows_here, row_size // left_parts, rows_here
-    )
-    sent = jnp.transpose(got, (1, 4, 0, 2, 3, 5)).reshape(row_size, channels_here, patch)
-    crossed = exchange(sent, "row").reshape(channels, patch)
+    sent = pl.pallas_call(
+        functools.partial(multiply_kernel, columns_here, row_size),
+        out_shape=jax.ShapeDtypeStruct((col_size, rows_here, width), jnp.bfloat16),
+        in_specs=[vmem],
+        out_specs=vmem,
+        scratch_shapes=[pltpu.VMEM(tiled(width, width), jnp.float32)],
+        compiler_params=spacious,
+        cost_estimate=work(2 * tokens * width * width),
+    )(got)
+    got = exchange(sent, "col")
+    sent = pl.pallas_call(
+        functools.partial(returned_kernel, channels_here, row_size),
+        out_shape=jax.ShapeDtypeStruct((channels, patch), jnp.bfloat16),
+        in_specs=[vmem],
+        out_specs=vmem,
+        scratch_shapes=[pltpu.VMEM(tiled(channels, patch), jnp.float32)],
+        compiler_params=spacious,
+        cost_estimate=work(patch * channels),
+    )(got)
+    crossed = exchange(sent.reshape(row_size, channels_here, patch), "row").reshape(channels, patch)
     coupling_refreshed, sent = pl.pallas_call(
-        update_kernel,
+        functools.partial(update_kernel, columns_here),
         out_shape=(
-            jax.ShapeDtypeStruct(pair_state.shape, jnp.bfloat16),
+            jax.ShapeDtypeStruct((patch, channels), jnp.bfloat16),
             jax.ShapeDtypeStruct((columns_here + 8, rows_here * heads), jnp.float32),
         ),
         in_specs=[smem] + [vmem] * 6,
         out_specs=(vmem, vmem),
-        scratch_shapes=[pltpu.VMEM((patch, channels), jnp.float32)],
-        compiler_params=pltpu.CompilerParams(vmem_limit_bytes=32 * 1024 * 1024),
-        cost_estimate=pl.CostEstimate(
-            flops=4 * patch * channels * channels, bytes_accessed=2**20, transcendentals=0
-        ),
+        compiler_params=spacious,
+        cost_estimate=work(4 * patch * channels * channels),
     )(
         token_valid_mask,
         token_valid_mask.reshape(4, -1),
         crossed,
         out_gate,
-        pair_state,
+        pair_state.reshape(patch, channels),
         triangle_output_weight,
         jnp.tile(pair_head_bias, (1, rows_here)),
     )
+    coupling_refreshed = coupling_refreshed.reshape(rows_here, columns_here, channels)
     sent = sent.astype(jnp.bfloat16)
 
     sent = lax.ppermute(sent, ("row", "col"), moves)
@@ -292,9 +390,6 @@
         axis_index_groups=groups,
         tiled=True,
     )
-    swap = [(a, (a + col_size) % row_size) for a in range(row_size)]
-    other = lax.ppermute(mine, "row", swap)
-
     sequence_all = apply_layer_norm(sequence_all.astype(jnp.float32), 3).astype(jnp.bfloat16)
     values = jnp.einsum(
         "qsjf,fg->qjsg",
@@ -302,6 +397,10 @@
         sequence_entry_matrix[:, :value_width],
         preferred_element_type=jnp.float32,
     ).astype(jnp.bfloat16).reshape(tokens, msa_rows * value_width)
+    mine, values = lax.optimization_barrier((mine, values))
+    swap = [(a, (a + col_size) % row_size) for a in range(row_size)]
+    other = lax.ppermute(mine, "row", swap)
+
     places = lax.dynamic_index_in_dim(jnp.asarray(places), col_index, 0, keepdims=False)
     half_index = row_index // col_size
 

time: 149 us -> 144 us (0.966)
  local copies, waits for them, and re-layouts: 12 us -> 7.86 us
  other arithmetic: 7.13 us -> 3.55 us
  Pallas kernels: 6.57 us -> 9.16 us
    all_to_all x1, waiting for transfers between devices: 12.7 us -> 9.09 us  [shards(): lax.all_to_all(jnp.broadcast_to(sent[None], (col_size,) + sent.shape), 'r...]
    pallas_call x1 -> x4, Pallas kernels: 1.61 us -> 4.27 us  [the longest x1 1.6 us: shards(): pl.pallas_call(functools.partial(update_kernel, columns_here), out_shape=...]
    ppermute x1, waiting for transfers between devices: 0.01 us -> 2.06 us  [shards(): other = lax.ppermute(mine, 'row', swap)]
    all_to_all x4, waiting for transfers between devices: 51.6 us -> 53.4 us  [exchange(): return lax.all_to_all(blocks, axis, split_axis=0, concat_axis=0, tiled=True)]
    slice x4 -> x0, local copies, waits for them, and re-layouts: 1.62 us -> none  [the longest x2 0.89 us: shards(): got[0].reshape(channels_here, columns_here, left_parts, left_width)]
  transfers between devices with their start and end apart: 8 -> 8, of which waited for: 6 -> 7; matrix products, arithmetic and copies ran while one was open for 10% -> 8% of each run, Pallas kernels for 1% -> 1%
where the time goes in v6:
time: 144 us; the launch traced here: 143 us
  waiting for transfers between devices  72.1 us (50%)
  starting transfers between devices  47.3 us (33%)
  Pallas kernels  9.16 us (6%)
  local copies, waits for them, and re-layouts  7.86 us (5%)
  other arithmetic  3.55 us (2%)
  matrix products  1.83 us (1%)
    all_to_all x4, waiting for transfers between devices, exchange(): return lax.all_to_all(blocks, axis, split_axis=0, concat_axis=0, tiled=True)  53.4 us
    all_to_all x4, starting transfers between devices, exchange(): return lax.all_to_all(blocks, axis, split_axis=0, concat_axis=0, tiled=True)  31.5 us
    all_to_all x1, waiting for transfers between devices, shards(): lax.all_to_all(jnp.broadcast_to(sent[None], (col_size,) + sent.shape), 'r...  9.09 us
    all_to_all x1, starting transfers between devices, shards(): lax.all_to_all(jnp.broadcast_to(sent[None], (col_size,) + sent.shape), 'r...  7.99 us
    ppermute x1, waiting for transfers between devices, shards(): sent = lax.ppermute(sent, ('row', 'col'), moves)  7.58 us
    ppermute x1, starting transfers between devices, shards(): other = lax.ppermute(mine, 'row', swap)  2.93 us
  transfers between devices with their start and end apart: 8, of which 7 were waited for; matrix products, arithmetic and copies ran while one was open for 8% of the time, Pallas kernels for 1%

profile of v6, /device:TPU:32, one launch (start us, length us, event | category | flops | bytes accessed | tf_op | source)
XLA Modules:
  0.0 142.9 jit_solution(3874304129368928963)
XLA Ops:
  0.7 2.4 %shard_map.113 = (bf16[256,512]{1,0:T(8,128)(2,1)}, f32[512,128]{1,0:T(8,128)}) custom-call(s32[512]{0:T(512)} %mask.1, bf16[16,32,128]{2,1,0:T(8,128)(2,1)} %pair_far.1, bf16[128,640]{1,0:T(8,128)(2,1)} %weight_far.1), custom_call_target="tpu_custom_call" | custom-call | flops 83886080 | bytes 1048576 | tf_op jit(solution)/shard_map/pallas_call | solution.py:299
  3.1 16.3 %all-to-all-start = ((bf16[32,8,512]{2,1,0:T(8,128)(2,1)}), bf16[32,8,512]{2,1,0:T(8,128)(2,1)S(1)}, u32[]{:S(2)}, u32[]{:S(2)}) async-start(bf16[32,8,512]{2,1,0:T(8,128)(2,1)} %bitcast.60), calls=%async_computation | async-start | bytes 524288 | tf_op jit(solution)/shard_map/all_to_all | solution.py:24
  20.2 20.3 %all-to-all-done.got = bf16[32,8,512]{2,1,0:T(8,128)(2,1)S(1)} async-done(((bf16[32,8,512]{2,1,0:T(8,128)(2,1)}), bf16[32,8,512]{2,1,0:T(8,128)(2,1)S(1)}, u32[]{:S(2)}, u32[]{:S(2)}) %all-to-all-start) | async-done | bytes 262176 | tf_op jit(solution)/shard_map/all_to_all | solution.py:24
  40.4 1.3 shard_map.114
  41.8 6.7 %all-to-all-start.1 = ((bf16[16,48,512]{2,1,0:T(8,128)(2,1)}), bf16[16,48,512]{2,1,0:T(8,128)(2,1)S(1)}, u32[]{:S(2)}, u32[]{:S(2)}) async-start(bf16[16,48,512]{2,1,0:T(8,128)(2,1)} %shard_map.114), calls=%async_computation.1 | async-start | bytes 1572864 | tf_op jit(solution)/shard_map/all_to_all | solution.py:24
  48.8 14.9 %all-to-all-done.1.got = bf16[16,48,512]{2,1,0:T(8,128)(2,1)S(1)} async-done(((bf16[16,48,512]{2,1,0:T(8,128)(2,1)}), bf16[16,48,512]{2,1,0:T(8,128)(2,1)S(1)}, u32[]{:S(2)}, u32[]{:S(2)}) %all-to-all-start.1) | async-done | bytes 786464 | tf_op jit(solution)/shard_map/all_to_all | solution.py:24
  64.8 3.5 %all-to-all-start.2 = ((bf16[16,16,256]{2,1,0:T(8,128)(2,1)}), bf16[16,16,256]{2,1,0:T(8,128)(2,1)S(1)}, u32[]{:S(2)}, u32[]{:S(2)}) async-start(bf16[16,16,256]{2,1,0:T(8,128)(2,1)} %shard_map.115), calls=%async_computation.2 | async-start | bytes 262144 | tf_op jit(solution)/shard_map/all_to_all | solution.py:24
  68.3 2.2 %collective-permute-start.1 = (bf16[16,16,512]{2,1,0:T(8,128)(2,1)S(1)}, bf16[16,16,512]{2,1,0:T(8,128)(2,1)S(1)}, u32[]{:S(2)}, u32[]{:S(2)}) collective-permute-start(bf16[16,16,512]{2,1,0:T(8,128)(2,1)S(1)} %slice.12), channel_id=1, source_target_pairs={{0,1},{1,0},{2,3},{3,2},{4,5},{5,4},{6,7},{7,6},{8,9},{9,8},{10,11... | collective-permute-start | bytes 786440 | tf_op jit(solution)/shard_map/ppermute | solution.py:336
  70.9 5.6 %all-to-all-done.2.got = bf16[16,16,256]{2,1,0:T(8,128)(2,1)S(1)} async-done(((bf16[16,16,256]{2,1,0:T(8,128)(2,1)}), bf16[16,16,256]{2,1,0:T(8,128)(2,1)S(1)}, u32[]{:S(2)}, u32[]{:S(2)}) %all-to-all-start.2) | async-done | bytes 131104 | tf_op jit(solution)/shard_map/all_to_all | solution.py:24
  77.4 4.9 %all-to-all-start.3 = ((bf16[32,4,512]{2,1,0:T(4,128)(2,1)}), bf16[32,4,512]{2,1,0:T(4,128)(2,1)S(1)}, u32[]{:S(2)}, u32[]{:S(2)}) async-start(bf16[32,4,512]{2,1,0:T(4,128)(2,1)} %reshape.80), calls=%async_computation.3 | async-start | bytes 262144 | tf_op jit(solution)/shard_map/all_to_all | solution.py:24
  83.6 1.6 %reshape.87 = f32[16,8,32,64]{3,2,1,0:T(8,128)S(1)} reshape(f32[16,32,512]{2,1,0:T(8,128)} %maximum_convert_fusion) | data formatting | bytes 2097152 | tf_op jit(solution)/shard_map/convert_element_type | solution.py:393
  85.8 12.6 %all-to-all-done.3 = bf16[32,4,512]{2,1,0:T(4,128)(2,1)S(1)} async-done(((bf16[32,4,512]{2,1,0:T(4,128)(2,1)}), bf16[32,4,512]{2,1,0:T(4,128)(2,1)S(1)}, u32[]{:S(2)}, u32[]{:S(2)}) %all-to-all-start.3) | async-done | bytes 131104 | tf_op jit(solution)/shard_map/all_to_all | solution.py:24
  98.5 1.6 %shard_map.117 = (bf16[512,128]{1,0:T(8,128)(2,1)}, f32[40,128]{1,0:T(8,128)S(1)}) custom-call(s32[512]{0:T(512)S(1)} %copy-done.4, s32[4,128]{1,0:T(4,128)S(1)} %bitcast.56, bf16[128,512]{1,0:T(8,128)(2,1)S(1)} %reshape.81.crossed, f32[512,128]{1,0:T(8,128)S(1)} %copy-done.1, bf16[512,128]{1,0:T(8,128)(2,1)S(1)} %bitcast.55, ...), custom_call_target="tpu_custom_call" | custom-call | flops 33554432 | bytes 1048576 | tf_op jit(solution)/shard_map/pallas_call | solution.py:361
  100.1 2.8 %collective-permute-start = (bf16[40,128]{1,0:T(8,128)(2,1)S(1)}, bf16[40,128]{1,0:T(8,128)(2,1)S(1)}, u32[]{:S(2)}, u32[]{:S(2)}) collective-permute-start(bf16[40,128]{1,0:T(8,128)(2,1)S(1)} %convert_element_type.40), channel_id=1, source_target_pairs={{0,128},{1,96},{2,144},{3,64},{4,176},{5,32},{6,112},{7,80},{8,160... | collective-permute-start | bytes 30728 | tf_op jit(solution)/shard_map/ppermute | solution.py:383
  102.9 7.6 %collective-permute-done = bf16[40,128]{1,0:T(8,128)(2,1)S(1)} collective-permute-done((bf16[40,128]{1,0:T(8,128)(2,1)S(1)}, bf16[40,128]{1,0:T(8,128)(2,1)S(1)}, u32[]{:S(2)}, u32[]{:S(2)}) %collective-permute-start) | collective-permute-done | bytes 10272 | tf_op jit(solution)/shard_map/ppermute | solution.py:383
  111.2 8.0 %all-to-all-start.4 = ((bf16[16,40,128]{2,1,0:T(8,128)(2,1)}), bf16[16,40,128]{2,1,0:T(8,128)(2,1)S(1)}, u32[]{:S(2)}, u32[]{:S(2)}) async-start(bf16[16,40,128]{2,1,0:T(8,128)(2,1)} %broadcast_in_dim.2), calls=%async_computation.4 | async-start | bytes 327680 | tf_op jit(solution)/shard_map/all_to_all | solution.py:385
  119.2 1.3 multiply_reduce_fusion
  120.5 1.5 %convert_bitcast_fusion = bf16[16,32,8,256]{3,1,2,0:T(8,128)(2,1)S(1)} fusion(f32[16,8,32,64]{3,2,1,0:T(8,128)S(1)} %reshape.87, f32[16,8,32]{2,1,0:T(8,128)S(1)} %add_rsqrt_fusion, f32[16,8,32]{2,1,0:T(8,128)S(1)} %broadcast_multiply_fusion, bf16[64,512]{1,0:T(8,128)(2,1)S(1)} %copy-done.6), kind=kOutput, calls=%fused_computation | convolution fusion | flops 136052736 | bytes 4358144 | tf_op jit(solution)/shard_map/qsjf,fg->qjsg/dot_general | solution.py:394
  122.0 1.4 %copy.15 = bf16[16,32,8,256]{3,2,1,0:T(8,128)(2,1)S(1)} copy(bf16[16,32,8,256]{3,1,2,0:T(8,128)(2,1)S(1)} %convert_bitcast_fusion) | data formatting | bytes 4194304 | tf_op jit(solution)/shard_map/convert_element_type | solution.py:399
  124.2 9.1 %all-to-all-done.4.got = bf16[16,40,128]{2,1,0:T(8,128)(2,1)S(1)} async-done(((bf16[16,40,128]{2,1,0:T(8,128)(2,1)}), bf16[16,40,128]{2,1,0:T(8,128)(2,1)S(1)}, u32[]{:S(2)}, u32[]{:S(2)}) %all-to-all-start.4) | async-done | bytes 163872 | tf_op jit(solution)/shard_map/all_to_all | solution.py:385
  133.2 2.9 %collective-permute-start.2 = (bf16[16,40,128]{2,1,0:T(8,128)(2,1)S(1)}, bf16[16,40,128]{2,1,0:T(8,128)(2,1)S(1)}, u32[]{:S(2)}, u32[]{:S(2)}) collective-permute-start(bf16[16,40,128]{2,1,0:T(8,128)(2,1)S(1)} %all-to-all-done.4.got), channel_id=1, source_target_pairs={{0,256},{16,272},{32,288},{48,304},{64,320},{80,336},{96,352},{112... | collective-permute-start | bytes 491528 | tf_op jit(solution)/shard_map/ppermute | solution.py:402
  137.1 1.2 shard_map.118
  138.4 2.1 %collective-permute-done.2.got = bf16[16,40,128]{2,1,0:T(8,128)(2,1)S(1)} collective-permute-done((bf16[16,40,128]{2,1,0:T(8,128)(2,1)S(1)}, bf16[16,40,128]{2,1,0:T(8,128)(2,1)S(1)}, u32[]{:S(2)}, u32[]{:S(2)}) %collective-permute-start.2) | collective-permute-done | bytes 163872 | tf_op jit(solution)/shard_map/ppermute | solution.py:402
  140.4 1.2 shard_map.119
  (49 shorter events, 8.7 us)
Async XLA Ops:
  0.6 141.2 %copy-start = (bf16[256,64]{0,1:T(8,128)(2,1)S(1)}, bf16[256,64]{0,1:T(8,128)(2,1)}, u32[]{:S(2)}) copy-start(bf16[256,64]{0,1:T(8,128)(2,1)} %param.18) | copy-start | bytes 98308
  0.6 47.9 %copy-start.5 = (bf16[8,2048]{1,0:T(8,128)(2,1)S(1)}, bf16[8,2048]{1,0:T(8,128)(2,1)}, u32[]{:S(2)}) copy-start(bf16[8,2048]{1,0:T(8,128)(2,1)} %param.11) | copy-start | bytes 98308
  0.7 48.1 %copy-start.7 = (bf16[128,8]{0,1:T(8,128)(2,1)S(1)}, bf16[128,8]{0,1:T(8,128)(2,1)}, u32[]{:S(2)}) copy-start(bf16[128,8]{0,1:T(8,128)(2,1)} %param.16) | copy-start | bytes 6148
  3.1 37.3 %all-to-all-start = ((bf16[32,8,512]{2,1,0:T(8,128)(2,1)}), bf16[32,8,512]{2,1,0:T(8,128)(2,1)S(1)}, u32[]{:S(2)}, u32[]{:S(2)}) async-start(bf16[32,8,512]{2,1,0:T(8,128)(2,1)} %bitcast.60), calls=%async_computation | async-start | bytes 524288 | tf_op jit(solution)/shard_map/all_to_all | solution.py:24
  41.8 21.9 %all-to-all-start.1 = ((bf16[16,48,512]{2,1,0:T(8,128)(2,1)}), bf16[16,48,512]{2,1,0:T(8,128)(2,1)S(1)}, u32[]{:S(2)}, u32[]{:S(2)}) async-start(bf16[16,48,512]{2,1,0:T(8,128)(2,1)} %shard_map.114), calls=%async_computation.1 | async-start | bytes 1572864 | tf_op jit(solution)/shard_map/all_to_all | solution.py:24
  64.8 11.7 %all-to-all-start.2 = ((bf16[16,16,256]{2,1,0:T(8,128)(2,1)}), bf16[16,16,256]{2,1,0:T(8,128)(2,1)S(1)}, u32[]{:S(2)}, u32[]{:S(2)}) async-start(bf16[16,16,256]{2,1,0:T(8,128)(2,1)} %shard_map.115), calls=%async_computation.2 | async-start | bytes 262144 | tf_op jit(solution)/shard_map/all_to_all | solution.py:24
  68.3 14.1 %collective-permute-start.1 = (bf16[16,16,512]{2,1,0:T(8,128)(2,1)S(1)}, bf16[16,16,512]{2,1,0:T(8,128)(2,1)S(1)}, u32[]{:S(2)}, u32[]{:S(2)}) collective-permute-start(bf16[16,16,512]{2,1,0:T(8,128)(2,1)S(1)} %slice.12), channel_id=1, source_target_pairs={{0,1},{1,0},{2,3},{3,2},{4,5},{5,4},{6,7},{7,6},{8,9},{9,8},{10,11... | collective-permute-start | bytes 786440 | tf_op jit(solution)/shard_map/ppermute | solution.py:336
  77.4 21.0 %all-to-all-start.3 = ((bf16[32,4,512]{2,1,0:T(4,128)(2,1)}), bf16[32,4,512]{2,1,0:T(4,128)(2,1)S(1)}, u32[]{:S(2)}, u32[]{:S(2)}) async-start(bf16[32,4,512]{2,1,0:T(4,128)(2,1)} %reshape.80), calls=%async_computation.3 | async-start | bytes 262144 | tf_op jit(solution)/shard_map/all_to_all | solution.py:24
  83.6 14.9 %copy-start.1 = (f32[512,128]{1,0:T(8,128)S(1)}, f32[512,128]{1,0:T(8,128)}, u32[]{:S(2)}) copy-start(f32[512,128]{1,0:T(8,128)} %get-tuple-element.9.gate) | copy-start | bytes 786436
  83.6 14.9 %copy-start.2 = (bf16[16,32,128]{2,1,0:T(8,128)(2,1)S(1)}, bf16[16,32,128]{2,1,0:T(8,128)(2,1)}, u32[]{:S(2)}) copy-start(bf16[16,32,128]{2,1,0:T(8,128)(2,1)} %pair_far.1) | copy-start | bytes 393220
  83.6 14.9 %copy-start.3 = (bf16[128,128]{1,0:T(8,128)(2,1)S(1)}, bf16[128,128]{1,0:T(8,128)(2,1)}, u32[]{:S(2)}) copy-start(bf16[128,128]{1,0:T(8,128)(2,1)} %weight.1) | copy-start | bytes 98308
  83.6 14.9 %copy-start.4 = (s32[512]{0:T(512)S(1)}, s32[512]{0:T(512)}, u32[]{:S(2)}) copy-start(s32[512]{0:T(512)} %mask.1) | copy-start | bytes 6148
  85.8 34.7 %copy-start.6 = (bf16[64,512]{1,0:T(8,128)(2,1)S(1)}, bf16[64,512]{1,0:T(8,128)(2,1)}, u32[]{:S(2)}) copy-start(bf16[64,512]{1,0:T(8,128)(2,1)} %param.17) | copy-start | bytes 196612
  100.1 10.4 %collective-permute-start = (bf16[40,128]{1,0:T(8,128)(2,1)S(1)}, bf16[40,128]{1,0:T(8,128)(2,1)S(1)}, u32[]{:S(2)}, u32[]{:S(2)}) collective-permute-start(bf16[40,128]{1,0:T(8,128)(2,1)S(1)} %convert_element_type.40), channel_id=1, source_target_pairs={{0,128},{1,96},{2,144},{3,64},{4,176},{5,32},{6,112},{7,80},{8,160... | collective-permute-start | bytes 30728 | tf_op jit(solution)/shard_map/ppermute | solution.py:383
  111.2 22.1 %all-to-all-start.4 = ((bf16[16,40,128]{2,1,0:T(8,128)(2,1)}), bf16[16,40,128]{2,1,0:T(8,128)(2,1)S(1)}, u32[]{:S(2)}, u32[]{:S(2)}) async-start(bf16[16,40,128]{2,1,0:T(8,128)(2,1)} %broadcast_in_dim.2), calls=%async_computation.4 | async-start | bytes 327680 | tf_op jit(solution)/shard_map/all_to_all | solution.py:385
  123.5 12.9 %copy-start.8 = (s32[8]{0:T(128)S(1)}, s32[8]{0:T(128)}, u32[]{:S(2)}) copy-start(s32[8]{0:T(128)} %param.13) | copy-start | bytes 100
  133.2 7.2 %collective-permute-start.2 = (bf16[16,40,128]{2,1,0:T(8,128)(2,1)S(1)}, bf16[16,40,128]{2,1,0:T(8,128)(2,1)S(1)}, u32[]{:S(2)}, u32[]{:S(2)}) collective-permute-start(bf16[16,40,128]{2,1,0:T(8,128)(2,1)S(1)} %all-to-all-done.4.got), channel_id=1, source_target_pairs={{0,256},{16,272},{32,288},{48,304},{64,320},{80,336},{96,352},{112... | collective-permute-start | bytes 491528 | tf_op jit(solution)/shard_map/ppermute | solution.py:402

commit v7 on v6

--- a/solution.py
+++ b/solution.py
@@ -164,17 +164,28 @@
                     stacked.append(got[place].astype(jnp.float32)[m * half : (m + 1) * half])
         turned = jnp.concatenate(stacked, axis=0).T
         pieces += [turned[t * row_size : (t + 1) * row_size] for t in range(half)]
+    lanes = wide.shape[1]
+    deep = wide.shape[0] // row_size
     for c, block in enumerate(regroup(pieces, here)):
-        put_tiles(wide, block, pl.ds(c, row_size, stride=here))
-    sent[...] = get_tiles(wide, slice(None)).astype(jnp.bfloat16)
-
-
-def update_kernel(columns, mask, all_valid, crossed, gate, pair, weight, bias, coupling, spread):
+        for tile in range(deep // here):
+            wide[pl.ds(c * (deep // here) + tile, row_size, stride=deep), :] = block[
+                :, tile * lanes : (tile + 1) * lanes
+            ]
+    sent[...] = wide[...].astype(jnp.bfloat16)
+
+
+def update_kernel(
+    columns, mask, all_valid, crossed, gate, pair, weight, bias, coupling, spread, wide
+):
     patch, channels = pair.shape
     rows = patch // columns
     lanes = bias.shape[1]
     heads = lanes // rows
-    cross = crossed[...].astype(jnp.float32)
+    wide[...] = crossed[...].astype(jnp.float32)
+    tiles = crossed.shape[0] // channels
+    cross = jnp.concatenate(
+        [wide[pl.ds(tile, channels, stride=tiles), :] for tile in range(tiles)], axis=1
+    )
     average = jnp.mean(cross, axis=0, keepdims=True)
     centred = cross - average
     variance = jnp.mean(centred * centred, axis=0, keepdims=True)
@@ -206,7 +217,7 @@
     spread[columns:, :] = jnp.broadcast_to(top, (spread.shape[0] - columns, lanes))
 
 
-def average_kernel(value_width, places, got, values, averaged, wide, ordered):
+def average(value_width, places, got, values, averaged, wide, ordered):
     blocks, deep, lanes = got.shape
     columns = deep - 8
     rows, across = averaged.shape
@@ -233,6 +244,39 @@
         )
         product = jnp.where(own, product, 0.0).reshape(rows, heads, value_width)
         averaged[:, start : start + value_width] = jnp.sum(product, axis=1)
+
+
+def finish_kernel(
+    value_width, features, places, flags, got, values, mine, gates, exits, tile, refreshed,
+    other, wide, ordered, gated, lines,
+):
+    average(value_width, places, got, values, other, wide, ordered)
+    half, across = mine.shape
+    msa_rows = across // value_width
+    low = lax.axis_index("row") < lax.axis_size("col")
+    put_tiles(gated, gates[:half, :] * jnp.where(low, mine[...], other[...]), pl.ds(0, half))
+    put_tiles(gated, gates[half:, :] * jnp.where(low, other[...], mine[...]), pl.ds(half, half))
+    parts = gated.shape[0] // msa_rows
+    for s in range(msa_rows):
+        line = 0.0
+        for parity in range(2):
+            rows = jnp.concatenate(
+                [gated[s * parts + part, pl.ds(parity, half, stride=2), :] for part in range(parts)],
+                axis=1,
+            ).astype(jnp.bfloat16)
+            line = line + jnp.dot(rows, exits[parity], preferred_element_type=jnp.float32)
+        lines[pl.ds(s, half, stride=msa_rows), :] = line
+    place = lax.broadcasted_iota(jnp.int32, (msa_rows, 2 * features), 0)
+    present = jnp.zeros((msa_rows, 2 * features), jnp.int32)
+    for s in range(msa_rows):
+        present = jnp.where(place == s, flags[s], present)
+    present = present.astype(jnp.float32)
+    for pair in range(half):
+        lane = slice(pair * 2 * features, (pair + 1) * 2 * features)
+        refreshed[:, lane] = (
+            tile[:, lane].astype(jnp.float32)
+            + present * lines[pair * msa_rows : (pair + 1) * msa_rows, :]
+        ).astype(jnp.bfloat16)
 
 
 def ring(a, b, size):
@@ -282,6 +326,7 @@
     patch = rows_here * columns_here
     channels_here = channels // row_size
     width = tokens // 2
+    lanes = min(patch, 128)
     places = score_places(row_size, col_size)
     moves = []
     for row in range(row_size):
@@ -350,14 +395,14 @@
     got = exchange(sent, "col")
     sent = pl.pallas_call(
         functools.partial(returned_kernel, channels_here, row_size),
-        out_shape=jax.ShapeDtypeStruct((channels, patch), jnp.bfloat16),
+        out_shape=jax.ShapeDtypeStruct((channels * patch // lanes, lanes), jnp.bfloat16),
         in_specs=[vmem],
         out_specs=vmem,
-        scratch_shapes=[pltpu.VMEM(tiled(channels, patch), jnp.float32)],
+        scratch_shapes=[pltpu.VMEM((channels * patch // lanes, lanes), jnp.float32)],
         compiler_params=spacious,
         cost_estimate=work(patch * channels),
     )(got)
-    crossed = exchange(sent.reshape(row_size, channels_here, patch), "row").reshape(channels, patch)
+    crossed = exchange(sent.reshape(row_size, -1, lanes), "row").reshape(-1, lanes)
     coupling_refreshed, sent = pl.pallas_call(
         functools.partial(update_kernel, columns_here),
         out_shape=(
@@ -366,6 +411,7 @@
         ),
         in_specs=[smem] + [vmem] * 6,
         out_specs=(vmem, vmem),
+        scratch_shapes=[pltpu.VMEM((channels * patch // lanes, lanes), jnp.float32)],
         compiler_params=spacious,
         cost_estimate=work(4 * patch * channels * channels),
     )(
@@ -397,39 +443,7 @@
         sequence_entry_matrix[:, :value_width],
         preferred_element_type=jnp.float32,
     ).astype(jnp.bfloat16).reshape(tokens, msa_rows * value_width)
-    mine, values = lax.optimization_barrier((mine, values))
-    swap = [(a, (a + col_size) % row_size) for a in range(row_size)]
-    other = lax.ppermute(mine, "row", swap)
-
     places = lax.dynamic_index_in_dim(jnp.asarray(places), col_index, 0, keepdims=False)
-    half_index = row_index // col_size
-
-    def average(got, which):
-        return pl.pallas_call(
-            functools.partial(average_kernel, value_width),
-            out_shape=jax.ShapeDtypeStruct((rows_here, msa_rows * value_width), jnp.float32),
-            in_specs=[smem, vmem, vmem],
-            out_specs=vmem,
-            scratch_shapes=[
-                pltpu.VMEM(got.shape, jnp.float32),
-                pltpu.VMEM((tokens, rows_here * heads), jnp.float32),
-            ],
-            compiler_params=pltpu.CompilerParams(vmem_limit_bytes=32 * 1024 * 1024),
-            cost_estimate=pl.CostEstimate(
-                flops=2 * tokens * rows_here * heads * msa_rows * value_width,
-                bytes_accessed=3 * 2**20,
-                transcendentals=0,
-            ),
-        )(
-            lax.dynamic_index_in_dim(places, which, 0, keepdims=False), got, values
-        ).reshape(rows_here, msa_rows, value_width)
-
-    mine = average(mine, half_index)
-    other = average(other, 1 - half_index)
-    low = row_index < col_size
-    averaged = jnp.concatenate(
-        [jnp.where(low, mine, other), jnp.where(low, other, mine)], axis=0
-    )
     sequence_slab = sequence_embedding.reshape(msa_rows, columns_here, features).astype(jnp.float32)
     sequence_normed = apply_layer_norm(sequence_slab, 2).astype(jnp.bfloat16)
     sequence_switch = jax.nn.sigmoid(
@@ -439,18 +453,63 @@
             sequence_entry_matrix[:, value_width:],
             preferred_element_type=jnp.float32,
         )
-    )
-    switched = (sequence_switch * averaged).astype(jnp.bfloat16)
-    final_output = jnp.einsum(
-        "isg,gf->sif", switched, sequence_exit_matrix, preferred_element_type=jnp.float32
-    )
-    sequence_refreshed = (
-        sequence_slab + sequence_present_flags.astype(jnp.float32)[:, None, None] * final_output
-    ).astype(jnp.bfloat16)
-    return (
-        coupling_refreshed,
-        sequence_refreshed.reshape(msa_rows, columns_here * features),
-    )
+    ).reshape(columns_here, msa_rows * value_width)
+    blank = jnp.zeros_like(sequence_exit_matrix)
+    exits = jnp.stack(
+        [
+            jnp.concatenate([sequence_exit_matrix, blank], axis=1),
+            jnp.concatenate([blank, sequence_exit_matrix], axis=1),
+        ]
+    )
+    mine, values, sequence_switch, exits, places = lax.optimization_barrier(
+        (mine, values, sequence_switch, exits, places)
+    )
+    swap = [(a, (a + col_size) % row_size) for a in range(row_size)]
+    other = lax.ppermute(mine, "row", swap)
+
+    half_index = row_index // col_size
+
+    mine_places = lax.dynamic_index_in_dim(places, half_index, 0, keepdims=False)
+    other_places = lax.dynamic_index_in_dim(places, 1 - half_index, 0, keepdims=False)
+    across = msa_rows * value_width
+    averaging = [
+        pltpu.VMEM(mine.shape, jnp.float32),
+        pltpu.VMEM((tokens, rows_here * heads), jnp.float32),
+    ]
+    flops = 2 * tokens * rows_here * heads * across
+    mine = pl.pallas_call(
+        functools.partial(average, value_width),
+        out_shape=jax.ShapeDtypeStruct((rows_here, across), jnp.float32),
+        in_specs=[smem, vmem, vmem],
+        out_specs=vmem,
+        scratch_shapes=averaging,
+        compiler_params=spacious,
+        cost_estimate=work(flops),
+    )(mine_places, mine, values)
+    sequence_refreshed = pl.pallas_call(
+        functools.partial(finish_kernel, value_width, features),
+        out_shape=jax.ShapeDtypeStruct(sequence_embedding.shape, jnp.bfloat16),
+        in_specs=[smem, smem] + [vmem] * 6,
+        out_specs=vmem,
+        scratch_shapes=[pltpu.VMEM((rows_here, across), jnp.float32)]
+        + averaging
+        + [
+            pltpu.VMEM(tiled(columns_here, across), jnp.float32),
+            pltpu.VMEM((msa_rows * rows_here, 2 * features), jnp.float32),
+        ],
+        compiler_params=spacious,
+        cost_estimate=work(flops),
+    )(
+        other_places,
+        sequence_present_flags,
+        other,
+        values,
+        mine,
+        sequence_switch,
+        exits,
+        sequence_embedding,
+    )
+    return coupling_refreshed, sequence_refreshed
 
 
 def solution(mesh):

time: 144 us -> 143 us (level)
  Pallas kernels: 9.16 us -> 10.7 us
    all_to_all x4, waiting for transfers between devices: 53.4 us -> 51.4 us  [exchange(): return lax.all_to_all(blocks, axis, split_axis=0, concat_axis=0, tiled=True)]
    reshape x3 -> x1, local copies, waits for them, and re-layouts: 1.47 us -> 0.02 us  [shards(): sequence_switch = jax.nn.sigmoid(jnp.einsum('sjf,fg->jsg', sequence_norme...]
  transfers between devices with their start and end apart: 8 -> 8, of which waited for: 7 -> 7; matrix products, arithmetic and copies ran while one was open for 8% -> 8% of each run, Pallas kernels for 1% -> 2%
where the time goes in v7:
time: 143 us
  waiting for transfers between devices  71 us (50%)
  starting transfers between devices  47.5 us (33%)
  Pallas kernels  10.7 us (7%)
  local copies, waits for them, and re-layouts  7.2 us (5%)
  other arithmetic  3.43 us (2%)
  matrix products  1.78 us (1%)
    all_to_all x4, waiting for transfers between devices, exchange(): return lax.all_to_all(blocks, axis, split_axis=0, concat_axis=0, tiled=True)  51.4 us
    all_to_all x4, starting transfers between devices, exchange(): return lax.all_to_all(blocks, axis, split_axis=0, concat_axis=0, tiled=True)  31.6 us
    all_to_all x1, waiting for transfers between devices, shards(): lax.all_to_all(jnp.broadcast_to(sent[None], (col_size,) + sent.shape), 'r...  9.06 us
    all_to_all x1, starting transfers between devices, shards(): lax.all_to_all(jnp.broadcast_to(sent[None], (col_size,) + sent.shape), 'r...  7.99 us
    ppermute x1, waiting for transfers between devices, shards(): sent = lax.ppermute(sent, ('row', 'col'), moves)  7.58 us
    ppermute x1, waiting for transfers between devices, shards(): other = lax.ppermute(mine, 'row', swap)  2.98 us
    ppermute x1, starting transfers between devices, shards(): other = lax.ppermute(mine, 'row', swap)  2.93 us
  transfers between devices with their start and end apart: 8, of which 7 were waited for; matrix products, arithmetic and copies ran while one was open for 8% of the time, Pallas kernels for 2%

profile of v7, /device:TPU:32, one launch (start us, length us, event | category | flops | bytes accessed | tf_op | source)
XLA Modules:
  0.0 142.6 jit_solution(3188905832040420309)
XLA Ops:
  0.6 2.4 %shard_map.113 = (bf16[256,512]{1,0:T(8,128)(2,1)}, f32[512,128]{1,0:T(8,128)}) custom-call(s32[512]{0:T(512)} %mask.1, bf16[16,32,128]{2,1,0:T(8,128)(2,1)} %pair_far.1, bf16[128,640]{1,0:T(8,128)(2,1)} %weight_far.1), custom_call_target="tpu_custom_call" | custom-call | flops 83886080 | bytes 1048576 | tf_op jit(solution)/shard_map/pallas_call | solution.py:344
  3.1 16.3 %all-to-all-start = ((bf16[32,8,512]{2,1,0:T(8,128)(2,1)}), bf16[32,8,512]{2,1,0:T(8,128)(2,1)S(1)}, u32[]{:S(2)}, u32[]{:S(2)}) async-start(bf16[32,8,512]{2,1,0:T(8,128)(2,1)} %bitcast.42), calls=%async_computation | async-start | bytes 524288 | tf_op jit(solution)/shard_map/all_to_all | solution.py:24
  21.2 19.3 %all-to-all-done.got = bf16[32,8,512]{2,1,0:T(8,128)(2,1)S(1)} async-done(((bf16[32,8,512]{2,1,0:T(8,128)(2,1)}), bf16[32,8,512]{2,1,0:T(8,128)(2,1)S(1)}, u32[]{:S(2)}, u32[]{:S(2)}) %all-to-all-start) | async-done | bytes 262176 | tf_op jit(solution)/shard_map/all_to_all | solution.py:24
  40.4 1.3 shard_map.114
  41.7 6.9 %all-to-all-start.1 = ((bf16[16,48,512]{2,1,0:T(8,128)(2,1)}), bf16[16,48,512]{2,1,0:T(8,128)(2,1)S(1)}, u32[]{:S(2)}, u32[]{:S(2)}) async-start(bf16[16,48,512]{2,1,0:T(8,128)(2,1)} %shard_map.114), calls=%async_computation.1 | async-start | bytes 1572864 | tf_op jit(solution)/shard_map/all_to_all | solution.py:24
  48.8 14.9 %all-to-all-done.1.got = bf16[16,48,512]{2,1,0:T(8,128)(2,1)S(1)} async-done(((bf16[16,48,512]{2,1,0:T(8,128)(2,1)}), bf16[16,48,512]{2,1,0:T(8,128)(2,1)S(1)}, u32[]{:S(2)}, u32[]{:S(2)}) %all-to-all-start.1) | async-done | bytes 786464 | tf_op jit(solution)/shard_map/all_to_all | solution.py:24
  64.9 3.5 %all-to-all-start.2 = ((bf16[16,16,256]{2,1,0:T(8,128)(2,1)}), bf16[16,16,256]{2,1,0:T(8,128)(2,1)S(1)}, u32[]{:S(2)}, u32[]{:S(2)}) async-start(bf16[16,16,256]{2,1,0:T(8,128)(2,1)} %shard_map.115), calls=%async_computation.2 | async-start | bytes 262144 | tf_op jit(solution)/shard_map/all_to_all | solution.py:24
  68.8 2.2 %collective-permute-start.1 = (bf16[16,16,512]{2,1,0:T(8,128)(2,1)S(1)}, bf16[16,16,512]{2,1,0:T(8,128)(2,1)S(1)}, u32[]{:S(2)}, u32[]{:S(2)}) collective-permute-start(bf16[16,16,512]{2,1,0:T(8,128)(2,1)S(1)} %slice.12), channel_id=1, source_target_pairs={{0,1},{1,0},{2,3},{3,2},{4,5},{5,4},{6,7},{7,6},{8,9},{9,8},{10,11... | collective-permute-start | bytes 786440 | tf_op jit(solution)/shard_map/ppermute | solution.py:381
  71.1 5.4 %all-to-all-done.2.got = bf16[16,16,256]{2,1,0:T(8,128)(2,1)S(1)} async-done(((bf16[16,16,256]{2,1,0:T(8,128)(2,1)}), bf16[16,16,256]{2,1,0:T(8,128)(2,1)S(1)}, u32[]{:S(2)}, u32[]{:S(2)}) %all-to-all-start.2) | async-done | bytes 131104 | tf_op jit(solution)/shard_map/all_to_all | solution.py:24
  77.5 4.9 %all-to-all-start.3 = ((bf16[32,16,128]{2,1,0:T(8,128)(2,1)}), bf16[32,16,128]{2,1,0:T(8,128)(2,1)S(1)}, u32[]{:S(2)}, u32[]{:S(2)}) async-start(bf16[32,16,128]{2,1,0:T(8,128)(2,1)} %bitcast.2), calls=%async_computation.3 | async-start | bytes 262144 | tf_op jit(solution)/shard_map/all_to_all | solution.py:24
  84.5 1.6 %reshape.75 = f32[16,8,32,64]{3,2,1,0:T(8,128)S(1)} reshape(f32[16,32,512]{2,1,0:T(8,128)} %maximum_convert_fusion) | data formatting | bytes 2097152 | tf_op jit(solution)/shard_map/convert_element_type | solution.py:439
  86.8 11.8 %all-to-all-done.3 = bf16[32,16,128]{2,1,0:T(8,128)(2,1)S(1)} async-done(((bf16[32,16,128]{2,1,0:T(8,128)(2,1)}), bf16[32,16,128]{2,1,0:T(8,128)(2,1)S(1)}, u32[]{:S(2)}, u32[]{:S(2)}) %all-to-all-start.3) | async-done | bytes 131104 | tf_op jit(solution)/shard_map/all_to_all | solution.py:24
  98.6 1.6 %shard_map.117 = (bf16[512,128]{1,0:T(8,128)(2,1)}, f32[40,128]{1,0:T(8,128)S(1)}) custom-call(s32[512]{0:T(512)S(1)} %copy-done.5, s32[4,128]{1,0:T(4,128)S(1)} %bitcast.40, bf16[512,128]{1,0:T(8,128)(2,1)S(1)} %bitcast.38, f32[512,128]{1,0:T(8,128)S(1)} %copy-done.2, bf16[512,128]{1,0:T(8,128)(2,1)S(1)} %bitcast.39, bf16[128,128]{1,0:T(8,128)(2,1)S(1)} %copy-done.4, ...), custom_call_target="tpu_custom_call" | custom-call | flops 33554432 | bytes 1048576 | tf_op jit(solution)/shard_map/pallas_call | solution.py:406
  100.2 2.8 %collective-permute-start = (bf16[40,128]{1,0:T(8,128)(2,1)S(1)}, bf16[40,128]{1,0:T(8,128)(2,1)S(1)}, u32[]{:S(2)}, u32[]{:S(2)}) collective-permute-start(bf16[40,128]{1,0:T(8,128)(2,1)S(1)} %convert_element_type.27), channel_id=1, source_target_pairs={{0,128},{1,96},{2,144},{3,64},{4,176},{5,32},{6,112},{7,80},{8,160... | collective-permute-start | bytes 30728 | tf_op jit(solution)/shard_map/ppermute | solution.py:429
  103.0 7.6 %collective-permute-done = bf16[40,128]{1,0:T(8,128)(2,1)S(1)} collective-permute-done((bf16[40,128]{1,0:T(8,128)(2,1)S(1)}, bf16[40,128]{1,0:T(8,128)(2,1)S(1)}, u32[]{:S(2)}, u32[]{:S(2)}) %collective-permute-start) | collective-permute-done | bytes 10272 | tf_op jit(solution)/shard_map/ppermute | solution.py:429
  111.2 8.0 %all-to-all-start.4 = ((bf16[16,40,128]{2,1,0:T(8,128)(2,1)}), bf16[16,40,128]{2,1,0:T(8,128)(2,1)S(1)}, u32[]{:S(2)}, u32[]{:S(2)}) async-start(bf16[16,40,128]{2,1,0:T(8,128)(2,1)} %broadcast_in_dim.2), calls=%async_computation.4 | async-start | bytes 327680 | tf_op jit(solution)/shard_map/all_to_all | solution.py:431
  119.2 1.3 multiply_reduce_fusion
  120.6 1.5 %convert_bitcast_fusion = bf16[16,32,8,256]{3,1,2,0:T(8,128)(2,1)S(1)} fusion(f32[16,8,32,64]{3,2,1,0:T(8,128)S(1)} %reshape.75, f32[16,8,32]{2,1,0:T(8,128)S(1)} %add_rsqrt_fusion, f32[16,8,32]{2,1,0:T(8,128)S(1)} %broadcast_multiply_fusion, bf16[64,512]{1,0:T(8,128)(2,1)S(1)} %copy-done.8), kind=kOutput, calls=%fused_computation | convolution fusion | flops 136052736 | bytes 4358144 | tf_op jit(solution)/shard_map/qsjf,fg->qjsg/dot_general | solution.py:440
  122.1 1.4 %copy.18 = bf16[16,32,8,256]{3,2,1,0:T(8,128)(2,1)S(1)} copy(bf16[16,32,8,256]{3,1,2,0:T(8,128)(2,1)S(1)} %convert_bitcast_fusion) | data formatting | bytes 4194304 | tf_op jit(solution)/shard_map/convert_element_type | solution.py:445
  124.2 9.1 %all-to-all-done.4.got = bf16[16,40,128]{2,1,0:T(8,128)(2,1)S(1)} async-done(((bf16[16,40,128]{2,1,0:T(8,128)(2,1)}), bf16[16,40,128]{2,1,0:T(8,128)(2,1)S(1)}, u32[]{:S(2)}, u32[]{:S(2)}) %all-to-all-start.4) | async-done | bytes 163872 | tf_op jit(solution)/shard_map/all_to_all | solution.py:431
  133.3 2.9 %collective-permute-start.2 = (bf16[16,40,128]{2,1,0:T(8,128)(2,1)S(1)}, bf16[16,40,128]{2,1,0:T(8,128)(2,1)S(1)}, u32[]{:S(2)}, u32[]{:S(2)}) collective-permute-start(bf16[16,40,128]{2,1,0:T(8,128)(2,1)S(1)} %all-to-all-done.4.got), channel_id=1, source_target_pairs={{0,256},{16,272},{32,288},{48,304},{64,320},{80,336},{96,352},{112... | collective-permute-start | bytes 491528 | tf_op jit(solution)/shard_map/ppermute | solution.py:468
  136.3 1.2 shard_map.118.mine
  137.5 3.0 %collective-permute-done.2.got = bf16[16,40,128]{2,1,0:T(8,128)(2,1)S(1)} collective-permute-done((bf16[16,40,128]{2,1,0:T(8,128)(2,1)S(1)}, bf16[16,40,128]{2,1,0:T(8,128)(2,1)S(1)}, u32[]{:S(2)}, u32[]{:S(2)}) %collective-permute-start.2) | collective-permute-done | bytes 163872 | tf_op jit(solution)/shard_map/ppermute | solution.py:468
  140.5 2.1 %shard_map.119 = bf16[8,2048]{1,0:T(8,128)(2,1)} custom-call(s32[16]{0:T(128)S(1)} %get-tuple-element.25.places, s32[8]{0:T(128)S(1)} %copy-done.6, bf16[16,40,128]{2,1,0:T(8,128)(2,1)S(1)} %collective-permute-done.2.got, bf16[512,2048]{1,0:T(8,128)(2,1)S(1)} %bitcast.36, f32[16,2048]{1,0:T(8,128)S(1)} %shard_map.118.mine, f32[32,2048]{1,0:T(8,128)S(1)} %bitcast.37, ...), custom_call_target="tpu_custom_call" | custom-call | flops 268435456 | bytes 1048576 | tf_op jit(solution)/shard_map/pallas_call | solution.py:489
  (45 shorter events, 8.6 us)
Async XLA Ops:
  0.6 48.2 %copy-start = (bf16[128,8]{0,1:T(8,128)(2,1)S(1)}, bf16[128,8]{0,1:T(8,128)(2,1)}, u32[]{:S(2)}) copy-start(bf16[128,8]{0,1:T(8,128)(2,1)} %param.16) | copy-start | bytes 6148
  3.1 37.3 %all-to-all-start = ((bf16[32,8,512]{2,1,0:T(8,128)(2,1)}), bf16[32,8,512]{2,1,0:T(8,128)(2,1)S(1)}, u32[]{:S(2)}, u32[]{:S(2)}) async-start(bf16[32,8,512]{2,1,0:T(8,128)(2,1)} %bitcast.42), calls=%async_computation | async-start | bytes 524288 | tf_op jit(solution)/shard_map/all_to_all | solution.py:24
  21.0 47.4 %copy-start.8 = (bf16[64,512]{1,0:T(8,128)(2,1)S(1)}, bf16[64,512]{1,0:T(8,128)(2,1)}, u32[]{:S(2)}) copy-start(bf16[64,512]{1,0:T(8,128)(2,1)} %param.17) | copy-start | bytes 196612
  41.7 27.0 %copy-start.7 = (bf16[256,64]{0,1:T(8,128)(2,1)S(1)}, bf16[256,64]{0,1:T(8,128)(2,1)}, u32[]{:S(2)}) copy-start(bf16[256,64]{0,1:T(8,128)(2,1)} %param.18) | copy-start | bytes 98308
  41.7 22.1 %all-to-all-start.1 = ((bf16[16,48,512]{2,1,0:T(8,128)(2,1)}), bf16[16,48,512]{2,1,0:T(8,128)(2,1)S(1)}, u32[]{:S(2)}, u32[]{:S(2)}) async-start(bf16[16,48,512]{2,1,0:T(8,128)(2,1)} %shard_map.114), calls=%async_computation.1 | async-start | bytes 1572864 | tf_op jit(solution)/shard_map/all_to_all | solution.py:24
  64.9 11.7 %all-to-all-start.2 = ((bf16[16,16,256]{2,1,0:T(8,128)(2,1)}), bf16[16,16,256]{2,1,0:T(8,128)(2,1)S(1)}, u32[]{:S(2)}, u32[]{:S(2)}) async-start(bf16[16,16,256]{2,1,0:T(8,128)(2,1)} %shard_map.115), calls=%async_computation.2 | async-start | bytes 262144 | tf_op jit(solution)/shard_map/all_to_all | solution.py:24
  68.8 14.5 %collective-permute-start.1 = (bf16[16,16,512]{2,1,0:T(8,128)(2,1)S(1)}, bf16[16,16,512]{2,1,0:T(8,128)(2,1)S(1)}, u32[]{:S(2)}, u32[]{:S(2)}) collective-permute-start(bf16[16,16,512]{2,1,0:T(8,128)(2,1)S(1)} %slice.12), channel_id=1, source_target_pairs={{0,1},{1,0},{2,3},{3,2},{4,5},{5,4},{6,7},{7,6},{8,9},{9,8},{10,11... | collective-permute-start | bytes 786440 | tf_op jit(solution)/shard_map/ppermute | solution.py:381
  77.5 21.0 %all-to-all-start.3 = ((bf16[32,16,128]{2,1,0:T(8,128)(2,1)}), bf16[32,16,128]{2,1,0:T(8,128)(2,1)S(1)}, u32[]{:S(2)}, u32[]{:S(2)}) async-start(bf16[32,16,128]{2,1,0:T(8,128)(2,1)} %bitcast.2), calls=%async_computation.3 | async-start | bytes 262144 | tf_op jit(solution)/shard_map/all_to_all | solution.py:24
  84.5 14.0 %copy-start.2 = (f32[512,128]{1,0:T(8,128)S(1)}, f32[512,128]{1,0:T(8,128)}, u32[]{:S(2)}) copy-start(f32[512,128]{1,0:T(8,128)} %get-tuple-element.12.gate) | copy-start | bytes 786436
  84.5 14.0 %copy-start.3 = (bf16[16,32,128]{2,1,0:T(8,128)(2,1)S(1)}, bf16[16,32,128]{2,1,0:T(8,128)(2,1)}, u32[]{:S(2)}) copy-start(bf16[16,32,128]{2,1,0:T(8,128)(2,1)} %pair_far.1) | copy-start | bytes 393220
  84.5 14.0 %copy-start.4 = (bf16[128,128]{1,0:T(8,128)(2,1)S(1)}, bf16[128,128]{1,0:T(8,128)(2,1)}, u32[]{:S(2)}) copy-start(bf16[128,128]{1,0:T(8,128)(2,1)} %weight.1) | copy-start | bytes 98308
  84.5 14.0 %copy-start.5 = (s32[512]{0:T(512)S(1)}, s32[512]{0:T(512)}, u32[]{:S(2)}) copy-start(s32[512]{0:T(512)} %mask.1) | copy-start | bytes 6148
  100.2 10.4 %collective-permute-start = (bf16[40,128]{1,0:T(8,128)(2,1)S(1)}, bf16[40,128]{1,0:T(8,128)(2,1)S(1)}, u32[]{:S(2)}, u32[]{:S(2)}) collective-permute-start(bf16[40,128]{1,0:T(8,128)(2,1)S(1)} %convert_element_type.27), channel_id=1, source_target_pairs={{0,128},{1,96},{2,144},{3,64},{4,176},{5,32},{6,112},{7,80},{8,160... | collective-permute-start | bytes 30728 | tf_op jit(solution)/shard_map/ppermute | solution.py:429
  111.2 22.1 %all-to-all-start.4 = ((bf16[16,40,128]{2,1,0:T(8,128)(2,1)}), bf16[16,40,128]{2,1,0:T(8,128)(2,1)S(1)}, u32[]{:S(2)}, u32[]{:S(2)}) async-start(bf16[16,40,128]{2,1,0:T(8,128)(2,1)} %broadcast_in_dim.2), calls=%async_computation.4 | async-start | bytes 327680 | tf_op jit(solution)/shard_map/all_to_all | solution.py:431
  124.2 16.3 %copy-start.1 = (bf16[8,2048]{1,0:T(8,128)(2,1)S(1)}, bf16[8,2048]{1,0:T(8,128)(2,1)}, u32[]{:S(2)}) copy-start(bf16[8,2048]{1,0:T(8,128)(2,1)} %tile.13) | copy-start | bytes 98308
  124.2 16.3 %copy-start.6 = (s32[8]{0:T(128)S(1)}, s32[8]{0:T(128)}, u32[]{:S(2)}) copy-start(s32[8]{0:T(128)} %flags.1) | copy-start | bytes 100
  133.3 7.2 %collective-permute-start.2 = (bf16[16,40,128]{2,1,0:T(8,128)(2,1)S(1)}, bf16[16,40,128]{2,1,0:T(8,128)(2,1)S(1)}, u32[]{:S(2)}, u32[]{:S(2)}) collective-permute-start(bf16[16,40,128]{2,1,0:T(8,128)(2,1)S(1)} %all-to-all-done.4.got), channel_id=1, source_target_pairs={{0,256},{16,272},{32,288},{48,304},{64,320},{80,336},{96,352},{112... | collective-permute-start | bytes 491528 | tf_op jit(solution)/shard_map/ppermute | solution.py:468

commit v8 on v7

--- a/solution.py
+++ b/solution.py
@@ -134,7 +134,7 @@
                 place = (c * 2 + i) * 2 + j
                 sent[place, :columns, :width] = sides[0][i][c]
                 sent[place, :columns, width:] = sides[1][j][c]
-                sent[place, columns:, :] = rider[place % 2]
+                sent[place, columns:, :] = rider[place % 4]
 
 
 def multiply_kernel(columns, row_size, got, crossed, wide):
@@ -196,13 +196,11 @@
     after = (pair[...].astype(jnp.float32) + gate[...] * update).astype(jnp.bfloat16)
     coupling[...] = after
     normed = normed_rows(after.astype(jnp.float32)).astype(jnp.bfloat16)
-    lane = lax.broadcasted_iota(jnp.int32, (channels, lanes), 1)
+    every = jnp.dot(normed, bias[...], preferred_element_type=jnp.float32)
+    lane = lax.broadcasted_iota(jnp.int32, (columns, lanes), 1) // heads
     scores = jnp.zeros((columns, lanes), jnp.float32)
     for i in range(rows):
-        own = jnp.where(lane // heads == i, bias[...], jnp.zeros((), jnp.bfloat16))
-        scores = scores + jnp.dot(
-            normed[i * columns : (i + 1) * columns], own, preferred_element_type=jnp.float32
-        )
+        scores = jnp.where(lane == i, every[i * columns : (i + 1) * columns], scores)
     place = lax.broadcasted_iota(jnp.int32, (columns, lanes), 0)
     first_column = lax.axis_index("col") * columns
     valid = jnp.zeros((columns, lanes), jnp.int32)
@@ -361,7 +359,7 @@
     )(token_valid_mask, pair_state, triangle_input_weight)
 
     got = exchange(sent.reshape(row_size, 2 * channels_here, patch), "row")
-    rider = sequence_embedding.reshape(2, -1, 2 * width)
+    rider = sequence_embedding.reshape(4, -1, 2 * width)
     sent = pl.pallas_call(
         functools.partial(gathered_kernel, columns_here),
         out_shape=jax.ShapeDtypeStruct(
@@ -377,12 +375,14 @@
         cost_estimate=work(patch * channels),
     )(got, rider)
     got = exchange(sent, "col")
-    half = got[:, columns_here:]
-    half_other = lax.ppermute(half, "col", [(a, a ^ 1) for a in range(col_size)])
-    first = col_index % 2 == 0
-    sequence_all = jnp.concatenate(
-        [jnp.where(first, half, half_other), jnp.where(first, half_other, half)], axis=1
-    ).reshape(col_size, msa_rows, columns_here, features)
+    share = got[:, columns_here:]
+    for step in (1, 2):
+        swapped = lax.ppermute(share, "col", [(a, a ^ step) for a in range(col_size)])
+        first = col_index // step % 2 == 0
+        share = jnp.concatenate(
+            [jnp.where(first, share, swapped), jnp.where(first, swapped, share)], axis=1
+        )
+    sequence_all = share.reshape(col_size, msa_rows, columns_here, features)
     sent = pl.pallas_call(
         functools.partial(multiply_kernel, columns_here, row_size),
         out_shape=jax.ShapeDtypeStruct((col_size, rows_here, width), jnp.bfloat16),

time: 143 us -> 144 us (level)
  the two profiles are of different devices: /device:TPU:32 before, /device:TPU:2 now
where the time goes in v8:
time: 144 us; the launch traced here: 143 us
  waiting for transfers between devices  65.4 us (45%)
  starting transfers between devices  53.6 us (37%)
  Pallas kernels  10.6 us (7%)
  local copies, waits for them, and re-layouts  7.2 us (5%)
  other arithmetic  3.62 us (3%)
  matrix products  1.79 us (1%)
    all_to_all x4, waiting for transfers between devices, exchange(): return lax.all_to_all(blocks, axis, split_axis=0, concat_axis=0, tiled=True)  48.2 us
    all_to_all x4, starting transfers between devices, exchange(): return lax.all_to_all(blocks, axis, split_axis=0, concat_axis=0, tiled=True)  32.1 us
    all_to_all x1, starting transfers between devices, shards(): lax.all_to_all(jnp.broadcast_to(sent[None], (col_size,) + sent.shape), 'r...  10.5 us
    all_to_all x1, waiting for transfers between devices, shards(): lax.all_to_all(jnp.broadcast_to(sent[None], (col_size,) + sent.shape), 'r...  8.36 us
    ppermute x1, waiting for transfers between devices, shards(): sent = lax.ppermute(sent, ('row', 'col'), moves)  5.9 us
    ppermute x2, starting transfers between devices, shards(): lax.ppermute(share, 'col', [(a, a ^ step) for a in range(col_size)])  5.64 us
    ppermute x1, starting transfers between devices, shards(): other = lax.ppermute(mine, 'row', swap)  3 us
    ppermute x1, waiting for transfers between devices, shards(): other = lax.ppermute(mine, 'row', swap)  2.9 us
  transfers between devices with their start and end apart: 9, of which 7 were waited for; matrix products, arithmetic and copies ran while one was open for 8% of the time, Pallas kernels for 2%

profile of v8, /device:TPU:2, one launch (start us, length us, event | category | flops | bytes accessed | tf_op | source)
XLA Modules:
  0.0 143.2 jit_solution(4198895014470770910)
XLA Ops:
  0.7 2.4 %shard_map.113 = (bf16[256,512]{1,0:T(8,128)(2,1)}, f32[512,128]{1,0:T(8,128)}) custom-call(s32[512]{0:T(512)} %mask.1, bf16[16,32,128]{2,1,0:T(8,128)(2,1)} %pair_far.1, bf16[128,640]{1,0:T(8,128)(2,1)} %weight_far.1), custom_call_target="tpu_custom_call" | custom-call | flops 83886080 | bytes 1048576 | tf_op jit(solution)/shard_map/pallas_call | solution.py:342
  3.1 16.7 %all-to-all-start = ((bf16[32,8,512]{2,1,0:T(8,128)(2,1)}), bf16[32,8,512]{2,1,0:T(8,128)(2,1)S(1)}, u32[]{:S(2)}, u32[]{:S(2)}) async-start(bf16[32,8,512]{2,1,0:T(8,128)(2,1)} %bitcast.42), calls=%async_computation | async-start | bytes 524288 | tf_op jit(solution)/shard_map/all_to_all | solution.py:24
  21.6 19.2 %all-to-all-done.got = bf16[32,8,512]{2,1,0:T(8,128)(2,1)S(1)} async-done(((bf16[32,8,512]{2,1,0:T(8,128)(2,1)}), bf16[32,8,512]{2,1,0:T(8,128)(2,1)S(1)}, u32[]{:S(2)}, u32[]{:S(2)}) %all-to-all-start) | async-done | bytes 262176 | tf_op jit(solution)/shard_map/all_to_all | solution.py:24
  40.8 1.3 shard_map.114
  42.0 6.1 %all-to-all-start.1 = ((bf16[16,40,512]{2,1,0:T(8,128)(2,1)}), bf16[16,40,512]{2,1,0:T(8,128)(2,1)S(1)}, u32[]{:S(2)}, u32[]{:S(2)}) async-start(bf16[16,40,512]{2,1,0:T(8,128)(2,1)} %shard_map.114), calls=%async_computation.1 | async-start | bytes 1310720 | tf_op jit(solution)/shard_map/all_to_all | solution.py:24
  48.6 13.4 %all-to-all-done.1.got = bf16[16,40,512]{2,1,0:T(8,128)(2,1)S(1)} async-done(((bf16[16,40,512]{2,1,0:T(8,128)(2,1)}), bf16[16,40,512]{2,1,0:T(8,128)(2,1)S(1)}, u32[]{:S(2)}, u32[]{:S(2)}) %all-to-all-start.1) | async-done | bytes 655392 | tf_op jit(solution)/shard_map/all_to_all | solution.py:24
  62.0 1.9 %collective-permute-start.1 = (bf16[16,8,512]{2,1,0:T(8,128)(2,1)S(1)}, bf16[16,8,512]{2,1,0:T(8,128)(2,1)S(1)}, u32[]{:S(2)}, u32[]{:S(2)}) collective-permute-start(bf16[16,8,512]{2,1,0:T(8,128)(2,1)S(1)} %slice.12), channel_id=1, source_target_pairs={{0,1},{1,0},{2,3},{3,2},{4,5},{5,4},{6,7},{7,6},{8,9},{9,8},{10,11... | collective-permute-start | bytes 393224 | tf_op jit(solution)/shard_map/ppermute | solution.py:380
  65.3 3.5 %all-to-all-start.2 = ((bf16[16,16,256]{2,1,0:T(8,128)(2,1)}), bf16[16,16,256]{2,1,0:T(8,128)(2,1)S(1)}, u32[]{:S(2)}, u32[]{:S(2)}) async-start(bf16[16,16,256]{2,1,0:T(8,128)(2,1)} %shard_map.115), calls=%async_computation.2 | async-start | bytes 262144 | tf_op jit(solution)/shard_map/all_to_all | solution.py:24
  68.9 3.7 %collective-permute-start.2 = (bf16[16,16,512]{2,1,0:T(8,128)(2,1)S(1)}, bf16[16,16,512]{2,1,0:T(8,128)(2,1)S(1)}, u32[]{:S(2)}, u32[]{:S(2)}) collective-permute-start(bf16[16,16,512]{2,1,0:T(8,128)(2,1)S(1)} %pad_maximum_fusion), channel_id=1, source_target_pairs={{0,2},{1,3},{2,0},{3,1},{4,6},{5,7},{6,4},{7,5},{8,10},{9,11},{10,... | collective-permute-start | bytes 786440 | tf_op jit(solution)/shard_map/ppermute | solution.py:380
  72.7 4.3 %all-to-all-done.2.got = bf16[16,16,256]{2,1,0:T(8,128)(2,1)S(1)} async-done(((bf16[16,16,256]{2,1,0:T(8,128)(2,1)}), bf16[16,16,256]{2,1,0:T(8,128)(2,1)S(1)}, u32[]{:S(2)}, u32[]{:S(2)}) %all-to-all-start.2) | async-done | bytes 131104 | tf_op jit(solution)/shard_map/all_to_all | solution.py:24
  78.0 5.7 %all-to-all-start.3 = ((bf16[32,16,128]{2,1,0:T(8,128)(2,1)}), bf16[32,16,128]{2,1,0:T(8,128)(2,1)S(1)}, u32[]{:S(2)}, u32[]{:S(2)}) async-start(bf16[32,16,128]{2,1,0:T(8,128)(2,1)} %bitcast.2), calls=%async_computation.3 | async-start | bytes 262144 | tf_op jit(solution)/shard_map/all_to_all | solution.py:24
  85.9 1.6 %reshape.75 = f32[16,8,32,64]{3,2,1,0:T(8,128)S(1)} reshape(f32[16,32,512]{2,1,0:T(8,128)} %maximum_convert_fusion) | data formatting | bytes 2097152 | tf_op jit(solution)/shard_map/convert_element_type | solution.py:439
  88.1 11.4 %all-to-all-done.3 = bf16[32,16,128]{2,1,0:T(8,128)(2,1)S(1)} async-done(((bf16[32,16,128]{2,1,0:T(8,128)(2,1)}), bf16[32,16,128]{2,1,0:T(8,128)(2,1)S(1)}, u32[]{:S(2)}, u32[]{:S(2)}) %all-to-all-start.3) | async-done | bytes 131104 | tf_op jit(solution)/shard_map/all_to_all | solution.py:24
  99.5 1.5 %shard_map.117 = (bf16[512,128]{1,0:T(8,128)(2,1)}, f32[40,128]{1,0:T(8,128)S(1)}) custom-call(s32[512]{0:T(512)S(1)} %copy-done.5, s32[4,128]{1,0:T(4,128)S(1)} %bitcast.40, bf16[512,128]{1,0:T(8,128)(2,1)S(1)} %bitcast.38, f32[512,128]{1,0:T(8,128)S(1)} %copy-done.2, bf16[512,128]{1,0:T(8,128)(2,1)S(1)} %bitcast.39, bf16[128,128]{1,0:T(8,128)(2,1)S(1)} %copy-done.4, ...), custom_call_target="tpu_custom_call" | custom-call | flops 33554432 | bytes 1048576 | tf_op jit(solution)/shard_map/pallas_call | solution.py:406
  101.0 2.4 %collective-permute-start = (bf16[40,128]{1,0:T(8,128)(2,1)S(1)}, bf16[40,128]{1,0:T(8,128)(2,1)S(1)}, u32[]{:S(2)}, u32[]{:S(2)}) collective-permute-start(bf16[40,128]{1,0:T(8,128)(2,1)S(1)} %convert_element_type.27), channel_id=1, source_target_pairs={{0,128},{1,96},{2,144},{3,64},{4,176},{5,32},{6,112},{7,80},{8,160... | collective-permute-start | bytes 30728 | tf_op jit(solution)/shard_map/ppermute | solution.py:429
  103.4 5.9 %collective-permute-done = bf16[40,128]{1,0:T(8,128)(2,1)S(1)} collective-permute-done((bf16[40,128]{1,0:T(8,128)(2,1)S(1)}, bf16[40,128]{1,0:T(8,128)(2,1)S(1)}, u32[]{:S(2)}, u32[]{:S(2)}) %collective-permute-start) | collective-permute-done | bytes 10272 | tf_op jit(solution)/shard_map/ppermute | solution.py:429
  110.0 10.5 %all-to-all-start.4 = ((bf16[16,40,128]{2,1,0:T(8,128)(2,1)}), bf16[16,40,128]{2,1,0:T(8,128)(2,1)S(1)}, u32[]{:S(2)}, u32[]{:S(2)}) async-start(bf16[16,40,128]{2,1,0:T(8,128)(2,1)} %broadcast_in_dim.2), calls=%async_computation.4 | async-start | bytes 327680 | tf_op jit(solution)/shard_map/all_to_all | solution.py:431
  120.5 1.3 multiply_reduce_fusion
  121.9 1.5 %convert_bitcast_fusion = bf16[16,32,8,256]{3,1,2,0:T(8,128)(2,1)S(1)} fusion(f32[16,8,32,64]{3,2,1,0:T(8,128)S(1)} %reshape.75, f32[16,8,32]{2,1,0:T(8,128)S(1)} %add_rsqrt_fusion, f32[16,8,32]{2,1,0:T(8,128)S(1)} %broadcast_multiply_fusion, bf16[64,512]{1,0:T(8,128)(2,1)S(1)} %copy-done.8), kind=kOutput, calls=%fused_computation | convolution fusion | flops 136052736 | bytes 4358144 | tf_op jit(solution)/shard_map/qsjf,fg->qjsg/dot_general | solution.py:440
  123.4 1.4 %copy.18 = bf16[16,32,8,256]{3,2,1,0:T(8,128)(2,1)S(1)} copy(bf16[16,32,8,256]{3,1,2,0:T(8,128)(2,1)S(1)} %convert_bitcast_fusion) | data formatting | bytes 4194304 | tf_op jit(solution)/shard_map/convert_element_type | solution.py:445
  125.6 8.4 %all-to-all-done.4.got = bf16[16,40,128]{2,1,0:T(8,128)(2,1)S(1)} async-done(((bf16[16,40,128]{2,1,0:T(8,128)(2,1)}), bf16[16,40,128]{2,1,0:T(8,128)(2,1)S(1)}, u32[]{:S(2)}, u32[]{:S(2)}) %all-to-all-start.4) | async-done | bytes 163872 | tf_op jit(solution)/shard_map/all_to_all | solution.py:431
  133.9 3.0 %collective-permute-start.3 = (bf16[16,40,128]{2,1,0:T(8,128)(2,1)S(1)}, bf16[16,40,128]{2,1,0:T(8,128)(2,1)S(1)}, u32[]{:S(2)}, u32[]{:S(2)}) collective-permute-start(bf16[16,40,128]{2,1,0:T(8,128)(2,1)S(1)} %all-to-all-done.4.got), channel_id=1, source_target_pairs={{0,256},{16,272},{32,288},{48,304},{64,320},{80,336},{96,352},{112... | collective-permute-start | bytes 491528 | tf_op jit(solution)/shard_map/ppermute | solution.py:468
  138.2 2.9 %collective-permute-done.3.got = bf16[16,40,128]{2,1,0:T(8,128)(2,1)S(1)} collective-permute-done((bf16[16,40,128]{2,1,0:T(8,128)(2,1)S(1)}, bf16[16,40,128]{2,1,0:T(8,128)(2,1)S(1)}, u32[]{:S(2)}, u32[]{:S(2)}) %collective-permute-start.3) | collective-permute-done | bytes 163872 | tf_op jit(solution)/shard_map/ppermute | solution.py:468
  141.1 2.1 %shard_map.119 = bf16[8,2048]{1,0:T(8,128)(2,1)} custom-call(s32[16]{0:T(128)S(1)} %get-tuple-element.27.places, s32[8]{0:T(128)S(1)} %copy-done.6, bf16[16,40,128]{2,1,0:T(8,128)(2,1)S(1)} %collective-permute-done.3.got, bf16[512,2048]{1,0:T(8,128)(2,1)S(1)} %bitcast.36, f32[16,2048]{1,0:T(8,128)S(1)} %shard_map.118.mine, f32[32,2048]{1,0:T(8,128)S(1)} %bitcast.37, ...), custom_call_target="tpu_custom_call" | custom-call | flops 268435456 | bytes 1048576 | tf_op jit(solution)/shard_map/pallas_call | solution.py:489
  (49 shorter events, 10.0 us)
Async XLA Ops:
  0.6 47.9 %copy-start = (bf16[128,8]{0,1:T(8,128)(2,1)S(1)}, bf16[128,8]{0,1:T(8,128)(2,1)}, u32[]{:S(2)}) copy-start(bf16[128,8]{0,1:T(8,128)(2,1)} %param.16) | copy-start | bytes 6148
  0.6 47.6 %copy-start.7 = (bf16[256,64]{0,1:T(8,128)(2,1)S(1)}, bf16[256,64]{0,1:T(8,128)(2,1)}, u32[]{:S(2)}) copy-start(bf16[256,64]{0,1:T(8,128)(2,1)} %param.18) | copy-start | bytes 98308
  0.7 63.3 %copy-start.8 = (bf16[64,512]{1,0:T(8,128)(2,1)S(1)}, bf16[64,512]{1,0:T(8,128)(2,1)}, u32[]{:S(2)}) copy-start(bf16[64,512]{1,0:T(8,128)(2,1)} %param.17) | copy-start | bytes 196612
  3.1 37.7 %all-to-all-start = ((bf16[32,8,512]{2,1,0:T(8,128)(2,1)}), bf16[32,8,512]{2,1,0:T(8,128)(2,1)S(1)}, u32[]{:S(2)}, u32[]{:S(2)}) async-start(bf16[32,8,512]{2,1,0:T(8,128)(2,1)} %bitcast.42), calls=%async_computation | async-start | bytes 524288 | tf_op jit(solution)/shard_map/all_to_all | solution.py:24
  42.0 20.0 %all-to-all-start.1 = ((bf16[16,40,512]{2,1,0:T(8,128)(2,1)}), bf16[16,40,512]{2,1,0:T(8,128)(2,1)S(1)}, u32[]{:S(2)}, u32[]{:S(2)}) async-start(bf16[16,40,512]{2,1,0:T(8,128)(2,1)} %shard_map.114), calls=%async_computation.1 | async-start | bytes 1310720 | tf_op jit(solution)/shard_map/all_to_all | solution.py:24
  62.0 6.8 %collective-permute-start.1 = (bf16[16,8,512]{2,1,0:T(8,128)(2,1)S(1)}, bf16[16,8,512]{2,1,0:T(8,128)(2,1)S(1)}, u32[]{:S(2)}, u32[]{:S(2)}) collective-permute-start(bf16[16,8,512]{2,1,0:T(8,128)(2,1)S(1)} %slice.12), channel_id=1, source_target_pairs={{0,1},{1,0},{2,3},{3,2},{4,5},{5,4},{6,7},{7,6},{8,9},{9,8},{10,11... | collective-permute-start | bytes 393224 | tf_op jit(solution)/shard_map/ppermute | solution.py:380
  65.3 11.7 %all-to-all-start.2 = ((bf16[16,16,256]{2,1,0:T(8,128)(2,1)}), bf16[16,16,256]{2,1,0:T(8,128)(2,1)S(1)}, u32[]{:S(2)}, u32[]{:S(2)}) async-start(bf16[16,16,256]{2,1,0:T(8,128)(2,1)} %shard_map.115), calls=%async_computation.2 | async-start | bytes 262144 | tf_op jit(solution)/shard_map/all_to_all | solution.py:24
  68.9 15.6 %collective-permute-start.2 = (bf16[16,16,512]{2,1,0:T(8,128)(2,1)S(1)}, bf16[16,16,512]{2,1,0:T(8,128)(2,1)S(1)}, u32[]{:S(2)}, u32[]{:S(2)}) collective-permute-start(bf16[16,16,512]{2,1,0:T(8,128)(2,1)S(1)} %pad_maximum_fusion), channel_id=1, source_target_pairs={{0,2},{1,3},{2,0},{3,1},{4,6},{5,7},{6,4},{7,5},{8,10},{9,11},{10,... | collective-permute-start | bytes 786440 | tf_op jit(solution)/shard_map/ppermute | solution.py:380
  78.0 21.5 %all-to-all-start.3 = ((bf16[32,16,128]{2,1,0:T(8,128)(2,1)}), bf16[32,16,128]{2,1,0:T(8,128)(2,1)S(1)}, u32[]{:S(2)}, u32[]{:S(2)}) async-start(bf16[32,16,128]{2,1,0:T(8,128)(2,1)} %bitcast.2), calls=%async_computation.3 | async-start | bytes 262144 | tf_op jit(solution)/shard_map/all_to_all | solution.py:24
  85.9 13.6 %copy-start.2 = (f32[512,128]{1,0:T(8,128)S(1)}, f32[512,128]{1,0:T(8,128)}, u32[]{:S(2)}) copy-start(f32[512,128]{1,0:T(8,128)} %get-tuple-element.12.gate) | copy-start | bytes 786436
  85.9 13.6 %copy-start.3 = (bf16[16,32,128]{2,1,0:T(8,128)(2,1)S(1)}, bf16[16,32,128]{2,1,0:T(8,128)(2,1)}, u32[]{:S(2)}) copy-start(bf16[16,32,128]{2,1,0:T(8,128)(2,1)} %pair_far.1) | copy-start | bytes 393220
  85.9 13.6 %copy-start.4 = (bf16[128,128]{1,0:T(8,128)(2,1)S(1)}, bf16[128,128]{1,0:T(8,128)(2,1)}, u32[]{:S(2)}) copy-start(bf16[128,128]{1,0:T(8,128)(2,1)} %weight.1) | copy-start | bytes 98308
  85.9 13.6 %copy-start.5 = (s32[512]{0:T(512)S(1)}, s32[512]{0:T(512)}, u32[]{:S(2)}) copy-start(s32[512]{0:T(512)} %mask.1) | copy-start | bytes 6148
  101.0 8.3 %collective-permute-start = (bf16[40,128]{1,0:T(8,128)(2,1)S(1)}, bf16[40,128]{1,0:T(8,128)(2,1)S(1)}, u32[]{:S(2)}, u32[]{:S(2)}) collective-permute-start(bf16[40,128]{1,0:T(8,128)(2,1)S(1)} %convert_element_type.27), channel_id=1, source_target_pairs={{0,128},{1,96},{2,144},{3,64},{4,176},{5,32},{6,112},{7,80},{8,160... | collective-permute-start | bytes 30728 | tf_op jit(solution)/shard_map/ppermute | solution.py:429
  110.0 23.9 %all-to-all-start.4 = ((bf16[16,40,128]{2,1,0:T(8,128)(2,1)}), bf16[16,40,128]{2,1,0:T(8,128)(2,1)S(1)}, u32[]{:S(2)}, u32[]{:S(2)}) async-start(bf16[16,40,128]{2,1,0:T(8,128)(2,1)} %broadcast_in_dim.2), calls=%async_computation.4 | async-start | bytes 327680 | tf_op jit(solution)/shard_map/all_to_all | solution.py:431
  125.6 15.6 %copy-start.1 = (bf16[8,2048]{1,0:T(8,128)(2,1)S(1)}, bf16[8,2048]{1,0:T(8,128)(2,1)}, u32[]{:S(2)}) copy-start(bf16[8,2048]{1,0:T(8,128)(2,1)} %tile.13) | copy-start | bytes 98308
  125.6 15.6 %copy-start.6 = (s32[8]{0:T(128)S(1)}, s32[8]{0:T(128)}, u32[]{:S(2)}) copy-start(s32[8]{0:T(128)} %flags.1) | copy-start | bytes 100
  133.9 7.2 %collective-permute-start.3 = (bf16[16,40,128]{2,1,0:T(8,128)(2,1)S(1)}, bf16[16,40,128]{2,1,0:T(8,128)(2,1)S(1)}, u32[]{:S(2)}, u32[]{:S(2)}) collective-permute-start(bf16[16,40,128]{2,1,0:T(8,128)(2,1)S(1)} %all-to-all-done.4.got), channel_id=1, source_target_pairs={{0,256},{16,272},{32,288},{48,304},{64,320},{80,336},{96,352},{112... | collective-permute-start | bytes 491528 | tf_op jit(solution)/shard_map/ppermute | solution.py:468

commit v9 on v8

--- a/solution.py
+++ b/solution.py
@@ -376,13 +376,14 @@
     )(got, rider)
     got = exchange(sent, "col")
     share = got[:, columns_here:]
-    for step in (1, 2):
+
+    def swap_share(share, step):
         swapped = lax.ppermute(share, "col", [(a, a ^ step) for a in range(col_size)])
         first = col_index // step % 2 == 0
-        share = jnp.concatenate(
+        return jnp.concatenate(
             [jnp.where(first, share, swapped), jnp.where(first, swapped, share)], axis=1
         )
-    sequence_all = share.reshape(col_size, msa_rows, columns_here, features)
+
     sent = pl.pallas_call(
         functools.partial(multiply_kernel, columns_here, row_size),
         out_shape=jax.ShapeDtypeStruct((col_size, rows_here, width), jnp.bfloat16),
@@ -392,6 +393,8 @@
         compiler_params=spacious,
         cost_estimate=work(2 * tokens * width * width),
     )(got)
+    share, sent = lax.optimization_barrier((share, sent))
+    share = swap_share(share, 1)
     got = exchange(sent, "col")
     sent = pl.pallas_call(
         functools.partial(returned_kernel, channels_here, row_size),
@@ -402,6 +405,8 @@
         compiler_params=spacious,
         cost_estimate=work(patch * channels),
     )(got)
+    share, sent = lax.optimization_barrier((share, sent))
+    sequence_all = swap_share(share, 2).reshape(col_size, msa_rows, columns_here, features)
     crossed = exchange(sent.reshape(row_size, -1, lanes), "row").reshape(-1, lanes)
     coupling_refreshed, sent = pl.pallas_call(
         functools.partial(update_kernel, columns_here),

time: 144 us -> 146 us (1.014)
  the two profiles are of different devices: /device:TPU:2 before, /device:TPU:32 now
where the time goes in v9:
time: 146 us; the launch traced here: 145 us
  waiting for transfers between devices  72.2 us (49%)
  starting transfers between devices  48.9 us (33%)
  Pallas kernels  10.6 us (7%)
  local copies, waits for them, and re-layouts  7.24 us (5%)
  other arithmetic  3.48 us (2%)
  matrix products  1.79 us (1%)
    all_to_all x4, waiting for transfers between devices, exchange(): return lax.all_to_all(blocks, axis, split_axis=0, concat_axis=0, tiled=True)  50.4 us
    all_to_all x4, starting transfers between devices, exchange(): return lax.all_to_all(blocks, axis, split_axis=0, concat_axis=0, tiled=True)  31.5 us
    all_to_all x1, waiting for transfers between devices, shards(): lax.all_to_all(jnp.broadcast_to(sent[None], (col_size,) + sent.shape), 'r...  9.22 us
    all_to_all x1, starting transfers between devices, shards(): lax.all_to_all(jnp.broadcast_to(sent[None], (col_size,) + sent.shape), 'r...  7.84 us
    ppermute x1, waiting for transfers between devices, shards(): sent = lax.ppermute(sent, ('row', 'col'), moves)  7.64 us
    ppermute x2, starting transfers between devices, swap_share(): lax.ppermute(share, 'col', [(a, a ^ step) for a in range(col_size)])  3.9 us
    ppermute x1, waiting for transfers between devices, shards(): other = lax.ppermute(mine, 'row', swap)  2.98 us
    ppermute x1, starting transfers between devices, shards(): other = lax.ppermute(mine, 'row', swap)  2.93 us
  transfers between devices with their start and end apart: 9, of which 8 were waited for; matrix products, arithmetic and copies ran while one was open for 8% of the time, Pallas kernels for 2%

profile of v9, /device:TPU:32, one launch (start us, length us, event | category | flops | bytes accessed | tf_op | source)
XLA Modules:
  0.0 145.2 jit_solution(7180446097791260062)
XLA Ops:
  0.7 2.4 %shard_map.113 = (bf16[256,512]{1,0:T(8,128)(2,1)}, f32[512,128]{1,0:T(8,128)}) custom-call(s32[512]{0:T(512)} %mask.1, bf16[16,32,128]{2,1,0:T(8,128)(2,1)} %pair_far.1, bf16[128,640]{1,0:T(8,128)(2,1)} %weight_far.1), custom_call_target="tpu_custom_call" | custom-call | flops 83886080 | bytes 1048576 | tf_op jit(solution)/shard_map/pallas_call | solution.py:342
  3.1 16.3 %all-to-all-start = ((bf16[32,8,512]{2,1,0:T(8,128)(2,1)}), bf16[32,8,512]{2,1,0:T(8,128)(2,1)S(1)}, u32[]{:S(2)}, u32[]{:S(2)}) async-start(bf16[32,8,512]{2,1,0:T(8,128)(2,1)} %bitcast.42), calls=%async_computation | async-start | bytes 524288 | tf_op jit(solution)/shard_map/all_to_all | solution.py:24
  21.2 19.2 %all-to-all-done.got = bf16[32,8,512]{2,1,0:T(8,128)(2,1)S(1)} async-done(((bf16[32,8,512]{2,1,0:T(8,128)(2,1)}), bf16[32,8,512]{2,1,0:T(8,128)(2,1)S(1)}, u32[]{:S(2)}, u32[]{:S(2)}) %all-to-all-start) | async-done | bytes 262176 | tf_op jit(solution)/shard_map/all_to_all | solution.py:24
  41.7 6.7 %all-to-all-start.1 = ((bf16[16,40,512]{2,1,0:T(8,128)(2,1)}), bf16[16,40,512]{2,1,0:T(8,128)(2,1)S(1)}, u32[]{:S(2)}, u32[]{:S(2)}) async-start(bf16[16,40,512]{2,1,0:T(8,128)(2,1)} %shard_map.114), calls=%async_computation.1 | async-start | bytes 1310720 | tf_op jit(solution)/shard_map/all_to_all | solution.py:24
  48.8 13.4 %all-to-all-done.1.got = bf16[16,40,512]{2,1,0:T(8,128)(2,1)S(1)} async-done(((bf16[16,40,512]{2,1,0:T(8,128)(2,1)}), bf16[16,40,512]{2,1,0:T(8,128)(2,1)S(1)}, u32[]{:S(2)}, u32[]{:S(2)}) %all-to-all-start.1) | async-done | bytes 655392 | tf_op jit(solution)/shard_map/all_to_all | solution.py:24
  63.3 1.9 %collective-permute-start = (bf16[16,8,512]{2,1,0:T(8,128)(2,1)S(1)}, bf16[16,8,512]{2,1,0:T(8,128)(2,1)S(1)}, u32[]{:S(2)}, u32[]{:S(2)}) collective-permute-start(bf16[16,8,512]{2,1,0:T(8,128)(2,1)S(1)} %slice.12), channel_id=1, source_target_pairs={{0,1},{1,0},{2,3},{3,2},{4,5},{5,4},{6,7},{7,6},{8,9},{9,8},{10,11... | collective-permute-start | bytes 393224 | tf_op jit(solution)/shard_map/ppermute | solution.py:381
  65.2 3.5 %all-to-all-start.2 = ((bf16[16,16,256]{2,1,0:T(8,128)(2,1)}), bf16[16,16,256]{2,1,0:T(8,128)(2,1)S(1)}, u32[]{:S(2)}, u32[]{:S(2)}) async-start(bf16[16,16,256]{2,1,0:T(8,128)(2,1)} %shard_map.115), calls=%async_computation.2 | async-start | bytes 262144 | tf_op jit(solution)/shard_map/all_to_all | solution.py:24
  69.0 7.9 %all-to-all-done.2.got = bf16[16,16,256]{2,1,0:T(8,128)(2,1)S(1)} async-done(((bf16[16,16,256]{2,1,0:T(8,128)(2,1)}), bf16[16,16,256]{2,1,0:T(8,128)(2,1)S(1)}, u32[]{:S(2)}, u32[]{:S(2)}) %all-to-all-start.2) | async-done | bytes 131104 | tf_op jit(solution)/shard_map/all_to_all | solution.py:24
  77.9 2.0 %collective-permute-start.2 = (bf16[16,16,512]{2,1,0:T(8,128)(2,1)S(1)}, bf16[16,16,512]{2,1,0:T(8,128)(2,1)S(1)}, u32[]{:S(2)}, u32[]{:S(2)}) collective-permute-start(bf16[16,16,512]{2,1,0:T(8,128)(2,1)S(1)} %pad_maximum_fusion), channel_id=1, source_target_pairs={{0,2},{1,3},{2,0},{3,1},{4,6},{5,7},{6,4},{7,5},{8,10},{9,11},{10,... | collective-permute-start | bytes 786440 | tf_op jit(solution)/shard_map/ppermute | solution.py:381
  80.0 4.9 %all-to-all-start.3 = ((bf16[32,16,128]{2,1,0:T(8,128)(2,1)}), bf16[32,16,128]{2,1,0:T(8,128)(2,1)S(1)}, u32[]{:S(2)}, u32[]{:S(2)}) async-start(bf16[32,16,128]{2,1,0:T(8,128)(2,1)} %bitcast.2), calls=%async_computation.3 | async-start | bytes 262144 | tf_op jit(solution)/shard_map/all_to_all | solution.py:24
  85.9 2.0 %collective-permute-done.2 = bf16[16,16,512]{2,1,0:T(8,128)(2,1)S(1)} collective-permute-done((bf16[16,16,512]{2,1,0:T(8,128)(2,1)S(1)}, bf16[16,16,512]{2,1,0:T(8,128)(2,1)S(1)}, u32[]{:S(2)}, u32[]{:S(2)}) %collective-permute-start.2) | collective-permute-done | bytes 262176 | tf_op jit(solution)/shard_map/ppermute | solution.py:381
  89.1 1.6 %reshape.75 = f32[16,8,32,64]{3,2,1,0:T(8,128)S(1)} reshape(f32[16,32,512]{2,1,0:T(8,128)} %maximum_convert_fusion) | data formatting | bytes 2097152 | tf_op jit(solution)/shard_map/convert_element_type | solution.py:444
  91.3 9.9 %all-to-all-done.3 = bf16[32,16,128]{2,1,0:T(8,128)(2,1)S(1)} async-done(((bf16[32,16,128]{2,1,0:T(8,128)(2,1)}), bf16[32,16,128]{2,1,0:T(8,128)(2,1)S(1)}, u32[]{:S(2)}, u32[]{:S(2)}) %all-to-all-start.3) | async-done | bytes 131104 | tf_op jit(solution)/shard_map/all_to_all | solution.py:24
  101.2 1.5 %shard_map.117 = (bf16[512,128]{1,0:T(8,128)(2,1)}, f32[40,128]{1,0:T(8,128)S(1)}) custom-call(s32[512]{0:T(512)S(1)} %copy-done.5, s32[4,128]{1,0:T(4,128)S(1)} %bitcast.40, bf16[512,128]{1,0:T(8,128)(2,1)S(1)} %bitcast.38, f32[512,128]{1,0:T(8,128)S(1)} %copy-done.2, bf16[512,128]{1,0:T(8,128)(2,1)S(1)} %bitcast.39, bf16[128,128]{1,0:T(8,128)(2,1)S(1)} %copy-done.4, ...), custom_call_target="tpu_custom_call" | custom-call | flops 33554432 | bytes 1048576 | tf_op jit(solution)/shard_map/pallas_call | solution.py:411
  102.8 2.7 %collective-permute-start.1 = (bf16[40,128]{1,0:T(8,128)(2,1)S(1)}, bf16[40,128]{1,0:T(8,128)(2,1)S(1)}, u32[]{:S(2)}, u32[]{:S(2)}) collective-permute-start(bf16[40,128]{1,0:T(8,128)(2,1)S(1)} %convert_element_type.27), channel_id=1, source_target_pairs={{0,128},{1,96},{2,144},{3,64},{4,176},{5,32},{6,112},{7,80},{8,160... | collective-permute-start | bytes 30728 | tf_op jit(solution)/shard_map/ppermute | solution.py:434
  105.5 7.6 %collective-permute-done.1 = bf16[40,128]{1,0:T(8,128)(2,1)S(1)} collective-permute-done((bf16[40,128]{1,0:T(8,128)(2,1)S(1)}, bf16[40,128]{1,0:T(8,128)(2,1)S(1)}, u32[]{:S(2)}, u32[]{:S(2)}) %collective-permute-start.1) | collective-permute-done | bytes 10272 | tf_op jit(solution)/shard_map/ppermute | solution.py:434
  113.8 7.8 %all-to-all-start.4 = ((bf16[16,40,128]{2,1,0:T(8,128)(2,1)}), bf16[16,40,128]{2,1,0:T(8,128)(2,1)S(1)}, u32[]{:S(2)}, u32[]{:S(2)}) async-start(bf16[16,40,128]{2,1,0:T(8,128)(2,1)} %broadcast_in_dim.2), calls=%async_computation.4 | async-start | bytes 327680 | tf_op jit(solution)/shard_map/all_to_all | solution.py:436
  121.7 1.3 multiply_reduce_fusion
  123.0 1.5 %convert_bitcast_fusion = bf16[16,32,8,256]{3,1,2,0:T(8,128)(2,1)S(1)} fusion(f32[16,8,32,64]{3,2,1,0:T(8,128)S(1)} %reshape.75, f32[16,8,32]{2,1,0:T(8,128)S(1)} %add_rsqrt_fusion, f32[16,8,32]{2,1,0:T(8,128)S(1)} %broadcast_multiply_fusion, bf16[64,512]{1,0:T(8,128)(2,1)S(1)} %copy-done.8), kind=kOutput, calls=%fused_computation | convolution fusion | flops 136052736 | bytes 4358144 | tf_op jit(solution)/shard_map/qsjf,fg->qjsg/dot_general | solution.py:445
  124.5 1.4 copy.18
  126.7 9.2 %all-to-all-done.4.got = bf16[16,40,128]{2,1,0:T(8,128)(2,1)S(1)} async-done(((bf16[16,40,128]{2,1,0:T(8,128)(2,1)}), bf16[16,40,128]{2,1,0:T(8,128)(2,1)S(1)}, u32[]{:S(2)}, u32[]{:S(2)}) %all-to-all-start.4) | async-done | bytes 163872 | tf_op jit(solution)/shard_map/all_to_all | solution.py:436
  135.9 2.9 %collective-permute-start.3 = (bf16[16,40,128]{2,1,0:T(8,128)(2,1)S(1)}, bf16[16,40,128]{2,1,0:T(8,128)(2,1)S(1)}, u32[]{:S(2)}, u32[]{:S(2)}) collective-permute-start(bf16[16,40,128]{2,1,0:T(8,128)(2,1)S(1)} %all-to-all-done.4.got), channel_id=1, source_target_pairs={{0,256},{16,272},{32,288},{48,304},{64,320},{80,336},{96,352},{112... | collective-permute-start | bytes 491528 | tf_op jit(solution)/shard_map/ppermute | solution.py:473
  140.1 3.0 %collective-permute-done.3.got = bf16[16,40,128]{2,1,0:T(8,128)(2,1)S(1)} collective-permute-done((bf16[16,40,128]{2,1,0:T(8,128)(2,1)S(1)}, bf16[16,40,128]{2,1,0:T(8,128)(2,1)S(1)}, u32[]{:S(2)}, u32[]{:S(2)}) %collective-permute-start.3) | collective-permute-done | bytes 163872 | tf_op jit(solution)/shard_map/ppermute | solution.py:473
  143.1 2.1 %shard_map.119 = bf16[8,2048]{1,0:T(8,128)(2,1)} custom-call(s32[16]{0:T(128)S(1)} %get-tuple-element.35.places, s32[8]{0:T(128)S(1)} %copy-done.6, bf16[16,40,128]{2,1,0:T(8,128)(2,1)S(1)} %collective-permute-done.3.got, bf16[512,2048]{1,0:T(8,128)(2,1)S(1)} %bitcast.36, f32[16,2048]{1,0:T(8,128)S(1)} %shard_map.118.mine, f32[32,2048]{1,0:T(8,128)S(1)} %bitcast.37, ...), custom_call_target="tpu_custom_call" | custom-call | flops 268435456 | bytes 1048576 | tf_op jit(solution)/shard_map/pallas_call | solution.py:494
  (49 shorter events, 11.1 us)
Async XLA Ops:
  0.6 48.1 %copy-start = (bf16[128,8]{0,1:T(8,128)(2,1)S(1)}, bf16[128,8]{0,1:T(8,128)(2,1)}, u32[]{:S(2)}) copy-start(bf16[128,8]{0,1:T(8,128)(2,1)} %param.16) | copy-start | bytes 6148
  0.6 47.8 %copy-start.7 = (bf16[256,64]{0,1:T(8,128)(2,1)S(1)}, bf16[256,64]{0,1:T(8,128)(2,1)}, u32[]{:S(2)}) copy-start(bf16[256,64]{0,1:T(8,128)(2,1)} %param.18) | copy-start | bytes 98308
  3.1 37.3 %all-to-all-start = ((bf16[32,8,512]{2,1,0:T(8,128)(2,1)}), bf16[32,8,512]{2,1,0:T(8,128)(2,1)S(1)}, u32[]{:S(2)}, u32[]{:S(2)}) async-start(bf16[32,8,512]{2,1,0:T(8,128)(2,1)} %bitcast.42), calls=%async_computation | async-start | bytes 524288 | tf_op jit(solution)/shard_map/all_to_all | solution.py:24
  20.2 48.6 %copy-start.8 = (bf16[64,512]{1,0:T(8,128)(2,1)S(1)}, bf16[64,512]{1,0:T(8,128)(2,1)}, u32[]{:S(2)}) copy-start(bf16[64,512]{1,0:T(8,128)(2,1)} %param.17) | copy-start | bytes 196612
  41.7 20.5 %all-to-all-start.1 = ((bf16[16,40,512]{2,1,0:T(8,128)(2,1)}), bf16[16,40,512]{2,1,0:T(8,128)(2,1)S(1)}, u32[]{:S(2)}, u32[]{:S(2)}) async-start(bf16[16,40,512]{2,1,0:T(8,128)(2,1)} %shard_map.114), calls=%async_computation.1 | async-start | bytes 1310720 | tf_op jit(solution)/shard_map/all_to_all | solution.py:24
  63.3 14.6 %collective-permute-start = (bf16[16,8,512]{2,1,0:T(8,128)(2,1)S(1)}, bf16[16,8,512]{2,1,0:T(8,128)(2,1)S(1)}, u32[]{:S(2)}, u32[]{:S(2)}) collective-permute-start(bf16[16,8,512]{2,1,0:T(8,128)(2,1)S(1)} %slice.12), channel_id=1, source_target_pairs={{0,1},{1,0},{2,3},{3,2},{4,5},{5,4},{6,7},{7,6},{8,9},{9,8},{10,11... | collective-permute-start | bytes 393224 | tf_op jit(solution)/shard_map/ppermute | solution.py:381
  65.2 11.7 %all-to-all-start.2 = ((bf16[16,16,256]{2,1,0:T(8,128)(2,1)}), bf16[16,16,256]{2,1,0:T(8,128)(2,1)S(1)}, u32[]{:S(2)}, u32[]{:S(2)}) async-start(bf16[16,16,256]{2,1,0:T(8,128)(2,1)} %shard_map.115), calls=%async_computation.2 | async-start | bytes 262144 | tf_op jit(solution)/shard_map/all_to_all | solution.py:24
  77.9 9.9 %collective-permute-start.2 = (bf16[16,16,512]{2,1,0:T(8,128)(2,1)S(1)}, bf16[16,16,512]{2,1,0:T(8,128)(2,1)S(1)}, u32[]{:S(2)}, u32[]{:S(2)}) collective-permute-start(bf16[16,16,512]{2,1,0:T(8,128)(2,1)S(1)} %pad_maximum_fusion), channel_id=1, source_target_pairs={{0,2},{1,3},{2,0},{3,1},{4,6},{5,7},{6,4},{7,5},{8,10},{9,11},{10,... | collective-permute-start | bytes 786440 | tf_op jit(solution)/shard_map/ppermute | solution.py:381
  80.0 21.2 %all-to-all-start.3 = ((bf16[32,16,128]{2,1,0:T(8,128)(2,1)}), bf16[32,16,128]{2,1,0:T(8,128)(2,1)S(1)}, u32[]{:S(2)}, u32[]{:S(2)}) async-start(bf16[32,16,128]{2,1,0:T(8,128)(2,1)} %bitcast.2), calls=%async_computation.3 | async-start | bytes 262144 | tf_op jit(solution)/shard_map/all_to_all | solution.py:24
  89.1 12.1 %copy-start.2 = (f32[512,128]{1,0:T(8,128)S(1)}, f32[512,128]{1,0:T(8,128)}, u32[]{:S(2)}) copy-start(f32[512,128]{1,0:T(8,128)} %get-tuple-element.19.gate) | copy-start | bytes 786436
  89.1 12.1 %copy-start.3 = (bf16[16,32,128]{2,1,0:T(8,128)(2,1)S(1)}, bf16[16,32,128]{2,1,0:T(8,128)(2,1)}, u32[]{:S(2)}) copy-start(bf16[16,32,128]{2,1,0:T(8,128)(2,1)} %pair_far.1) | copy-start | bytes 393220
  89.1 12.1 %copy-start.4 = (bf16[128,128]{1,0:T(8,128)(2,1)S(1)}, bf16[128,128]{1,0:T(8,128)(2,1)}, u32[]{:S(2)}) copy-start(bf16[128,128]{1,0:T(8,128)(2,1)} %weight.1) | copy-start | bytes 98308
  89.1 12.1 %copy-start.5 = (s32[512]{0:T(512)S(1)}, s32[512]{0:T(512)}, u32[]{:S(2)}) copy-start(s32[512]{0:T(512)} %mask.1) | copy-start | bytes 6148
  102.8 10.4 %collective-permute-start.1 = (bf16[40,128]{1,0:T(8,128)(2,1)S(1)}, bf16[40,128]{1,0:T(8,128)(2,1)S(1)}, u32[]{:S(2)}, u32[]{:S(2)}) collective-permute-start(bf16[40,128]{1,0:T(8,128)(2,1)S(1)} %convert_element_type.27), channel_id=1, source_target_pairs={{0,128},{1,96},{2,144},{3,64},{4,176},{5,32},{6,112},{7,80},{8,160... | collective-permute-start | bytes 30728 | tf_op jit(solution)/shard_map/ppermute | solution.py:434
  113.8 22.1 %all-to-all-start.4 = ((bf16[16,40,128]{2,1,0:T(8,128)(2,1)}), bf16[16,40,128]{2,1,0:T(8,128)(2,1)S(1)}, u32[]{:S(2)}, u32[]{:S(2)}) async-start(bf16[16,40,128]{2,1,0:T(8,128)(2,1)} %broadcast_in_dim.2), calls=%async_computation.4 | async-start | bytes 327680 | tf_op jit(solution)/shard_map/all_to_all | solution.py:436
  126.7 16.4 %copy-start.1 = (bf16[8,2048]{1,0:T(8,128)(2,1)S(1)}, bf16[8,2048]{1,0:T(8,128)(2,1)}, u32[]{:S(2)}) copy-start(bf16[8,2048]{1,0:T(8,128)(2,1)} %tile.13) | copy-start | bytes 98308
  126.7 16.4 %copy-start.6 = (s32[8]{0:T(128)S(1)}, s32[8]{0:T(128)}, u32[]{:S(2)}) copy-start(s32[8]{0:T(128)} %flags.1) | copy-start | bytes 100
  135.9 7.2 %collective-permute-start.3 = (bf16[16,40,128]{2,1,0:T(8,128)(2,1)S(1)}, bf16[16,40,128]{2,1,0:T(8,128)(2,1)S(1)}, u32[]{:S(2)}, u32[]{:S(2)}) collective-permute-start(bf16[16,40,128]{2,1,0:T(8,128)(2,1)S(1)} %all-to-all-done.4.got), channel_id=1, source_target_pairs={{0,256},{16,272},{32,288},{48,304},{64,320},{80,336},{96,352},{112... | collective-permute-start | bytes 491528 | tf_op jit(solution)/shard_map/ppermute | solution.py:473
